TPU v7x, 128 devices: a whole 4x4x4 slice. The times are simulated.
128 devices in a mesh: fsdp: 64 (over x, y, z_lo, core), rep: 2 (over z_hi).
Axes of the slice: x: 4, y: 4, z: 4 (z_hi: 2, z_lo: 2; z = z_hi * 2 + z_lo), core: 2. Of those that a mesh axis runs over, the one named last changes fastest.
Arguments:
- block_input: bfloat16 [32768, 768], P(('fsdp', 'rep')), may hold values from -6 to 6
- segment_ids: int32 [128, 256], P(('fsdp', 'rep')), may hold values from 0 to 3, never falling along the last dimension, each value on 1 to 128 neighbouring positions
- norm1_gain: bfloat16 [768], P('fsdp'), may hold values from 0.099609375 to 1.8984375
- norm1_bias: bfloat16 [768], P('fsdp'), may hold values from -3 to 3
- query_weight: bfloat16 [768, 768], P('fsdp'), may hold values from -0.21875 to 0.21875
- key_weight: bfloat16 [768, 768], P('fsdp'), may hold values from -0.21875 to 0.21875
- value_weight: bfloat16 [768, 768], P('fsdp'), may hold values from -0.21875 to 0.21875
- out_weight: bfloat16 [768, 768], P('fsdp'), may hold values from -0.875 to 0.875
- norm2_gain: bfloat16 [768], P('fsdp'), may hold values from 0.099609375 to 1.8984375
- norm2_bias: bfloat16 [768], P('fsdp'), may hold values from -3 to 3
- up_weight: bfloat16 [768, 3072], P('fsdp'), may hold values from -0.21875 to 0.21875
- down_weight: bfloat16 [3072, 768], P('fsdp'), may hold values from -0.15625 to 0.15625
- out_cotangent: bfloat16 [32768, 768], P(('fsdp', 'rep')), may hold values from -6 to 6
Outputs:
- block_output: bfloat16 [32768, 768], P(('fsdp', 'rep'))
- input_grad: float32 [32768, 768], P(('fsdp', 'rep'))
- norm1_gain_grad: float32 [768], P('fsdp')
- norm1_bias_grad: float32 [768], P('fsdp')
- query_grad: float32 [768, 768], P('fsdp')
- key_grad: float32 [768, 768], P('fsdp')
- value_grad: float32 [768, 768], P('fsdp')
- outproj_grad: float32 [768, 768], P('fsdp')
- norm2_gain_grad: float32 [768], P('fsdp')
- norm2_bias_grad: float32 [768], P('fsdp')
- up_grad: float32 [768, 3072], P('fsdp')
- down_grad: float32 [3072, 768], P('fsdp')
Inputs may be any that keep to these rules, and one draw needn't show every extreme that they name: `segment_ids`: along each row segment numbers never fall; one number covers a run of 1 to 128 consecutive tokens, and some run has exactly 128.
All inputs are finite; a program needn't handle non-finite values.
Results may differ from a plain program's by a relative error of at most 0.012.
Values may be sent and summed in bfloat16 or wider, within the bound.
A program may use at most 128 MiB of HBM per device.

v0:
```python
import jax
import jax.numpy as jnp
from jax import lax
from jax.sharding import PartitionSpec as P

HEADS = 24
HEAD_DIM = 32


def layer_norm(values, gain, shift):
    centre = jnp.mean(values, axis=-1, keepdims=True)
    centred = values - centre
    spread = jnp.mean(centred * centred, axis=-1, keepdims=True)
    return centred * lax.rsqrt(spread + 1e-05) * gain + shift


def masked_scores(query, key, segment_ids):
    tokens = query.shape[0]
    query_heads = query.reshape(tokens, HEADS, HEAD_DIM)
    key_heads = key.reshape(tokens, HEADS, HEAD_DIM)
    scaled = jnp.einsum(
        "qhd,khd->hqk", query_heads, key_heads, preferred_element_type=jnp.float32
    ) * HEAD_DIM ** (-0.5)
    segments = segment_ids.reshape(tokens)
    rows_iota = lax.broadcasted_iota(jnp.int32, (tokens, tokens), 0)
    cols_iota = lax.broadcasted_iota(jnp.int32, (tokens, tokens), 1)
    allowed = (rows_iota >= cols_iota) & (segments[:, None] == segments[None, :])
    return jnp.where(allowed[None], scaled, -1e30)


def matmul_back(left, right):
    return jnp.einsum("te,de->td", left, right, preferred_element_type=jnp.float32)


def matmul_outer(left, right):
    return jnp.einsum("td,te->de", left, right, preferred_element_type=jnp.float32)


def per_device(
    block_input,
    segment_ids,
    norm1_gain,
    norm1_bias,
    query_weight,
    key_weight,
    value_weight,
    out_weight,
    norm2_gain,
    norm2_bias,
    up_weight,
    down_weight,
    out_cotangent,
):
    tokens = block_input.shape[0]
    inputs = block_input.astype(jnp.float32)
    attn_set = (
        lax.all_gather(norm1_gain, "fsdp", axis=0, tiled=True),
        lax.all_gather(norm1_bias, "fsdp", axis=0, tiled=True),
        lax.all_gather(query_weight, "fsdp", axis=0, tiled=True),
        lax.all_gather(key_weight, "fsdp", axis=0, tiled=True),
        lax.all_gather(value_weight, "fsdp", axis=0, tiled=True),
        lax.all_gather(out_weight, "fsdp", axis=0, tiled=True),
    )
    gain1 = attn_set[0].astype(jnp.float32)
    bias1 = attn_set[1].astype(jnp.float32)
    normed1_f, norm1_pull = jax.vjp(layer_norm, inputs, gain1, bias1)
    normed1 = normed1_f.astype(jnp.bfloat16)
    query = jnp.dot(normed1, attn_set[2], preferred_element_type=jnp.float32).astype(jnp.bfloat16)
    key = jnp.dot(normed1, attn_set[3], preferred_element_type=jnp.float32).astype(jnp.bfloat16)
    value = jnp.dot(normed1, attn_set[4], preferred_element_type=jnp.float32).astype(jnp.bfloat16)
    scores = masked_scores(query, key, segment_ids)
    maximum = jnp.max(scores, axis=-1, keepdims=True)
    exponent = jnp.exp(scores - maximum)
    summed = jnp.sum(exponent, axis=-1, keepdims=True)
    probs = exponent / summed
    log_total = maximum + jnp.log(summed)
    value_heads = value.reshape(tokens, HEADS, HEAD_DIM)
    mixed = jnp.einsum(
        "hqk,khd->qhd", probs.astype(jnp.bfloat16), value_heads, preferred_element_type=jnp.float32
    )
    mixed = mixed.reshape(tokens, HEADS * HEAD_DIM).astype(jnp.bfloat16)
    hidden_state = inputs + jnp.dot(mixed, attn_set[5], preferred_element_type=jnp.float32)
    ffn_set = (
        lax.all_gather(norm2_gain, "fsdp", axis=0, tiled=True),
        lax.all_gather(norm2_bias, "fsdp", axis=0, tiled=True),
        lax.all_gather(up_weight, "fsdp", axis=0, tiled=True),
        lax.all_gather(down_weight, "fsdp", axis=0, tiled=True),
    )
    gain2 = ffn_set[0].astype(jnp.float32)
    bias2 = ffn_set[1].astype(jnp.float32)
    normed2_f, norm2_pull = jax.vjp(layer_norm, hidden_state, gain2, bias2)
    normed2 = normed2_f.astype(jnp.bfloat16)
    pre_act = jnp.dot(normed2, ffn_set[2], preferred_element_type=jnp.float32)
    activated_f, gelu_pull = jax.vjp(jax.nn.gelu, pre_act)
    activated = activated_f.astype(jnp.bfloat16)
    output = (
        hidden_state + jnp.dot(activated, ffn_set[3], preferred_element_type=jnp.float32)
    ).astype(jnp.bfloat16)
    ffn_back = (
        lax.all_gather(norm2_gain, "fsdp", axis=0, tiled=True),
        lax.all_gather(norm2_bias, "fsdp", axis=0, tiled=True),
        lax.all_gather(up_weight, "fsdp", axis=0, tiled=True),
        lax.all_gather(down_weight, "fsdp", axis=0, tiled=True),
    )
    down_term = matmul_outer(activated, out_cotangent)
    act_grad = matmul_back(out_cotangent, ffn_back[3])
    pre_grad = gelu_pull(act_grad)[0].astype(jnp.bfloat16)
    up_term = matmul_outer(normed2, pre_grad)
    normed2_grad = matmul_back(pre_grad, ffn_back[2])
    hidden_extra, gain2_term, bias2_term = norm2_pull(normed2_grad)
    hidden_grad = out_cotangent.astype(jnp.float32) + hidden_extra
    ffn_shards = (
        lax.psum_scatter(gain2_term, "fsdp", scatter_dimension=0, tiled=True),
        lax.psum_scatter(bias2_term, "fsdp", scatter_dimension=0, tiled=True),
        lax.psum_scatter(up_term, "fsdp", scatter_dimension=0, tiled=True),
        lax.psum_scatter(down_term, "fsdp", scatter_dimension=0, tiled=True),
    )
    attn_back = (
        lax.all_gather(norm1_gain, "fsdp", axis=0, tiled=True),
        lax.all_gather(norm1_bias, "fsdp", axis=0, tiled=True),
        lax.all_gather(query_weight, "fsdp", axis=0, tiled=True),
        lax.all_gather(key_weight, "fsdp", axis=0, tiled=True),
        lax.all_gather(value_weight, "fsdp", axis=0, tiled=True),
        lax.all_gather(out_weight, "fsdp", axis=0, tiled=True),
    )
    branch_grad = hidden_grad.astype(jnp.bfloat16)
    outproj_term = matmul_outer(mixed, branch_grad)
    mixed_grad = matmul_back(branch_grad, attn_back[5]).astype(jnp.bfloat16)
    mixed_heads = mixed_grad.reshape(tokens, HEADS, HEAD_DIM)
    again_probs = jnp.exp(masked_scores(query, key, segment_ids) - log_total)
    prob_grad = jnp.einsum(
        "qhd,khd->hqk", mixed_heads, value_heads, preferred_element_type=jnp.float32
    )
    value_act = jnp.einsum(
        "hqk,qhd->khd",
        again_probs.astype(jnp.bfloat16),
        mixed_heads,
        preferred_element_type=jnp.float32,
    )
    value_act = value_act.reshape(tokens, HEADS * HEAD_DIM).astype(jnp.bfloat16)
    row_dot = jnp.sum(prob_grad * again_probs, axis=-1, keepdims=True)
    score_grad = (again_probs * (prob_grad - row_dot)).astype(jnp.bfloat16)
    query_heads = query.reshape(tokens, HEADS, HEAD_DIM)
    key_heads = key.reshape(tokens, HEADS, HEAD_DIM)
    query_act = jnp.einsum(
        "hqk,khd->qhd", score_grad, key_heads, preferred_element_type=jnp.float32
    ) * HEAD_DIM ** (-0.5)
    key_act = jnp.einsum(
        "hqk,qhd->khd", score_grad, query_heads, preferred_element_type=jnp.float32
    ) * HEAD_DIM ** (-0.5)
    query_act = query_act.reshape(tokens, HEADS * HEAD_DIM).astype(jnp.bfloat16)
    key_act = key_act.reshape(tokens, HEADS * HEAD_DIM).astype(jnp.bfloat16)
    query_term = matmul_outer(normed1, query_act)
    key_term = matmul_outer(normed1, key_act)
    value_term = matmul_outer(normed1, value_act)
    normed1_grad = (
        matmul_back(query_act, attn_back[2])
        + matmul_back(key_act, attn_back[3])
        + matmul_back(value_act, attn_back[4])
    )
    input_extra, gain1_term, bias1_term = norm1_pull(normed1_grad)
    input_grad = hidden_grad + input_extra
    attn_shards = (
        lax.psum_scatter(gain1_term, "fsdp", scatter_dimension=0, tiled=True),
        lax.psum_scatter(bias1_term, "fsdp", scatter_dimension=0, tiled=True),
        lax.psum_scatter(query_term, "fsdp", scatter_dimension=0, tiled=True),
        lax.psum_scatter(key_term, "fsdp", scatter_dimension=0, tiled=True),
        lax.psum_scatter(value_term, "fsdp", scatter_dimension=0, tiled=True),
        lax.psum_scatter(outproj_term, "fsdp", scatter_dimension=0, tiled=True),
    )
    totals = lax.psum(
        (
            attn_shards[0],
            attn_shards[1],
            attn_shards[2],
            attn_shards[3],
            attn_shards[4],
            attn_shards[5],
            ffn_shards[0],
            ffn_shards[1],
            ffn_shards[2],
            ffn_shards[3],
        ),
        "rep",
    )
    return (
        output,
        input_grad,
        totals[0],
        totals[1],
        totals[2],
        totals[3],
        totals[4],
        totals[5],
        totals[6],
        totals[7],
        totals[8],
        totals[9],
    )


def solution(mesh):
    placed = (
        P(("fsdp", "rep"), None),
        P(("fsdp", "rep"), None),
        P("fsdp"),
        P("fsdp"),
        P("fsdp", None),
        P("fsdp", None),
        P("fsdp", None),
        P("fsdp", None),
        P("fsdp"),
        P("fsdp"),
        P("fsdp", None),
        P("fsdp", None),
        P(("fsdp", "rep"), None),
    )
    return jax.shard_map(
        per_device,
        mesh=mesh,
        in_specs=placed,
        out_specs=(
            P(("fsdp", "rep"), None),
            P(("fsdp", "rep"), None),
            P("fsdp"),
            P("fsdp"),
            P("fsdp", None),
            P("fsdp", None),
            P("fsdp", None),
            P("fsdp", None),
            P("fsdp"),
            P("fsdp"),
            P("fsdp", None),
            P("fsdp", None),
        ),
        check_vma=False,
    )
```

profile of v0, /device:TPU:1, one launch (start us, length us, event | category | flops | bytes accessed | tf_op | source)
XLA Modules:
  0.0 1737.4 jit_solution(10388257210947943961)
XLA Ops:
  16.6 142.1 %all-reduce.21 = (bf16[768]{0:T(1024)(128)(2,1)S(1)}, bf16[768]{0:T(1024)(128)(2,1)S(1)}, bf16[768]{0:T(1024)(128)(2,1)S(1)}, bf16[768]{0:T(1024)(128)(2,1)S(1)}) all-reduce(bf16[768]{0:T(1024)(128)(2,1)S(1)} %dynamic-update-slice.1, bf16[768]{0:T(1024)(128)(2,1)S(1)} %dynamic-update-slice, ...), channel_id=1, replica_groups=mesh['fsdp'=64,'rep'=2] {'fsdp'}, use_global_device_ids=true, to_apply=%add.1 | all-reduce | flops 3072 | bytes 12288
  162.1 2.3 reshape.180
  165.4 54.2 %all-gather.18.cloned.1.call-done = bf16[64,12,768]{2,1,0:T(8,128)(2,1)} async-done(((bf16[1,12,768]{2,1,0:T(8,128)(2,1)}), bf16[64,12,768]{2,1,0:T(8,128)(2,1)}) %all-gather.18.cloned.1.call-update) | async-done | bytes 1179664 | tf_op jit(solution)/shard_map/all_gather | solution.py:60
  219.6 2.2 reshape.182
  222.9 100.2 %all-gather.14.cloned.1.call-done = bf16[64,12,768]{2,1,0:T(8,128)(2,1)} async-done(((bf16[1,12,768]{2,1,0:T(8,128)(2,1)}), bf16[64,12,768]{2,1,0:T(8,128)(2,1)}) %all-gather.14.cloned.1.call-update) | async-done | bytes 1179664 | tf_op jit(solution)/shard_map/all_gather | solution.py:61
  323.2 2.2 reshape.178
  326.4 100.1 %all-gather.20.cloned.1.call-done = bf16[64,12,768]{2,1,0:T(8,128)(2,1)} async-done(((bf16[1,12,768]{2,1,0:T(8,128)(2,1)}), bf16[64,12,768]{2,1,0:T(8,128)(2,1)}) %all-gather.20.cloned.1.call-update) | async-done | bytes 1179664 | tf_op jit(solution)/shard_map/all_gather | solution.py:62
  426.5 2.2 reshape.184
  434.7 101.3 %all-gather.22.cloned.1.call-done = bf16[64,12,3072]{2,1,0:T(8,128)(2,1)} async-done(((bf16[1,12,3072]{2,1,0:T(8,128)(2,1)}), bf16[64,12,3072]{2,1,0:T(8,128)(2,1)}) %all-gather.22.cloned.1.call-update) | async-done | bytes 4718608 | tf_op jit(solution)/shard_map/all_gather | solution.py:86
  536.0 7.5 reshape.186
  543.5 100.0 %all-gather.12.cloned.1.call-done = bf16[3072,768]{1,0:T(8,128)(2,1)} async-done(((bf16[48,768]{1,0:T(8,128)(2,1)}), bf16[3072,768]{1,0:T(8,128)(2,1)}) %all-gather.12.cloned.1.call-update) | async-done | bytes 4718608 | tf_op jit(solution)/shard_map/all_gather | solution.py:87
  643.6 3.9 fusion.59
  647.5 4.7 fusion.13
  653.8 5.9 fusion.43
  659.9 4.5 multiply_reduce_fusion.1
  668.2 3.2 fusion.61
  671.4 4.0 fusion.21
  688.3 5.1 fusion.41
  693.4 362.8 %fusion.54 = (f32[16,768]{1,0:T(8,128)S(1)}, f32[16,768]{1,0:T(8,128)S(1)}, f32[16,768]{1,0:T(8,128)S(1)}, f32[16,768]{1,0:T(8,128)S(1)}, f32[16,3072]{1,0:T(8,128)}) fusion(f32[768,768]{1,0:T(8,128)} %fusion.48, f32[768,768]{1,0:T(8,128)} %fusion.46, f32[768,768]{1,0:T(8,128)} %fusion.44, f32[768,768]{1,0:T(8,128)} %fusion.61, f32[768,3072]{1,0:T(8,128)} %fusion.41), kind=kCustom, calls=%all-reduce-scatter.5 | all-reduce-scatter fusion | flops 6291457 | bytes 19268096
  1059.0 2.5 collective-permute-start.47
  1061.5 2.9 collective-permute-start.31
  1066.4 5.4 collective-permute-start.13
  1075.3 2.5 collective-permute-start.10
  1077.8 5.0 collective-permute-start.9
  1082.8 2.8 collective-permute-start.8
  1087.8 3.6 collective-permute-start.6
  1092.7 4.5 collective-permute-start.4
  1098.5 2.5 collective-permute-start.2
  1101.1 3.6 collective-permute-start.1
  1104.7 3.7 collective-permute-start
  1116.0 2.8 collective-permute-start.25
  1118.9 3.1 collective-permute-start.24
  1122.0 2.2 collective-permute-start.23
  1124.3 2.5 collective-permute-start.22
  1128.2 3.7 collective-permute-start.20
  1136.1 4.0 collective-permute-start.17
  1140.1 2.5 collective-permute-start.16
  1151.3 2.3 collective-permute-start.41
  1153.8 6.0 fusion.18
  1161.9 2.8 collective-permute-start.39
  1164.7 2.2 collective-permute-start.38
  1168.9 3.4 collective-permute-start.36
  1176.3 3.4 collective-permute-start.33
  1179.7 3.7 collective-permute-start.32
  1194.6 2.5 collective-permute-start.56
  1197.1 2.5 collective-permute-start.55
  1199.6 2.5 collective-permute-start.54
  1203.9 3.3 collective-permute-start.52
  1210.8 2.9 collective-permute-start.49
  1213.7 3.7 collective-permute-start.48
  1219.2 268.9 %all-reduce.18 = (f32[768]{0:T(1024)S(1)}, f32[768]{0:T(1024)S(1)}, f32[768]{0:T(1024)S(1)}, f32[768]{0:T(1024)S(1)}) all-reduce(f32[768]{0:T(1024)S(1)} %get-tuple-element.14, f32[768]{0:T(1024)S(1)} %get-tuple-element.17, f32[768]{0:T(1024)S(1)} %get-tuple-element.12, ...), channel_id=2, replica_groups=mesh['fsdp'=64,'rep'=2] {'fsdp'}, use_global_device_ids=true, to_apply=%region_12.13.clone | all-reduce | flops 3072 | bytes 24576
  1500.5 25.1 %concatenate = f32[268,768]{1,0:T(8,128)} concatenate(f32[12,768]{1,0:T(8,128)} %copy-done.40, f32[16,768]{1,0:T(8,128)} %copy-done.39, f32[16,768]{1,0:T(8,128)} %copy-done.41, f32[16,768]{1,0:T(8,128)} %copy-done.42, f32[16,768]{1,0:T(8,128)} %copy-done.43, f32[16,768]{1,0:T(8,128)} %copy-done.44, f32[16,768]{1,0:T(8,128)} %copy-done.45, f32[16,768]{1,0:T(8,128)} %copy-done.46, ...), dimensions={0} | concatenate | bytes 1646592
  1525.7 25.0 %concatenate.1 = f32[268,768]{1,0:T(8,128)} concatenate(f32[12,768]{1,0:T(8,128)} %copy-done.38, f32[16,768]{1,0:T(8,128)} %copy-done.55, f32[16,768]{1,0:T(8,128)} %copy-done.56, f32[16,768]{1,0:T(8,128)} %copy-done.57, f32[16,768]{1,0:T(8,128)} %copy-done.58, f32[16,768]{1,0:T(8,128)} %copy-done.59, f32[16,768]{1,0:T(8,128)} %copy-done.60, f32[16,768]{1,0:T(8,128)} %copy-done.61, ...), dimensions={0} | concatenate | bytes 1646592
  1550.7 12.5 concatenate.2
  1563.2 24.2 %concatenate.3 = f32[268,768]{1,0:T(8,128)} concatenate(f32[12,768]{1,0:T(8,128)S(1)} %copy-done.35, f32[16,768]{1,0:T(8,128)} %copy-done.81, f32[16,768]{1,0:T(8,128)} %copy-done.82, f32[16,768]{1,0:T(8,128)} %copy-done.83, f32[16,768]{1,0:T(8,128)} %copy-done.84, f32[16,768]{1,0:T(8,128)} %copy-done.85, f32[16,768]{1,0:T(8,128)} %copy-done.86, f32[16,768]{1,0:T(8,128)} %copy-done.87, ...), dimensions={0} | concatenate | bytes 1646592
  1587.4 12.9 collective-permute-start.73
  1600.3 3.5 collective-permute-start.72
  1605.1 3.7 collective-permute-start.70
  1613.2 5.5 collective-permute-start.68
  1620.7 2.5 collective-permute-start.66
  1623.2 12.0 collective-permute-start.65
  1635.2 2.3 collective-permute-start.64
  1642.1 42.9 %concatenate.4 = f32[268,3072]{1,0:T(8,128)} concatenate(f32[12,3072]{1,0:T(8,128)S(1)} %collective-permute-done.79, f32[16,3072]{1,0:T(8,128)} %collective-permute-done.78, f32[16,3072]{1,0:T(8,128)} %collective-permute-done.77, f32[16,3072]{1,0:T(8,128)} %collective-permute-done.76, f32[16,3072]{1,0:T(8,128)} %collective-permute-done.75, f32[16,3072]{1,0:T(8,128)} %collective-permute-done.74, ...), dimensions={0} | concatenate | bytes 6586368
  1687.9 29.1 %all-reduce.28.cloned.1.call-done = (f32[12,3072]{1,0:T(8,128)}, f32[48,768]{1,0:T(8,128)}) async-done(((f32[12,3072]{1,0:T(8,128)}, f32[48,768]{1,0:T(8,128)}), (f32[12,3072]{1,0:T(8,128)}, f32[48,768]{1,0:T(8,128)})) %all-reduce.28.cloned.1.call-update) | async-done | bytes 294928 | tf_op jit(solution)/shard_map/psum | solution.py:171
  (417 shorter events, 139.2 us)
Async XLA Ops:
  7.2 154.9 %all-gather.16.cloned.1.call-start = ((), (), s32[]{:S(2)}) async-start(), calls=%async_computation.4 | async-start | bytes 1597440 | tf_op jit(solution)/shard_map/all_gather | solution.py:59
  7.9 211.7 %all-gather.18.cloned.1.call-start = ((), (), s32[]{:S(2)}) async-start(), calls=%async_computation.5 | async-start | bytes 1597440 | tf_op jit(solution)/shard_map/all_gather | solution.py:60
  8.7 314.5 %all-gather.14.cloned.1.call-start = ((), (), s32[]{:S(2)}) async-start(), calls=%async_computation.3 | async-start | bytes 1597440 | tf_op jit(solution)/shard_map/all_gather | solution.py:61
  9.4 417.1 %all-gather.20.cloned.1.call-start = ((), (), s32[]{:S(2)}) async-start(), calls=%async_computation.6 | async-start | bytes 1597440 | tf_op jit(solution)/shard_map/all_gather | solution.py:62
  10.0 526.0 %all-gather.22.cloned.1.call-start = ((), (), s32[]{:S(2)}) async-start(), calls=%async_computation.7 | async-start | bytes 6389760 | tf_op jit(solution)/shard_map/all_gather | solution.py:86
  10.6 633.0 %all-gather.12.cloned.1.call-start = ((), (), s32[]{:S(2)}) async-start(), calls=%async_computation.1 | async-start | bytes 4792320 | tf_op jit(solution)/shard_map/all_gather | solution.py:87
  11.1 1675.4 %reduce-scatter.12.cloned.1.call-start = ((), (), s32[]{:S(2)}) async-start(), calls=%async_computation.2 | async-start | bytes 9584640 | tf_op jit(solution)/shard_map/reduce_scatter | solution.py:116
  659.7 1028.2 %all-reduce.26.cloned.1.call-start = ((), (), s32[]{:S(2)}) async-start(), calls=%async_computation.8 | async-start | bytes 397312 | tf_op jit(solution)/shard_map/psum | solution.py:171
  1056.2 21.5 %collective-permute-start.14 = (f32[16,768]{1,0:T(8,128)S(1)}, f32[16,768]{1,0:T(8,128)S(1)}, u32[]{:S(2)}, u32[]{:S(2)}) collective-permute-start(f32[16,768]{1,0:T(8,128)S(1)} %get-tuple-element.42), channel_id=1, source_target_pairs={{0,30},{2,32},{4,34},{6,36},{8,38},{10,40},{12,42},{14,44},{16,46}... | collective-permute-start | bytes 147464
  1059.0 12.8 collective-permute-start.47
  1061.5 12.4 collective-permute-start.31
  1066.4 16.4 collective-permute-start.13
  1071.8 13.9 collective-permute-start.12
  1074.0 13.8 collective-permute-start.11
  1075.3 16.1 collective-permute-start.10
  1077.8 14.9 collective-permute-start.9
  1082.8 14.4 collective-permute-start.8
  1085.7 12.8 collective-permute-start.7
  1087.8 13.3 collective-permute-start.6
  1091.4 13.3 collective-permute-start.5
  1092.7 15.7 collective-permute-start.4
  1097.2 12.5 collective-permute-start.3
  1098.5 12.6 collective-permute-start.2
  1114.3 12.5 collective-permute-start.26
  1118.9 13.0 collective-permute-start.24
  1126.8 13.2 collective-permute-start.21
  1128.2 14.4 collective-permute-start.20
  1131.9 14.1 collective-permute-start.19
  1133.8 13.6 collective-permute-start.18
  1136.1 12.6 collective-permute-start.17
  1146.0 13.8 collective-permute-start.45
  1147.4 14.5 collective-permute-start.44
  1148.7 16.0 collective-permute-start.43
  1150.0 16.9 collective-permute-start.42
  1151.3 17.6 %collective-permute-start.41 = (f32[16,768]{1,0:T(8,128)S(1)}, f32[16,768]{1,0:T(8,128)S(1)}, u32[]{:S(2)}, u32[]{:S(2)}) collective-permute-start(f32[16,768]{1,0:T(8,128)S(1)} %get-tuple-element.44), channel_id=1, source_target_pairs={{0,20},{2,22},{4,24},{6,26},{8,28},{10,30},{12,32},{14,34},{16,36}... | collective-permute-start | bytes 147464
  1159.8 13.1 collective-permute-start.40
  1161.9 12.4 collective-permute-start.39
  1167.0 12.7 collective-permute-start.37
  1168.9 14.5 collective-permute-start.36
  1172.9 13.0 collective-permute-start.35
  1174.3 12.9 collective-permute-start.34
  1176.3 12.3 collective-permute-start.33
  1194.6 12.7 collective-permute-start.56
  1203.9 13.5 collective-permute-start.52
  1207.3 283.1 %collective-permute-start.51 = (f32[16,768]{1,0:T(8,128)S(1)}, f32[16,768]{1,0:T(8,128)S(1)}, u32[]{:S(2)}, u32[]{:S(2)}) collective-permute-start(f32[16,768]{1,0:T(8,128)S(1)} %get-tuple-element.45), channel_id=1, source_target_pairs={{0,8},{2,10},{4,12},{6,14},{8,16},{10,18},{12,20},{14,22},{16,24},... | collective-permute-start | bytes 147464
  1208.6 283.8 %collective-permute-start.50 = (f32[16,768]{1,0:T(8,128)S(1)}, f32[16,768]{1,0:T(8,128)S(1)}, u32[]{:S(2)}, u32[]{:S(2)}) collective-permute-start(f32[16,768]{1,0:T(8,128)S(1)} %get-tuple-element.45), channel_id=1, source_target_pairs={{0,6},{2,8},{4,10},{6,12},{8,14},{10,16},{12,18},{14,20},{16,22},{... | collective-permute-start | bytes 147464
  1210.8 283.5 %collective-permute-start.49 = (f32[16,768]{1,0:T(8,128)S(1)}, f32[16,768]{1,0:T(8,128)S(1)}, u32[]{:S(2)}, u32[]{:S(2)}) collective-permute-start(f32[16,768]{1,0:T(8,128)S(1)} %get-tuple-element.45), channel_id=1, source_target_pairs={{0,4},{2,6},{4,8},{6,10},{8,12},{10,14},{12,16},{14,18},{16,20},{1... | collective-permute-start | bytes 147464
  1213.7 282.6 %collective-permute-start.48 = (f32[16,768]{1,0:T(8,128)S(1)}, f32[16,768]{1,0:T(8,128)S(1)}, u32[]{:S(2)}, u32[]{:S(2)}) collective-permute-start(f32[16,768]{1,0:T(8,128)S(1)} %get-tuple-element.45), channel_id=1, source_target_pairs={{0,2},{2,4},{4,6},{6,8},{8,10},{10,12},{12,14},{14,16},{16,18},{18... | collective-permute-start | bytes 147464
  1217.4 280.9 %collective-permute-start.79 = (f32[12,3072]{1,0:T(8,128)S(1)}, f32[12,3072]{1,0:T(8,128)S(1)}, u32[]{:S(2)}, u32[]{:S(2)}) collective-permute-start(f32[12,3072]{1,0:T(8,128)S(1)} %slice.4), channel_id=1, source_target_pairs={{0,32},{2,34},{4,36},{6,38},{8,40},{10,42},{12,44},{14,46},{16,48}... | collective-permute-start | bytes 442376
  1490.4 97.0 %collective-permute-start.78 = (f32[16,3072]{1,0:T(8,128)S(1)}, f32[16,3072]{1,0:T(8,128)}, u32[]{:S(2)}, u32[]{:S(2)}) collective-permute-start(f32[16,3072]{1,0:T(8,128)S(1)} %copy-done.21), channel_id=1, source_target_pairs={{0,30},{2,32},{4,34},{6,36},{8,38},{10,40},{12,42},{14,44},{16,46}... | collective-permute-start | bytes 589832
  1492.4 108.0 %collective-permute-start.77 = (f32[16,3072]{1,0:T(8,128)S(1)}, f32[16,3072]{1,0:T(8,128)}, u32[]{:S(2)}, u32[]{:S(2)}) collective-permute-start(f32[16,3072]{1,0:T(8,128)S(1)} %copy-done.21), channel_id=1, source_target_pairs={{0,28},{2,30},{4,32},{6,34},{8,36},{10,38},{12,40},{14,42},{16,44}... | collective-permute-start | bytes 589832
  1494.3 109.5 %collective-permute-start.76 = (f32[16,3072]{1,0:T(8,128)S(1)}, f32[16,3072]{1,0:T(8,128)}, u32[]{:S(2)}, u32[]{:S(2)}) collective-permute-start(f32[16,3072]{1,0:T(8,128)S(1)} %copy-done.21), channel_id=1, source_target_pairs={{0,26},{2,28},{4,30},{6,32},{8,34},{10,36},{12,38},{14,40},{16,42}... | collective-permute-start | bytes 589832
  1496.3 108.8 %collective-permute-start.75 = (f32[16,3072]{1,0:T(8,128)S(1)}, f32[16,3072]{1,0:T(8,128)}, u32[]{:S(2)}, u32[]{:S(2)}) collective-permute-start(f32[16,3072]{1,0:T(8,128)S(1)} %copy-done.21), channel_id=1, source_target_pairs={{0,24},{2,26},{4,28},{6,30},{8,32},{10,34},{12,36},{14,38},{16,40}... | collective-permute-start | bytes 589832
  1498.3 110.5 %collective-permute-start.74 = (f32[16,3072]{1,0:T(8,128)S(1)}, f32[16,3072]{1,0:T(8,128)}, u32[]{:S(2)}, u32[]{:S(2)}) collective-permute-start(f32[16,3072]{1,0:T(8,128)S(1)} %copy-done.21), channel_id=1, source_target_pairs={{0,22},{2,24},{4,26},{6,28},{8,30},{10,32},{12,34},{14,36},{16,38}... | collective-permute-start | bytes 589832
  1587.4 25.8 %collective-permute-start.73 = (f32[16,3072]{1,0:T(8,128)S(1)}, f32[16,3072]{1,0:T(8,128)S(1)}, u32[]{:S(2)}, u32[]{:S(2)}) collective-permute-start(f32[16,3072]{1,0:T(8,128)S(1)} %copy-done.21), channel_id=1, source_target_pairs={{0,20},{2,22},{4,24},{6,26},{8,28},{10,30},{12,32},{14,34},{16,36}... | collective-permute-start | bytes 589832
  1600.3 18.4 %collective-permute-start.72 = (f32[16,3072]{1,0:T(8,128)S(1)}, f32[16,3072]{1,0:T(8,128)S(1)}, u32[]{:S(2)}, u32[]{:S(2)}) collective-permute-start(f32[16,3072]{1,0:T(8,128)S(1)} %copy-done.21), channel_id=1, source_target_pairs={{0,18},{2,20},{4,22},{6,24},{8,26},{10,28},{12,30},{14,32},{16,34}... | collective-permute-start | bytes 589832
  1603.8 16.9 collective-permute-start.71
  1605.1 18.0 %collective-permute-start.70 = (f32[16,3072]{1,0:T(8,128)S(1)}, f32[16,3072]{1,0:T(8,128)S(1)}, u32[]{:S(2)}, u32[]{:S(2)}) collective-permute-start(f32[16,3072]{1,0:T(8,128)S(1)} %copy-done.21), channel_id=1, source_target_pairs={{0,14},{2,16},{4,18},{6,20},{8,22},{10,24},{12,26},{14,28},{16,30}... | collective-permute-start | bytes 589832
  1608.8 26.4 %collective-permute-start.69 = (f32[16,3072]{1,0:T(8,128)S(1)}, f32[16,3072]{1,0:T(8,128)S(1)}, u32[]{:S(2)}, u32[]{:S(2)}) collective-permute-start(f32[16,3072]{1,0:T(8,128)S(1)} %copy-done.21), channel_id=1, source_target_pairs={{0,12},{2,14},{4,16},{6,18},{8,20},{10,22},{12,24},{14,26},{16,28}... | collective-permute-start | bytes 589832
  1613.2 26.6 %collective-permute-start.68 = (f32[16,3072]{1,0:T(8,128)S(1)}, f32[16,3072]{1,0:T(8,128)}, u32[]{:S(2)}, u32[]{:S(2)}) collective-permute-start(f32[16,3072]{1,0:T(8,128)S(1)} %copy-done.21), channel_id=1, source_target_pairs={{0,10},{2,12},{4,14},{6,16},{8,18},{10,20},{12,22},{14,24},{16,26}... | collective-permute-start | bytes 589832
  1618.7 21.1 %collective-permute-start.67 = (f32[16,3072]{1,0:T(8,128)S(1)}, f32[16,3072]{1,0:T(8,128)}, u32[]{:S(2)}, u32[]{:S(2)}) collective-permute-start(f32[16,3072]{1,0:T(8,128)S(1)} %copy-done.21), channel_id=1, source_target_pairs={{0,8},{2,10},{4,12},{6,14},{8,16},{10,18},{12,20},{14,22},{16,24},... | collective-permute-start | bytes 589832
  1620.7 19.1 %collective-permute-start.66 = (f32[16,3072]{1,0:T(8,128)S(1)}, f32[16,3072]{1,0:T(8,128)}, u32[]{:S(2)}, u32[]{:S(2)}) collective-permute-start(f32[16,3072]{1,0:T(8,128)S(1)} %copy-done.21), channel_id=1, source_target_pairs={{0,6},{2,8},{4,10},{6,12},{8,14},{10,16},{12,18},{14,20},{16,22},{... | collective-permute-start | bytes 589832
  1623.2 16.6 collective-permute-start.65
  1639.8 77.2 %all-reduce.28.cloned.1.call-start = ((), (), s32[]{:S(2)}) async-start(), calls=%async_computation.9 | async-start | bytes 688128 | tf_op jit(solution)/shard_map/psum | solution.py:171
  (123 other events, 6382.5 us)
Sparse Core Ops, SparseCore 0:
  9.7 106.2 all-gather.15
  117.8 101.8 all-gather.17
  221.4 101.7 all-gather.13
  324.7 101.7 all-gather.19
  428.1 107.8 all-gather.21
  537.6 105.9 all-gather.11
  659.8 303.9 reduce-scatter.11
  1639.9 27.1 all-reduce.25
  1686.7 30.2 all-reduce.27
where the time goes:
time: 1760 us; the launch traced here: 1740 us
  blocking collectives  774 us (44%)
  waiting for transfers between devices  491 us (28%)
  starting transfers between devices  208 us (12%)
  local copies, waits for them, and re-layouts  182 us (10%)
  matrix products  55.2 us (3%)
  between operations  18.8 us (1%)
    unnamed x3, blocking collectives  774 us
    unnamed x80, starting transfers between devices  207 us
    unnamed x239, local copies, waits for them, and re-layouts  181 us
    all_gather x1, waiting for transfers between devices, per_device(): lax.all_gather(up_weight, 'fsdp', axis=0, tiled=True)  101 us
    all_gather x1, waiting for transfers between devices, per_device(): lax.all_gather(value_weight, 'fsdp', axis=0, tiled=True)  100 us
    all_gather x1, waiting for transfers between devices, per_device(): lax.all_gather(out_weight, 'fsdp', axis=0, tiled=True)  100 us
    all_gather x1, waiting for transfers between devices, per_device(): lax.all_gather(down_weight, 'fsdp', axis=0, tiled=True)  100 us
    all_gather x1, waiting for transfers between devices, per_device(): lax.all_gather(key_weight, 'fsdp', axis=0, tiled=True)  54.2 us
  transfers between devices with their start and end apart: 89, of which 7 were waited for; matrix products, arithmetic and copies ran while one was open for 33% of the time, Pallas kernels for 0%

commit v1 on v0

v1 whole, which is shorter than its diff:
```python
import functools

import jax
import jax.numpy as jnp
from jax import lax
from jax.experimental import pallas as pl
from jax.experimental.pallas import tpu as pltpu
from jax.sharding import PartitionSpec as P

HEADS = 24
HEAD_DIM = 32
D = 768
FF = 3072
BF = jnp.bfloat16
F32 = jnp.float32
MESH = pl.DeviceIdType.MESH

WIDE = 6400
START = (0, 2560)
HALF = (1280, 1920)
PART = ((640, 640), (896, 1024), (768, 768))
LOW = ((256, 256), (384, 512), (384, 384))
N_RECV = 240
N_SEND = 48


class Place:
    def __init__(self):
        f = lax.axis_index("fsdp")
        self.r = lax.axis_index("rep")
        self.c = lax.rem(f, 2)
        self.zl = lax.rem(lax.div(f, 2), 2)
        self.y = lax.rem(lax.div(f, 4), 4)
        self.x = lax.div(f, 16)

    def dev(self, dx=0, dy=0, zl=None, c=None, r=None):
        x, y = wrap(self.x, dx), wrap(self.y, dy)
        zl = self.zl if zl is None else zl
        c = self.c if c is None else c
        return {"fsdp": x * 16 + y * 4 + zl * 2 + c, "rep": self.r if r is None else r}

    def sibling(self):
        return self.dev(c=1 - self.c)

    def pair(self):
        return self.dev(zl=1 - self.zl)

    def other(self):
        return self.dev(r=1 - self.r)


def wrap(v, d):
    return v if d == 0 else lax.rem(v + (d + 4), 4)


class Wire:
    def __init__(self, place, send, recv):
        self.place, self.send_sem, self.recv_sem = place, send, recv
        self.n = self.m = 0
        self.open = {}

    def slot(self):
        k = self.m % N_SEND
        self.m += 1
        if k in self.open:
            self.open.pop(k).wait_send()
        return k

    def put(self, src, dst, to):
        k = self.slot()
        assert self.n < N_RECV
        copy = pltpu.make_async_remote_copy(
            src_ref=src,
            dst_ref=dst,
            send_sem=self.send_sem.at[k],
            recv_sem=self.recv_sem.at[self.n],
            device_id=to,
            device_id_type=MESH,
        )
        copy.start()
        self.open[k] = copy
        self.n += 1
        return copy

    def drain(self):
        for copy in self.open.values():
            copy.wait_send()
        self.open = {}


def greet(place):
    barrier = pltpu.get_barrier_semaphore()
    peers = [place.sibling(), place.pair(), place.other()]
    peers += [place.dev(dx=1), place.dev(dx=-1), place.dev(dy=1), place.dev(dy=-1)]
    for peer in peers:
        pl.semaphore_signal(barrier, inc=1, device_id=peer, device_id_type=MESH)
    pl.semaphore_wait(barrier, len(peers))


def span(g, p, h):
    if h is None:
        return 0, PART[g][p]
    return (0, LOW[g][p]) if h == 0 else (LOW[g][p], PART[g][p] - LOW[g][p])


def cols(g, p, c, h=None):
    off, width = span(g, p, h)
    base = START[g] + (PART[g][0] if p else 0) + off
    return pl.ds(pl.multiple_of(base + c * HALF[g], 128), width)


def block(wide, down, g, p, c, bx, by, h=None):
    if g < 2:
        return wide.at[bx, by, :, cols(g, p, c, h)]
    off, width = span(g, p, h)
    return down.at[bx, by, p, c, :, pl.ds(off, width)]


def gather_stream(wire, wide, down, g, p):
    me = wire.place

    def piece(du, dw, h=None, c=me.c):
        dx, dy = (du, dw) if p == 0 else (dw, du)
        return block(wide, down, g, p, c, wrap(me.x, dx), wrap(me.y, dy), h)

    def first(d):
        return me.dev(dx=d) if p == 0 else me.dev(dy=d)

    def second(d):
        return me.dev(dy=d) if p == 0 else me.dev(dx=d)

    def go(du, dw, to, h=None):
        ref = piece(du, dw, h)
        return wire.put(ref, ref, to)

    sib = []
    up, dn = {}, {}

    def spread(du):
        up[du] = go(du, 0, second(1))
        dn[du] = go(du, 0, second(-1))

    a, b = go(0, 0, first(1)), go(0, 0, first(-1))
    spread(0)
    yield
    a.wait_recv()
    far_a = go(-1, 0, first(1), 0)
    spread(-1)
    sib.append(go(-1, 0, me.sibling()))
    b.wait_recv()
    far_b = go(1, 0, first(-1), 1)
    spread(1)
    sib.append(go(1, 0, me.sibling()))
    yield
    far_a.wait_recv()
    far_b.wait_recv()
    spread(2)
    sib.append(go(2, 0, me.sibling()))
    yield
    far = {}
    for du in (0, -1, 1, 2):
        up[du].wait_recv()
        far_a = go(du, -1, second(1), 0)
        sib.append(go(du, -1, me.sibling()))
        dn[du].wait_recv()
        far_b = go(du, 1, second(-1), 1)
        sib.append(go(du, 1, me.sibling()))
        far[du] = far_a, far_b
        if du == -1:
            yield
    yield
    for du in (0, -1, 1, 2):
        far[du][0].wait_recv()
        far[du][1].wait_recv()
        sib.append(go(du, 2, me.sibling()))
    yield
    for copy in sib:
        copy.wait_recv()
    yield


def join(stage, wide, me, g):
    width = 2 * HALF[g]
    step = 640
    def body(i, _):
        at = pl.ds(pl.multiple_of(START[g] + i * step, 128), step)
        rows = [stage[o, :, at].astype(F32)[:12] for o in range(4)]
        wide[me.x, me.y, :, at] = jnp.concatenate(rows, axis=0).astype(BF)
        return 0
    lax.fori_loop(0, width // step, body, 0)


def gather_stage0(wire, own, own_down, stage, wide, down, g):
    me = wire.place
    mine = 2 * me.zl + me.c
    if g < 2:
        at = pl.ds(START[g], 2 * HALF[g])
        src, dst = own.at[:, at], lambda o: stage.at[o, :, at]
        hers = stage.at[2 * (1 - me.zl) + me.c, :, at]
        stage[mine, :, at] = own[:, at]
    else:
        src, dst = own_down, lambda o: down.at[me.x, me.y, me.zl, me.c]
        hers = down.at[me.x, me.y, 1 - me.zl, me.c]
        down[me.x, me.y, me.zl, me.c] = own_down[...]
    a = wire.put(src, dst(mine), me.pair())
    b = wire.put(src, dst(mine), me.sibling())
    yield
    a.wait_recv()
    c = wire.put(hers, hers, me.sibling())
    yield
    b.wait_recv()
    c.wait_recv()
    if g < 2:
        join(stage, wide, me, g)
    yield


def run(*streams):
    live = list(streams)
    while live:
        live = [s for s in live if next(s, StopIteration) is not StopIteration]


def chain(*streams):
    for s in streams:
        yield from s


def reduce_shapes():
    shapes = []
    for g in range(3):
        for p in range(2):
            n, low = PART[g][p], LOW[g][p]
            high = n - low
            shapes += [
                ((4, 4, 48, n), BF),
                ((4, 48, low), BF),
                ((4, 48, high), BF),
                ((4, 48, n), BF),
                ((4, 48, n), BF),
                ((48, low), BF),
                ((48, high), BF),
                ((48, n), BF),
                ((48, n), BF),
            ]
    return shapes


def reduce_stream(wire, wide, down, bufs, tail, g, p):
    me = wire.place
    sb, b1p, b1m, b2p, b2m, c1p, c1m, c2p, c2m = bufs
    low, n = LOW[g][p], PART[g][p]
    lo, hi = pl.ds(0, low), pl.ds(low, n - low)

    def first(d):
        return me.dev(dx=d) if p == 0 else me.dev(dy=d)

    def second(d):
        return me.dev(dy=d) if p == 0 else me.dev(dx=d)

    u, w = (me.x, me.y) if p == 0 else (me.y, me.x)

    def one(ui, wi, h=None, c=me.c):
        bx, by = (ui, wi) if p == 0 else (wi, ui)
        return block(wide, down, g, p, c, bx, by, h)

    def line(ui, h=None, c=me.c):
        bx, by = (ui, slice(None)) if p == 0 else (slice(None), ui)
        return block(wide, down, g, p, c, bx, by, h)

    def everything(c):
        return block(wide, down, g, p, c, slice(None), slice(None))

    def add_line(ui, h, fn):
        def body(i, _):
            ref = one(ui, i, h)
            ref[...] = fn(ref[...], i)
            return 0
        lax.fori_loop(0, 4, body, 0)

    got = wire.put(everything(1 - me.c), sb, me.sibling())
    yield
    got.wait_recv()

    def with_sibling(ui):
        def fn(v, i):
            bx, by = (ui, i) if p == 0 else (i, ui)
            return v + sb[bx, by]
        add_line(ui, None, fn)

    with_sibling(wrap(u, 2))
    r1p = wire.put(line(wrap(u, 2), 0), b1p, first(1))
    r1m = wire.put(line(wrap(u, 2), 1), b1m, first(-1))
    with_sibling(wrap(u, 1))
    r2p_hi = wire.put(line(wrap(u, 1), 1), b2p.at[:, :, hi], first(1))
    with_sibling(wrap(u, -1))
    r2m_lo = wire.put(line(wrap(u, -1), 0), b2m.at[:, :, lo], first(-1))
    with_sibling(u)
    yield
    r1p.wait_recv()
    add_line(wrap(u, 1), 0, lambda v, i: v + b1p[i])
    r2p_lo = wire.put(line(wrap(u, 1), 0), b2p.at[:, :, lo], first(1))
    r1m.wait_recv()
    add_line(wrap(u, -1), 1, lambda v, i: v + b1m[i])
    r2m_hi = wire.put(line(wrap(u, -1), 1), b2m.at[:, :, hi], first(-1))
    yield
    for copy in (r2p_hi, r2m_lo, r2p_lo, r2m_hi):
        copy.wait_recv()

    def close(wi):
        ref = one(u, wi)
        total = ref[...].astype(F32) + b2p[wi].astype(F32) + b2m[wi].astype(F32)
        ref[...] = total.astype(BF)

    close(wrap(w, 2))
    r1p = wire.put(one(u, wrap(w, 2), 0), c1p, second(1))
    r1m = wire.put(one(u, wrap(w, 2), 1), c1m, second(-1))
    close(wrap(w, 1))
    r2p_hi = wire.put(one(u, wrap(w, 1), 1), c2p.at[:, hi], second(1))
    close(wrap(w, -1))
    r2m_lo = wire.put(one(u, wrap(w, -1), 0), c2m.at[:, lo], second(-1))
    close(w)
    yield
    r1p.wait_recv()
    ref = one(u, wrap(w, 1), 0)
    ref[...] = ref[...] + c1p[...]
    r2p_lo = wire.put(ref, c2p.at[:, lo], second(1))
    r1m.wait_recv()
    ref = one(u, wrap(w, -1), 1)
    ref[...] = ref[...] + c1m[...]
    r2m_hi = wire.put(ref, c2m.at[:, hi], second(-1))
    yield
    for copy in (r2p_hi, r2m_lo, r2p_lo, r2m_hi):
        copy.wait_recv()
    total = one(u, w)[...].astype(F32) + c2p[...].astype(F32) + c2m[...].astype(F32)
    yield from tail(wire, total, g, p)


def tail_shapes():
    shapes = []
    for g in range(2):
        for p in range(2):
            n = PART[g][p]
            shapes += [((4, 16, n), BF), ((2, 16, n), BF), ((2, 16, n), BF), ((2, 16, n), BF), ((16, n), F32)]
    shapes += [((2, 48, 768), BF), ((48, 768), BF), ((48, 768), BF), ((48, 768), BF)]
    return shapes


def make_tail(bufs, final, final_down):
    done = []

    def tail(wire, total, g, p):
        me = wire.place
        if g < 2:
            st, rz, tt, rr, so = bufs[10 * g + 5 * p : 10 * g + 5 * p + 5]
            at = cols(g, p, me.c)
            zero = jnp.zeros((4, total.shape[1]), F32)
            for o in range(4):
                st[o] = jnp.concatenate([total[12 * o : 12 * o + 12], zero], axis=0).astype(BF)
            a = wire.put(st.at[pl.ds(2 * (1 - me.zl), 2)], rz, me.pair())
            yield
            a.wait_recv()
            tt[...] = (st[pl.ds(2 * me.zl, 2)].astype(F32) + rz[...].astype(F32)).astype(BF)
            b = wire.put(tt, rr, me.other())
            yield
            b.wait_recv()
            so[...] = tt[1 - me.c].astype(F32) + rr[1 - me.c].astype(F32)
            c = wire.put(so, final.at[:, at], me.sibling())
            final[:, at] = tt[me.c].astype(F32) + rr[me.c].astype(F32)
            yield
            c.wait_recv()
            yield
        else:
            sd, rz, tt, rr = bufs[20:24]
            sd[p] = total.astype(BF)
            done.append(p)
            if len(done) < 2:
                return
            a = wire.put(sd.at[1 - me.zl], rz, me.pair())
            yield
            a.wait_recv()
            tt[...] = (sd[me.zl].astype(F32) + rz[...].astype(F32)).astype(BF)
            b = wire.put(tt, rr, me.other())
            yield
            b.wait_recv()
            final_down[...] = tt[...].astype(F32) + rr[...].astype(F32)
            yield

    return tail


def gather_kernel(own, own_down, wide, down, stage, send, recv):
    place = Place()
    greet(place)
    wire = Wire(place, send, recv)
    front = [gather_stage0(wire, own, own_down, stage, wide, down, g) for g in range(3)]
    run(*front)
    run(*[gather_stream(wire, wide, down, g, p) for g in range(3) for p in range(2)])
    wire.drain()


def reduce_kernel(g_wide, g_down, final, final_down, wide, down, sems, *rest):
    nb = len(reduce_shapes())
    bufs, tbufs, (send, recv) = rest[:nb], rest[nb:-2], rest[-2:]
    place = Place()
    greet(place)
    a = pltpu.make_async_copy(g_wide, wide, sems.at[0])
    b = pltpu.make_async_copy(g_down, down, sems.at[1])
    a.start()
    b.start()
    a.wait()
    b.wait()
    wire = Wire(place, send, recv)
    tail = make_tail(tbufs, final, final_down)
    streams = []
    for g in (2, 1, 0):
        for p in range(2):
            k = 9 * (2 * g + p)
            streams.append(reduce_stream(wire, wide, down, bufs[k : k + 9], tail, g, p))
    run(*streams)
    wire.drain()


ANY = pl.BlockSpec(memory_space=pl.ANY)
VM = pl.BlockSpec(memory_space=pltpu.VMEM)


def gather_call(own, own_down):
    return pl.pallas_call(
        gather_kernel,
        out_shape=(
            jax.ShapeDtypeStruct((4, 4, 48, WIDE), BF),
            jax.ShapeDtypeStruct((4, 4, 2, 2, 48, 768), BF),
        ),
        in_specs=[VM, VM],
        out_specs=(VM, VM),
        scratch_shapes=[
            pltpu.VMEM((4, 16, WIDE), BF),
            pltpu.SemaphoreType.DMA((N_SEND,)),
            pltpu.SemaphoreType.DMA((N_RECV,)),
        ],
        compiler_params=pltpu.CompilerParams(
            collective_id=0, has_side_effects=True, vmem_limit_bytes=56 << 20
        ),
        name="gather",
    )(own, own_down)


def reduce_call(g_wide, g_down):
    return pl.pallas_call(
        reduce_kernel,
        out_shape=(
            jax.ShapeDtypeStruct((16, WIDE), F32),
            jax.ShapeDtypeStruct((48, 768), F32),
        ),
        in_specs=[ANY, ANY],
        out_specs=(VM, VM),
        scratch_shapes=[
            pltpu.VMEM((4, 4, 48, WIDE), BF),
            pltpu.VMEM((4, 4, 2, 2, 48, 768), BF),
            pltpu.SemaphoreType.DMA((2,)),
            *[pltpu.VMEM(s, t) for s, t in reduce_shapes()],
            *[pltpu.VMEM(s, t) for s, t in tail_shapes()],
            pltpu.SemaphoreType.DMA((N_SEND,)),
            pltpu.SemaphoreType.DMA((N_RECV,)),
        ],
        compiler_params=pltpu.CompilerParams(
            collective_id=1, has_side_effects=True, vmem_limit_bytes=56 << 20
        ),
        name="reduce",
    )(g_wide, g_down)


def pack_own(n1g, n1b, wq, wk, wv, wo, n2g, n2b, wu):
    def pad(*vs):
        return jnp.pad(jnp.stack(vs, axis=1), ((0, 0), (0, 128 - len(vs))))

    own = jnp.concatenate([wq, wk, wv, pad(n1g, n1b), pad(n2g, n2b), wo, wu], axis=1)
    return jnp.pad(own, ((0, 4), (0, 0)))


def layer_norm(values, gain, shift):
    centre = jnp.mean(values, axis=-1, keepdims=True)
    centred = values - centre
    spread = jnp.mean(centred * centred, axis=-1, keepdims=True)
    return centred * lax.rsqrt(spread + 1e-05) * gain + shift


def masked_scores(query, key, segment_ids):
    tokens = query.shape[0]
    query_heads = query.reshape(tokens, HEADS, HEAD_DIM)
    key_heads = key.reshape(tokens, HEADS, HEAD_DIM)
    scaled = jnp.einsum(
        "qhd,khd->hqk", query_heads, key_heads, preferred_element_type=jnp.float32
    ) * HEAD_DIM ** (-0.5)
    segments = segment_ids.reshape(tokens)
    rows_iota = lax.broadcasted_iota(jnp.int32, (tokens, tokens), 0)
    cols_iota = lax.broadcasted_iota(jnp.int32, (tokens, tokens), 1)
    allowed = (rows_iota >= cols_iota) & (segments[:, None] == segments[None, :])
    return jnp.where(allowed[None], scaled, -1e30)


def matmul_back(left, right):
    return jnp.einsum("te,de->td", left, right, preferred_element_type=jnp.float32)


def matmul_outer(left, right):
    return jnp.einsum("td,te->de", left, right, preferred_element_type=jnp.float32)


def per_device(
    block_input, segment_ids, norm1_gain, norm1_bias, query_weight, key_weight, value_weight, out_weight,
    norm2_gain, norm2_bias, up_weight, down_weight, out_cotangent,
):
    tokens = block_input.shape[0]
    inputs = block_input.astype(F32)
    own = pack_own(
        norm1_gain, norm1_bias, query_weight, key_weight, value_weight, out_weight, norm2_gain, norm2_bias, up_weight
    )
    wide, down = gather_call(own, down_weight)
    wide = wide.reshape(D, WIDE)
    down = down.reshape(FF, D)
    wq, wk, wv = wide[:, :768], wide[:, 768:1536], wide[:, 1536:2304]
    gain1, bias1 = wide[:, 2304].astype(F32), wide[:, 2305].astype(F32)
    gain2, bias2 = wide[:, 2432].astype(F32), wide[:, 2433].astype(F32)
    wo, wu = wide[:, 2560:3328], wide[:, 3328:]
    normed1_f, norm1_pull = jax.vjp(layer_norm, inputs, gain1, bias1)
    normed1 = normed1_f.astype(jnp.bfloat16)
    query = jnp.dot(normed1, wq, preferred_element_type=jnp.float32).astype(jnp.bfloat16)
    key = jnp.dot(normed1, wk, preferred_element_type=jnp.float32).astype(jnp.bfloat16)
    value = jnp.dot(normed1, wv, preferred_element_type=jnp.float32).astype(jnp.bfloat16)
    scores = masked_scores(query, key, segment_ids)
    maximum = jnp.max(scores, axis=-1, keepdims=True)
    exponent = jnp.exp(scores - maximum)
    summed = jnp.sum(exponent, axis=-1, keepdims=True)
    probs = exponent / summed
    log_total = maximum + jnp.log(summed)
    value_heads = value.reshape(tokens, HEADS, HEAD_DIM)
    mixed = jnp.einsum(
        "hqk,khd->qhd", probs.astype(jnp.bfloat16), value_heads, preferred_element_type=jnp.float32
    )
    mixed = mixed.reshape(tokens, HEADS * HEAD_DIM).astype(jnp.bfloat16)
    hidden_state = inputs + jnp.dot(mixed, wo, preferred_element_type=jnp.float32)
    normed2_f, norm2_pull = jax.vjp(layer_norm, hidden_state, gain2, bias2)
    normed2 = normed2_f.astype(jnp.bfloat16)
    pre_act = jnp.dot(normed2, wu, preferred_element_type=jnp.float32)
    activated_f, gelu_pull = jax.vjp(jax.nn.gelu, pre_act)
    activated = activated_f.astype(jnp.bfloat16)
    output = (
        hidden_state + jnp.dot(activated, down, preferred_element_type=jnp.float32)
    ).astype(jnp.bfloat16)
    down_term = matmul_outer(activated, out_cotangent)
    act_grad = matmul_back(out_cotangent, down)
    pre_grad = gelu_pull(act_grad)[0].astype(jnp.bfloat16)
    up_term = matmul_outer(normed2, pre_grad)
    normed2_grad = matmul_back(pre_grad, wu)
    hidden_extra, gain2_term, bias2_term = norm2_pull(normed2_grad)
    hidden_grad = out_cotangent.astype(jnp.float32) + hidden_extra
    branch_grad = hidden_grad.astype(jnp.bfloat16)
    outproj_term = matmul_outer(mixed, branch_grad)
    mixed_grad = matmul_back(branch_grad, wo).astype(jnp.bfloat16)
    mixed_heads = mixed_grad.reshape(tokens, HEADS, HEAD_DIM)
    again_probs = jnp.exp(masked_scores(query, key, segment_ids) - log_total)
    prob_grad = jnp.einsum(
        "qhd,khd->hqk", mixed_heads, value_heads, preferred_element_type=jnp.float32
    )
    value_act = jnp.einsum(
        "hqk,qhd->khd",
        again_probs.astype(jnp.bfloat16),
        mixed_heads,
        preferred_element_type=jnp.float32,
    )
    value_act = value_act.reshape(tokens, HEADS * HEAD_DIM).astype(jnp.bfloat16)
    row_dot = jnp.sum(prob_grad * again_probs, axis=-1, keepdims=True)
    score_grad = (again_probs * (prob_grad - row_dot)).astype(jnp.bfloat16)
    query_heads = query.reshape(tokens, HEADS, HEAD_DIM)
    key_heads = key.reshape(tokens, HEADS, HEAD_DIM)
    query_act = jnp.einsum(
        "hqk,khd->qhd", score_grad, key_heads, preferred_element_type=jnp.float32
    ) * HEAD_DIM ** (-0.5)
    key_act = jnp.einsum(
        "hqk,qhd->khd", score_grad, query_heads, preferred_element_type=jnp.float32
    ) * HEAD_DIM ** (-0.5)
    query_act = query_act.reshape(tokens, HEADS * HEAD_DIM).astype(jnp.bfloat16)
    key_act = key_act.reshape(tokens, HEADS * HEAD_DIM).astype(jnp.bfloat16)
    query_term = matmul_outer(normed1, query_act)
    key_term = matmul_outer(normed1, key_act)
    value_term = matmul_outer(normed1, value_act)
    normed1_grad = (
        matmul_back(query_act, wq)
        + matmul_back(key_act, wk)
        + matmul_back(value_act, wv)
    )
    input_extra, gain1_term, bias1_term = norm1_pull(normed1_grad)
    input_grad = hidden_grad + input_extra

    def columns(*vs):
        return jnp.pad(jnp.stack(vs, axis=1), ((0, 0), (0, 128 - len(vs)))).astype(BF)

    g_wide = jnp.concatenate(
        [
            query_term.astype(BF),
            key_term.astype(BF),
            value_term.astype(BF),
            columns(gain1_term, bias1_term),
            columns(gain2_term, bias2_term),
            outproj_term.astype(BF),
            up_term.astype(BF),
        ],
        axis=1,
    ).reshape(4, 4, 48, WIDE)
    g_down = down_term.astype(BF).reshape(4, 4, 2, 2, 48, 768)
    total, down_total = reduce_call(g_wide, g_down)
    total = total[:12]
    return (
        output,
        input_grad,
        total[:, 2304],
        total[:, 2305],
        total[:, :768],
        total[:, 768:1536],
        total[:, 1536:2304],
        total[:, 2560:3328],
        total[:, 2432],
        total[:, 2433],
        total[:, 3328:],
        down_total,
    )


def solution(mesh):
    placed = (
        P(("fsdp", "rep"), None),
        P(("fsdp", "rep"), None),
        P("fsdp"),
        P("fsdp"),
        P("fsdp", None),
        P("fsdp", None),
        P("fsdp", None),
        P("fsdp", None),
        P("fsdp"),
        P("fsdp"),
        P("fsdp", None),
        P("fsdp", None),
        P(("fsdp", "rep"), None),
    )
    return jax.shard_map(
        per_device,
        mesh=mesh,
        in_specs=placed,
        out_specs=(
            P(("fsdp", "rep"), None),
            P(("fsdp", "rep"), None),
            P("fsdp"),
            P("fsdp"),
            P("fsdp", None),
            P("fsdp", None),
            P("fsdp", None),
            P("fsdp", None),
            P("fsdp"),
            P("fsdp"),
            P("fsdp", None),
            P("fsdp", None),
        ),
        check_vma=False,
    )
```

time: 1760 us -> 225 us (0.13); the launches traced: 1740 us -> 224 us
  blocking collectives: 774 us -> 0 us
  waiting for transfers between devices: 491 us -> 0 us
  starting transfers between devices: 208 us -> 0 us
  local copies, waits for them, and re-layouts: 182 us -> 28.4 us
  Pallas kernels: 0 us -> 134 us
    unnamed x3 -> x0, blocking collectives: 774 us -> none
    all_gather x6 -> x0, waiting for transfers between devices: 456 us -> none  [the longest x1 101 us: per_device(): lax.all_gather(up_weight, 'fsdp', axis=0, tiled=True)]
    unnamed x80 -> x0, starting transfers between devices: 207 us -> none
    unnamed x239 -> x95, local copies, waits for them, and re-layouts: 181 us -> 13.9 us
    pallas_call x0 -> x2, Pallas kernels: none -> 134 us  [the longest x1 70.2 us: reduce_call(): pl.pallas_call(reduce_kernel, out_shape=(jax.ShapeDtypeStruct((16, WIDE),...]
    psum x2 -> x0, waiting for transfers between devices: 29.1 us -> none  [per_device(): lax.psum((attn_shards[0], attn_shards[1], attn_shards[2], attn_shards[3],...]
  transfers between devices with their start and end apart: 89 -> 0, of which waited for: 7 -> 0; matrix products, arithmetic and copies ran while one was open for 33% -> 0% of each run, Pallas kernels for 0% -> 0%
where the time goes in v1:
time: 225 us; the launch traced here: 224 us
  Pallas kernels  134 us (60%)
  matrix products  52.9 us (24%)
  local copies, waits for them, and re-layouts  28.4 us (13%)
  other arithmetic  7.38 us (3%)
    pallas_call x1, Pallas kernels, reduce_call(): pl.pallas_call(reduce_kernel, out_shape=(jax.ShapeDtypeStruct((16, WIDE),...  70.2 us
    pallas_call x1, Pallas kernels, gather_call(): pl.pallas_call(gather_kernel, out_shape=(jax.ShapeDtypeStruct((4, 4, 48,...  63.7 us
    dot_general x6, matrix products, matmul_outer(): jnp.einsum('td,te->de', left, right, preferred_element_type=jnp.float32)  16.5 us
    unnamed x95, local copies, waits for them, and re-layouts  13.9 us
    dot_general x6, matrix products, matmul_back(): jnp.einsum('te,de->td', left, right, preferred_element_type=jnp.float32)  11.5 us
    dot_general x1, matrix products, per_device(): jnp.einsum('qhd,khd->hqk', mixed_heads, value_heads, preferred_element_ty...  4.56 us

profile of v1, /device:TPU:1, one launch (start us, length us, event | category | flops | bytes accessed | tf_op | source)
XLA Modules:
  0.0 224.0 jit_solution(9155118255415158088)
XLA Ops:
  0.7 0.8 constant_dynamic-update-slice_fusion.6
  1.4 0.7 constant_dynamic-update-slice_fusion.5
  2.2 0.7 constant_dynamic-update-slice_fusion.4
  2.9 0.7 pad_maximum_fusion.2
  3.7 0.7 pad_maximum_fusion.3
  4.5 0.7 constant_dynamic-update-slice_fusion.1
  5.3 0.9 constant_dynamic-update-slice_fusion
  6.2 0.7 pad.22.own
  6.9 63.7 %gather.1 = (bf16[4,4,48,6400]{3,2,1,0:T(8,128)(2,1)}, bf16[4,4,2,2,48,768]{5,4,3,2,1,0:T(8,128)(2,1)}) custom-call(bf16[16,6400]{1,0:T(8,128)(2,1)} %pad.22.own, bf16[48,768]{1,0:T(8,128)(2,1)} %own_down.1), custom_call_target="tpu_custom_call" | custom-call | tf_op jit(solution)/shard_map/gather/pallas_call | solution.py:429
  70.6 1.4 fusion.57
  72.5 0.2 fusion.43
  72.8 1.8 convolution_convert_fusion.9
  74.6 0.2 copy.75
  74.8 2.0 convolution_convert_fusion.8
  76.8 0.2 copy.76
  77.0 1.8 convolution_convert_fusion.7
  78.8 0.2 copy.77
  79.1 1.2 fusion.59
  80.3 1.1 fusion
  81.4 1.6 copy-done
  83.0 1.2 fusion.24
  84.2 2.0 fusion.60
  86.5 0.2 multiply_reduce_fusion.3
  86.8 3.9 %fusion.5 = f32[256,3072]{1,0:T(8,128)S(1)} fusion(bf16[768,6400]{1,0:T(8,128)(2,1)} %bitcast.70, f32[256,768]{1,0:T(8,128)S(1)} %get-tuple-element.43, f32[768]{0:T(1024)S(1)} %get-tuple-element.51, f32[768]{0:T(1024)S(1)} %get-tuple-element.52, f32[256]{0:T(256)S(1)} %fusion.48, f32[256]{0:T(256)S(1)} %broadcast_multiply_fusion), kind=kOutput, calls=%fused_computation.15 | convolution fusion | flops 1208942592 | bytes 8658944 | tf_op jit(solution)/shard_map/dot_general | solution.py:546
  90.8 2.7 %fusion.18 = bf16[256,768]{1,0:T(8,128)(2,1)} fusion(f32[256,768]{1,0:T(8,128)S(1)} %get-tuple-element.43, bf16[3072,768]{1,0:T(8,128)(2,1)S(1)} %bitcast.91, f32[256,3072]{1,0:T(8,128)S(1)} %fusion.5), kind=kOutput, calls=%fused_computation.39 | convolution fusion | flops 1215430656 | bytes 9043968 | tf_op jit(solution)/shard_map/dot_general | solution.py:550
  93.5 3.1 %fusion.13 = bf16[256,3072]{1,0:T(8,128)(2,1)S(1)} fusion(f32[256,3072]{1,0:T(8,128)S(1)} %fusion.5, bf16[3072,768]{1,0:T(8,128)(2,1)S(1)} %bitcast.92, bf16[256,768]{1,0:T(8,128)(2,1)S(1)} %copy-done.6), kind=kOutput, calls=%fused_computation.24 | convolution fusion | flops 1223688192 | bytes 9830400 | tf_op jit(solution)/shard_map/te,de->td/dot_general | solution.py:504
  96.7 2.1 multiply_reduce_fusion.1
  98.8 0.3 fusion.56
  99.4 0.7 copy-done.8
  100.1 0.5 convolution_convert_fusion.6
  100.8 4.6 %multiply_reduce_fusion = (f32[24,256]{1,0:T(8,128)S(1)}, f32[24,256,256]{1,2,0:T(8,128)S(1)}) fusion(f32[24,256,256]{1,2,0:T(8,128)} %copy-done, f32[24,256]{1,0:T(8,128)S(1)} %log_add_fusion, bf16[256,24,32]{0,2,1:T(8,128)(2,1)S(1)} %bitcast.59, bf16[256,24,32]{0,2,1:T(8,128)(2,1)} %bitcast.79), kind=kOutput, calls=%fused_computation.1 | convolution fusion | flops 105375744 | bytes 13418496 | tf_op jit(solution)/shard_map/qhd,khd->hqk/dot_general | solution.py:564
  105.4 0.2 slice-done.1
  105.6 1.8 multiply_convert_fusion
  107.4 1.6 fusion.19
  109.0 1.8 fusion.33
  110.8 1.0 fusion.20
  111.9 1.9 convolution_add_fusion.1
  113.8 1.1 fusion.21
  115.0 2.1 fusion.44
  117.1 0.5 fusion.42
  117.6 1.3 add_add_fusion.2
  118.9 1.6 convolution_convert_fusion.4
  120.5 1.8 copy.88
  122.3 1.1 constant_dynamic-update-slice_fusion.10
  123.5 1.7 convolution_convert_fusion.3
  125.1 1.6 copy.89
  126.7 1.2 constant_dynamic-update-slice_fusion.9
  127.9 1.7 convolution_convert_fusion.2
  129.6 1.6 copy.90
  131.2 1.1 constant_dynamic-update-slice_fusion.8
  132.3 0.2 copy.86
  132.5 0.7 pad_dynamic-update-slice_fusion.1
  133.3 0.2 copy.87
  133.5 0.7 pad_dynamic-update-slice_fusion
  134.2 1.7 convolution_convert_fusion.5
  136.0 0.6 copy.91
  136.6 1.1 constant_dynamic-update-slice_fusion.7
  137.7 5.3 %fusion.1 = bf16[768,6400]{1,0:T(8,128)(2,1)} fusion(bf16[768,6400]{1,0:T(8,128)(2,1)} %constant_dynamic-update-slice_fusion.7, bf16[256,3072]{1,0:T(8,128)(2,1)} %copy-done.31, f32[256,768]{1,0:T(8,128)S(1)} %copy-done.4, f32[768]{0:T(1024)S(1)} %copy-done.23, f32[768]{0:T(1024)S(1)} %get-tuple-element.52, f32[256]{0:T(256)S(1)} %copy-done.21, ...), kind=kOutput, calls=%fused_computation.9 | convolution fusion | flops 1211301888 | bytes 7086080 | tf_op jit(solution)/shard_map/td,te->de/dot_general | solution.py:508
  143.1 4.5 %convolution_convert_fusion = bf16[3072,768]{1,0:T(8,128)(2,1)} fusion(bf16[256,768]{1,0:T(8,128)(2,1)S(1)} %copy-done.7, f32[256,3072]{1,0:T(8,128)S(1)} %copy-done.30), kind=kOutput, calls=%fused_computation.7 | convolution fusion | flops 1217396736 | bytes 8257536 | tf_op jit(solution)/shard_map/td,te->de/dot_general | solution.py:508
  147.5 70.2 %reduce.17 = (f32[16,6400]{1,0:T(8,128)}, f32[48,768]{1,0:T(8,128)}) custom-call(bf16[4,4,48,6400]{3,2,1,0:T(8,128)(2,1)} %bitcast.57, bf16[4,4,2,2,48,768]{5,4,3,2,1,0:T(8,128)(2,1)} %bitcast.58), custom_call_target="tpu_custom_call" | custom-call | tf_op jit(solution)/shard_map/reduce/pallas_call | solution.py:450
  217.8 1.5 slice_reduce_fusion
  219.3 1.5 fusion.58
  220.8 1.6 slice.81
  222.5 1.6 copy.114
  (107 shorter events, 1.7 us)
Async XLA Ops:
  0.6 71.7 %copy-start.1 = (bf16[256,768]{1,0:T(8,128)(2,1)S(1)}, bf16[256,768]{1,0:T(8,128)(2,1)}, u32[]{:S(2)}) copy-start(bf16[256,768]{1,0:T(8,128)(2,1)} %param.13) | copy-start | bytes 1179652
  72.3 4.6 %copy-start.24 = (f32[768]{0:T(1024)}, f32[768]{0:T(1024)S(1)}, u32[]{:S(2)}) copy-start(f32[768]{0:T(1024)S(1)} %get-tuple-element.49) | copy-start | bytes 9220
  72.7 4.0 %copy-start.16 = (f32[256]{0:T(256)}, f32[256]{0:T(256)S(1)}, u32[]{:S(2)}) copy-start(f32[256]{0:T(256)S(1)} %fusion.43) | copy-start | bytes 3076
  72.8 4.2 %copy-start.14 = (f32[256]{0:T(256)}, f32[256]{0:T(256)S(1)}, u32[]{:S(2)}) copy-start(f32[256]{0:T(256)S(1)} %fusion.47) | copy-start | bytes 3076
  74.8 6.6 %copy-start.5 = (bf16[256,768]{0,1:T(8,128)(2,1)}, bf16[256,768]{0,1:T(8,128)(2,1)S(1)}, u32[]{:S(2)}) copy-start(bf16[256,768]{0,1:T(8,128)(2,1)S(1)} %copy.75) | copy-start | bytes 1179652
  76.8 2.2 copy-start.26
  79.0 5.2 %copy-start.2 = (bf16[256,768]{0,1:T(8,128)(2,1)}, bf16[256,768]{0,1:T(8,128)(2,1)S(1)}, u32[]{:S(2)}) copy-start(bf16[256,768]{0,1:T(8,128)(2,1)S(1)} %copy.77) | copy-start | bytes 1179652
  80.3 2.7 %copy-start = (f32[24,256,256]{1,2,0:T(8,128)}, f32[24,256,256]{1,2,0:T(8,128)S(1)}, u32[]{:S(2)}) copy-start(f32[24,256,256]{1,2,0:T(8,128)S(1)} %get-tuple-element.41) | copy-start | bytes 18874372
  84.2 6.6 %copy-start.13 = (bf16[24,32,256]{2,1,0:T(8,128)(2,1)}, bf16[24,32,256]{2,1,0:T(8,128)(2,1)S(1)}, u32[]{:S(2)}) copy-start(bf16[24,32,256]{2,1,0:T(8,128)(2,1)S(1)} %fusion.24) | copy-start | bytes 1179652
  86.2 12.6 %copy-start.3 = (f32[256,768]{1,0:T(8,128)}, f32[256,768]{1,0:T(8,128)S(1)}, u32[]{:S(2)}) copy-start(f32[256,768]{1,0:T(8,128)S(1)} %get-tuple-element.43) | copy-start | bytes 2359300
  86.5 4.3 %copy-start.22 = (f32[768]{0:T(1024)}, f32[768]{0:T(1024)S(1)}, u32[]{:S(2)}) copy-start(f32[768]{0:T(1024)S(1)} %get-tuple-element.51) | copy-start | bytes 9220
  86.5 4.2 %slice-start.5 = ((s8[4718592]{0:T(1024)(128)(4,1)}), s8[4194304]{0:T(1024)(128)(4,1)S(1)}, s32[]{:S(2)}) async-start(s8[4718592]{0:T(1024)(128)(4,1)} %bitcast.89), calls=%async_computation.5 | async-start | bytes 8388608
  86.8 12.0 %copy-start.20 = (f32[256]{0:T(256)}, f32[256]{0:T(256)S(1)}, u32[]{:S(2)}) copy-start(f32[256]{0:T(256)S(1)} %fusion.48) | copy-start | bytes 3076
  86.8 4.0 %slice-start.6 = ((s8[4718592]{0:T(1024)(128)(4,1)}), s8[524288]{0:T(1024)(128)(4,1)S(1)}, s32[]{:S(2)}) async-start(s8[4718592]{0:T(1024)(128)(4,1)} %bitcast.89), calls=%async_computation.6 | async-start | bytes 1048576
  90.8 2.7 %copy-start.29 = (f32[256,3072]{1,0:T(8,128)}, f32[256,3072]{1,0:T(8,128)S(1)}, u32[]{:S(2)}) copy-start(f32[256,3072]{1,0:T(8,128)S(1)} %fusion.5) | copy-start | bytes 9437188
  90.8 2.7 %copy-start.6 = (bf16[256,768]{1,0:T(8,128)(2,1)S(1)}, bf16[256,768]{1,0:T(8,128)(2,1)}, u32[]{:S(2)}) copy-start(bf16[256,768]{1,0:T(8,128)(2,1)} %param.25) | copy-start | bytes 1179652
  90.8 5.9 %slice-start.2 = ((s8[9830400]{0:T(1024)(128)(4,1)}), s8[4194304]{0:T(1024)(128)(4,1)S(1)}, s32[]{:S(2)}) async-start(s8[9830400]{0:T(1024)(128)(4,1)} %bitcast.74), calls=%async_computation.2 | async-start | bytes 8388608
  93.5 3.1 %slice-start.3 = ((s8[9830400]{0:T(1024)(128)(4,1)}), s8[4194304]{0:T(1024)(128)(4,1)S(1)}, s32[]{:S(2)}) async-start(s8[9830400]{0:T(1024)(128)(4,1)} %bitcast.74), calls=%async_computation.3 | async-start | bytes 8388608
  93.5 3.1 %slice-start.4 = ((s8[9830400]{0:T(1024)(128)(4,1)}), s8[1441792]{0:T(1024)(128)(4,1)S(1)}, s32[]{:S(2)}) async-start(s8[9830400]{0:T(1024)(128)(4,1)} %bitcast.74), calls=%async_computation.4 | async-start | bytes 2883584
  96.7 2.1 copy-start.31
  99.2 1.6 copy-start.18
  99.4 0.7 copy-start.8
  100.8 4.6 %slice-start = ((s8[6291456]{0:T(1024)(128)(4,1)}), s8[4194304]{0:T(1024)(128)(4,1)S(1)}, s32[]{:S(2)}) async-start(s8[6291456]{0:T(1024)(128)(4,1)} %bitcast.55), calls=%async_computation | async-start | bytes 8388608
  100.8 4.8 %slice-start.1 = ((s8[6291456]{0:T(1024)(128)(4,1)}), s8[2097152]{0:T(1024)(128)(4,1)S(1)}, s32[]{:S(2)}) async-start(s8[6291456]{0:T(1024)(128)(4,1)} %bitcast.55), calls=%async_computation.1 | async-start | bytes 4194304
  111.9 3.0 %copy-start.9 = (bf16[24,32,256]{2,1,0:T(8,128)(2,1)}, bf16[24,32,256]{2,1,0:T(8,128)(2,1)S(1)}, u32[]{:S(2)}) copy-start(bf16[24,32,256]{2,1,0:T(8,128)(2,1)S(1)} %fusion.20) | copy-start | bytes 1179652
  114.9 4.0 %copy-start.11 = (bf16[24,32,256]{2,1,0:T(8,128)(2,1)}, bf16[24,32,256]{2,1,0:T(8,128)(2,1)S(1)}, u32[]{:S(2)}) copy-start(bf16[24,32,256]{2,1,0:T(8,128)(2,1)S(1)} %fusion.21) | copy-start | bytes 1179652
  114.9 2.2 copy-start.17
  114.9 2.2 copy-start.15
  114.9 2.7 %copy-start.7 = (bf16[256,768]{1,0:T(8,128)(2,1)S(1)}, bf16[256,768]{1,0:T(8,128)(2,1)}, u32[]{:S(2)}) copy-start(bf16[256,768]{1,0:T(8,128)(2,1)} %param.25) | copy-start | bytes 1179652
  114.9 2.7 %copy-start.19 = (f32[256]{0:T(256)S(1)}, f32[256]{0:T(256)}, u32[]{:S(2)}) copy-start(f32[256]{0:T(256)} %copy-done.18) | copy-start | bytes 3076
  114.9 3.9 %copy-start.25 = (f32[768]{0:T(1024)S(1)}, f32[768]{0:T(1024)}, u32[]{:S(2)}) copy-start(f32[768]{0:T(1024)} %copy-done.24) | copy-start | bytes 9220
  118.9 4.6 %copy-start.10 = (bf16[24,32,256]{2,1,0:T(8,128)(2,1)S(1)}, bf16[24,32,256]{2,1,0:T(8,128)(2,1)}, u32[]{:S(2)}) copy-start(bf16[24,32,256]{2,1,0:T(8,128)(2,1)} %copy-done.9) | copy-start | bytes 1179652
  123.5 4.4 %copy-start.12 = (bf16[24,32,256]{2,1,0:T(8,128)(2,1)S(1)}, bf16[24,32,256]{2,1,0:T(8,128)(2,1)}, u32[]{:S(2)}) copy-start(bf16[24,32,256]{2,1,0:T(8,128)(2,1)} %copy-done.11) | copy-start | bytes 1179652
  129.6 3.7 %copy-start.28 = (bf16[768]{0:T(1024)(128)(2,1)S(1)}, bf16[768]{0:T(1024)(128)(2,1)}, u32[]{:S(2)}) copy-start(bf16[768]{0:T(1024)(128)(2,1)} %get-tuple-element.24) | copy-start | bytes 4612
  129.6 3.7 %copy-start.27 = (bf16[768]{0:T(1024)(128)(2,1)S(1)}, bf16[768]{0:T(1024)(128)(2,1)}, u32[]{:S(2)}) copy-start(bf16[768]{0:T(1024)(128)(2,1)} %get-tuple-element.20) | copy-start | bytes 4612
  134.2 3.5 %copy-start.4 = (f32[256,768]{1,0:T(8,128)S(1)}, f32[256,768]{1,0:T(8,128)}, u32[]{:S(2)}) copy-start(f32[256,768]{1,0:T(8,128)} %copy-done.3) | copy-start | bytes 2359300
  134.2 3.5 %copy-start.21 = (f32[256]{0:T(256)S(1)}, f32[256]{0:T(256)}, u32[]{:S(2)}) copy-start(f32[256]{0:T(256)} %copy-done.20) | copy-start | bytes 3076
  134.2 3.5 %copy-start.23 = (f32[768]{0:T(1024)S(1)}, f32[768]{0:T(1024)}, u32[]{:S(2)}) copy-start(f32[768]{0:T(1024)} %copy-done.22) | copy-start | bytes 9220
  137.7 5.3 %copy-start.30 = (f32[256,3072]{1,0:T(8,128)S(1)}, f32[256,3072]{1,0:T(8,128)}, u32[]{:S(2)}) copy-start(f32[256,3072]{1,0:T(8,128)} %copy-done.29) | copy-start | bytes 9437188

commit v2 on v1

--- a/solution.py
+++ b/solution.py
@@ -20,7 +20,8 @@
 HALF = (1280, 1920)
 PART = ((640, 640), (896, 1024), (768, 768))
 LOW = ((256, 256), (384, 512), (384, 384))
-N_RECV = 240
+N_RECV = 340
+VMEM_BYTES = 63 << 20
 N_SEND = 48
 
 
@@ -182,6 +183,7 @@
 def join(stage, wide, me, g):
     width = 2 * HALF[g]
     step = 640
+
     def body(i, _):
         at = pl.ds(pl.multiple_of(START[g] + i * step, 128), step)
         rows = [stage[o, :, at].astype(F32)[:12] for o in range(4)]
@@ -190,14 +192,13 @@
     lax.fori_loop(0, width // step, body, 0)
 
 
-def gather_stage0(wire, own, own_down, stage, wide, down, g):
+def gather_stage0(wire, own_down, stage, wide, down, g):
     me = wire.place
     mine = 2 * me.zl + me.c
     if g < 2:
         at = pl.ds(START[g], 2 * HALF[g])
-        src, dst = own.at[:, at], lambda o: stage.at[o, :, at]
+        src, dst = stage.at[mine, :, at], lambda o: stage.at[o, :, at]
         hers = stage.at[2 * (1 - me.zl) + me.c, :, at]
-        stage[mine, :, at] = own[:, at]
     else:
         src, dst = own_down, lambda o: down.at[me.x, me.y, me.zl, me.c]
         hers = down.at[me.x, me.y, 1 - me.zl, me.c]
@@ -389,243 +390,405 @@
     return tail
 
 
-def gather_kernel(own, own_down, wide, down, stage, send, recv):
-    place = Place()
+def dot(a, b):
+    return lax.dot_general(a, b, (((1,), (0,)), ((), ())), preferred_element_type=F32)
+
+
+def dot_nt(a, b):
+    return lax.dot_general(a, b, (((1,), (1,)), ((), ())), preferred_element_type=F32)
+
+
+def loop(n, body):
+    def step(i, carry):
+        body(i)
+        return carry
+
+    lax.fori_loop(0, n, step, 0)
+
+
+def ds(i, n):
+    return pl.ds(pl.multiple_of(i * n, n), n)
+
+
+T = 256
+SCALE = HEAD_DIM ** (-0.5)
+O_AT, UP_AT, N1_AT, N2_AT = 2560, 3328, 2304, 2432
+ROW = 64
+
+
+def standardise(v):
+    centre = jnp.mean(v, axis=-1, keepdims=True)
+    centred = v - centre
+    spread = jnp.mean(centred * centred, axis=-1, keepdims=True)
+    rstd = lax.rsqrt(spread + 1e-05)
+    return centred * rstd, rstd
+
+
+def weight(wide, at, width):
+    return wide[:, :, :, pl.ds(at, width)].reshape(D, width)
+
+
+def layer_kernel(
+    x_ref, seg_ref, n1g_ref, n1b_ref, wq_ref, wk_ref, wv_ref, wo_ref, n2g_ref, n2b_ref, wu_ref, wd_ref, cot_ref,
+    out_ref, ig_ref, dn1g_ref, dn1b_ref, dq_ref, dk_ref, dv_ref, do_ref, dn2g_ref, dn2b_ref, du_ref, dd_ref,
+    *scratch,
+):
+    nb, nt = len(reduce_shapes()), len(tail_shapes())
+    bufs, scratch = scratch[:nb], scratch[nb:]
+    tbufs, scratch = scratch[:nt], scratch[nt:]
+    (
+        wide, down, gwide, gdown, stage, final, final_down,
+        mask, xhat, rstd1, xhat2, rstd2, n1, n1t, n2, qkv, mixed, probs, hidden,
+        act, slope, acc_out, acc_in, dqkv, rows1, rows2, send, recv,
+    ) = scratch
+    place = me = Place()
     greet(place)
     wire = Wire(place, send, recv)
-    front = [gather_stage0(wire, own, own_down, stage, wide, down, g) for g in range(3)]
-    run(*front)
-    run(*[gather_stream(wire, wide, down, g, p) for g in range(3) for p in range(2)])
+    mine = 2 * me.zl + me.c
+
+    zero4 = lambda n: jnp.zeros((4, n), F32)
+
+    def put_own(ref, at):
+        n = ref.shape[1]
+        rows = jnp.concatenate([ref[...].astype(F32), zero4(n)], axis=0)
+        stage[mine, :, pl.ds(at, n)] = rows.astype(BF)
+
+    def put_norm(gain, shift, at):
+        eye = lax.broadcasted_iota(jnp.int32, (16, 12), 0) == lax.broadcasted_iota(jnp.int32, (16, 12), 1)
+        lane = lax.broadcasted_iota(jnp.int32, (16, 128), 1)
+        a = jnp.sum(jnp.where(eye, gain[...].astype(F32), 0.0), axis=1, keepdims=True)
+        b = jnp.sum(jnp.where(eye, shift[...].astype(F32), 0.0), axis=1, keepdims=True)
+        both = jnp.where(lane == 0, a, jnp.where(lane == 1, b, 0.0))
+        stage[mine, :, pl.ds(at, 128)] = both.astype(BF)
+
+    for i, ref in enumerate((wq_ref, wk_ref, wv_ref)):
+        put_own(ref, 768 * i)
+    put_norm(n1g_ref, n1b_ref, N1_AT)
+    put_norm(n2g_ref, n2b_ref, N2_AT)
+    front = [gather_stage0(wire, wd_ref, stage, wide, down, g) for g in range(3)]
+    next(front[0])
+    put_own(wo_ref, O_AT)
+    put_own(wu_ref, UP_AT)
+    next(front[1])
+    next(front[2])
+
+    segs = jnp.broadcast_to(seg_ref[...], (T, T))
+    rows_iota = lax.broadcasted_iota(jnp.int32, (T, T), 0)
+    cols_iota = lax.broadcasted_iota(jnp.int32, (T, T), 1)
+    allowed = (rows_iota >= cols_iota) & (segs.astype(F32).T == segs.astype(F32))
+    mask[...] = jnp.where(allowed, 0.0, -1e30)
+
+    next(front[0])
+
+    def norm1_rows(i):
+        at = ds(i, ROW)
+        hat, rstd = standardise(x_ref[at, :].astype(F32))
+        xhat[at, :] = hat
+        rstd1[at, :] = rstd
+
+    loop(T // ROW, norm1_rows)
+    next(front[0])
+
+    def gather(g):
+        return [gather_stream(wire, wide, down, g, p) for p in range(2)]
+
+    def step(streams):
+        return [s for s in streams if next(s, StopIteration) is not StopIteration]
+
+    g0 = step(gather(0))
+    next(front[1])
+    next(front[2])
+    g0 = step(g0)
+    next(front[1])
+    g1 = step(gather(1))
+    g0 = step(g0)
+    next(front[2])
+    g2 = step(gather(2))
+    while g0:
+        g0 = step(g0)
+        g1 = step(g1)
+        g2 = step(g2)
+
+    eye = (
+        lax.broadcasted_iota(jnp.int32, (128, 128), 0) == lax.broadcasted_iota(jnp.int32, (128, 128), 1)
+    ).astype(BF)
+    rows1[...] = dot_nt(eye, weight(wide, N1_AT, 128))[:8]
+    rows2[...] = dot_nt(eye, weight(wide, N2_AT, 128))[:8]
+
+    def norm1_apply(i):
+        at = ds(i, ROW)
+        n1[at, :] = (xhat[at, :] * rows1[0:1, :] + rows1[1:2, :]).astype(BF)
+
+    loop(T // ROW, norm1_apply)
+
+    def project(i):
+        at = ds(i, 256)
+        w = wide[:, :, :, at].reshape(D, 256)
+        qkv[:, at] = dot(n1[...], w).astype(BF)
+
+    loop(9, project)
+    g1 = step(g1)
+    g2 = step(g2)
+    lane = lax.broadcasted_iota(jnp.int32, (1, 128), 1)
+    heads = [((lane >= 32 * h) & (lane < 32 * h + 32)).astype(F32).astype(BF) for h in range(4)]
+
+    def group(ref, which, t):
+        return ref[:, pl.ds(pl.multiple_of(768 * which + 128 * t, 128), 128)]
+
+    def attend(t):
+        q4, k4, v4 = [group(qkv, i, t) for i in range(3)]
+        vh = [v4 * heads[h] for h in range(4)]
+        for rb in range(2):
+            rows, nk = slice(128 * rb, 128 * rb + 128), 128 * rb + 128
+            total = jnp.zeros((128, 128), F32)
+            for h in range(4):
+                s = dot_nt(q4[rows] * heads[h], k4[:nk]) * SCALE + mask[rows, :nk]
+                e = jnp.exp(s - jnp.max(s, axis=1, keepdims=True))
+                p = (e * (1.0 / jnp.sum(e, axis=1, keepdims=True))).astype(BF)
+                probs[4 * t + h, rows, :nk] = p
+                total = total + dot(p, vh[h][:nk])
+            mixed[rows, pl.ds(pl.multiple_of(128 * t, 128), 128)] = total.astype(BF)
+
+    for part in range(3):
+        loop(2, lambda i: attend(2 * part + i))
+        g1 = step(g1)
+        g2 = step(g2)
+
+    n2t, mixt = [gwide.at[:, :, :, pl.ds(256 * k, 256)] for k in range(2)]
+
+    def transpose(src, dst):
+        def body(i):
+            dst[ds(i, 2)] = src[:, ds(i, 384)].T.reshape(2, 4, 48, T)
+
+        loop(2, body)
+
+    def turn_n1(i):
+        n1t[ds(i, 384), :] = n1[:, ds(i, 384)].T
+
+    transpose(mixed, mixt)
+    loop(2, turn_n1)
+    while g1:
+        g1 = step(g1)
+        g2 = step(g2)
+
+    def out_project(i):
+        at = ds(i, 256)
+        w = wide[:, :, :, pl.ds(pl.multiple_of(O_AT + 256 * i, 128), 256)].reshape(D, 256)
+        hidden[:, at] = x_ref[:, at].astype(F32) + dot(mixed[...], w)
+
+    loop(3, out_project)
+
+    def norm2_rows(i):
+        at = ds(i, ROW)
+        hat, rstd = standardise(hidden[at, :])
+        xhat2[at, :] = hat
+        rstd2[at, :] = rstd
+        n2[at, :] = (hat * rows2[0:1, :] + rows2[1:2, :]).astype(BF)
+
+    loop(T // ROW, norm2_rows)
+    transpose(n2, n2t)
+
+    c0 = (2.0 / 3.141592653589793) ** 0.5
+
+    def feed(i):
+        def part(j):
+            at = pl.ds(pl.multiple_of(UP_AT + 768 * i + 256 * j, 128), 256)
+            v = dot(n2[...], wide[:, :, :, at].reshape(D, 256))
+            sq = v * v
+            th = jnp.tanh(c0 * v * (1.0 + 0.044715 * sq))
+            half = 0.5 + 0.5 * th
+            a = (v * half).astype(BF)
+            keep = pl.ds(pl.multiple_of(768 * i + 256 * j, 128), 256)
+            act[:, keep] = a
+            slope[:, keep] = half + 0.5 * v * (1.0 - th * th) * (c0 * (1.0 + 0.134145 * sq))
+
+        loop(3, part)
+        a = act[:, ds(i, 768)].T
+
+        def grad(j):
+            at = ds(j, 256)
+            gdown[i, :, :, :, :, at] = dot(a, cot_ref[:, at]).astype(BF).reshape(4, 2, 2, 48, 256)
+
+        loop(3, grad)
+
+    loop(4, feed)
+    reduced = make_tail(tbufs, final, final_down)
+
+    def reduce(g):
+        return [
+            reduce_stream(wire, gwide, gdown, bufs[9 * (2 * g + p) : 9 * (2 * g + p) + 9], reduced, g, p)
+            for p in range(2)
+        ]
+
+    r2 = step(reduce(2))
+    while g2:
+        g2 = step(g2)
+    r2 = step(r2)
+
+    acc_out[...] = hidden[...]
+    acc_in[...] = jnp.zeros((T, D), F32)
+
+    def feed_back(i):
+        at = ds(i, 768)
+        wd = down[i].reshape(768, 768)
+        acc_out[...] += dot(act[:, at], wd)
+        pg = (dot_nt(cot_ref[...], wd) * slope[:, at]).astype(BF)
+        act[:, at] = pg
+        up_at = pl.ds(pl.multiple_of(UP_AT + 768 * i, 128), 768)
+        acc_in[...] += dot_nt(pg, wide[:, :, :, up_at].reshape(D, 768))
+
+        def grad(j):
+            cols_j = pl.ds(pl.multiple_of(UP_AT + 768 * i + 256 * j, 128), 256)
+            pg_j = act[:, pl.ds(pl.multiple_of(768 * i + 256 * j, 128), 256)]
+            gwide[:, :, :, cols_j] = dot(n2t[...].reshape(D, T), pg_j).astype(BF).reshape(4, 4, 48, 256)
+
+        loop(3, grad)
+
+    for part in range(2):
+        loop(2, lambda i: feed_back(2 * part + i))
+        r2 = step(r2)
+    out_ref[...] = acc_out[...].astype(BF)
+
+    def norm_back(grad, hat, rstd, gain, at):
+        gn = gain * grad
+        m1 = jnp.mean(gn, axis=-1, keepdims=True)
+        m2 = jnp.mean(gn * hat, axis=-1, keepdims=True)
+        return (gn - m1 - hat * m2) * rstd
+
+    def norm2_back(i, sums):
+        at = ds(i, ROW)
+        grad, hat = acc_in[at, :], xhat2[at, :]
+        extra = norm_back(grad, hat, rstd2[at, :], rows2[0:1, :], at)
+        hidden[at, :] = cot_ref[at, :].astype(F32) + extra
+        a, b = sums
+        return a + jnp.sum(grad * hat, axis=0, keepdims=True), b + jnp.sum(grad, axis=0, keepdims=True)
+
+    def as_columns(sums, at):
+        rows = jnp.concatenate([*sums, jnp.zeros((126, D), F32)], axis=0)
+        gwide[:, :, :, pl.ds(at, 128)] = rows.T.astype(BF).reshape(4, 4, 48, 128)
+
+    nothing = jnp.zeros((1, D), F32)
+    as_columns(lax.fori_loop(0, T // ROW, norm2_back, (nothing, nothing)), N2_AT)
+    n2[...] = hidden[...].astype(BF)
+
+    def o_back(i):
+        at = ds(i, 256)
+        b = n2[:, at]
+        gwide[:, :, :, pl.ds(pl.multiple_of(O_AT + 256 * i, 128), 256)] = (
+            dot(mixt[...].reshape(D, T), b).astype(BF).reshape(4, 4, 48, 256)
+        )
+
+    loop(3, o_back)
+    r1 = step(reduce(1))
+    mgrad = n1
+    mgrad[...] = dot_nt(n2[...], weight(wide, O_AT, D)).astype(BF)
+    r2 = step(r2)
+    r1 = step(r1)
+
+    def attend_back(t):
+        q4, k4, v4 = [group(qkv, i, t) for i in range(3)]
+        do4, o4 = group(mgrad, 0, t), group(mixed, 0, t)
+        q4t, do4t = q4.T, do4.T
+        kh = [k4 * heads[h] for h in range(4)]
+        dk, dv = [], []
+        total = [jnp.zeros((128, 128), F32)] * 2
+        for h in range(4):
+            hrows = slice(32 * h, 32 * h + 32)
+            dkh, dvh = [], []
+            for rb in range(2):
+                rows, nk = slice(128 * rb, 128 * rb + 128), 128 * rb + 128
+                dob = do4[rows] * heads[h]
+                dot_row = jnp.sum(dob.astype(F32) * o4[rows].astype(F32), axis=1, keepdims=True)
+                p = probs[4 * t + h, rows, :nk]
+                sg = (p.astype(F32) * (dot_nt(dob, v4[:nk]) - dot_row)).astype(BF)
+                total[rb] = total[rb] + dot(sg, kh[h][:nk])
+                dkh.append(dot(q4t[hrows, rows], sg))
+                dvh.append(dot(do4t[hrows, rows], p))
+            for both, parts in ((dk, dkh), (dv, dvh)):
+                both.append(jnp.concatenate([parts[1][:, :128] + parts[0], parts[1][:, 128:]], axis=1))
+        at = pl.multiple_of(128 * t, 128)
+        for rb in range(2):
+            dqkv[pl.ds(128 * rb, 128), pl.ds(at, 128)] = (total[rb] * SCALE).astype(BF)
+        dqkv[:, pl.ds(at + 768, 128)] = (jnp.concatenate(dk, axis=0).T * SCALE).astype(BF)
+        dqkv[:, pl.ds(at + 1536, 128)] = jnp.concatenate(dv, axis=0).T.astype(BF)
+
+    for part in range(3):
+        loop(2, lambda i: attend_back(2 * part + i))
+        r2 = step(r2)
+        r1 = step(r1)
+
+    acc_in[...] = dot_nt(dqkv[:, :768], weight(wide, 0, D))
+    acc_in[...] += dot_nt(dqkv[:, 768:1536], weight(wide, 768, D))
+    acc_in[...] += dot_nt(dqkv[:, 1536:], weight(wide, 1536, D))
+
+    def norm1_back(i, sums):
+        at = ds(i, ROW)
+        grad, hat = acc_in[at, :], xhat[at, :]
+        extra = norm_back(grad, hat, rstd1[at, :], rows1[0:1, :], at)
+        ig_ref[at, :] = hidden[at, :] + extra
+        a, b = sums
+        return a + jnp.sum(grad * hat, axis=0, keepdims=True), b + jnp.sum(grad, axis=0, keepdims=True)
+
+    as_columns(lax.fori_loop(0, T // ROW, norm1_back, (nothing, nothing)), N1_AT)
+    r2 = step(r2)
+    r1 = step(r1)
+
+    def qkv_grad(i):
+        at = ds(i, 256)
+        gwide[:, :, :, at] = dot(n1t[...], dqkv[:, at]).astype(BF).reshape(4, 4, 48, 256)
+
+    loop(9, qkv_grad)
+    r0 = step(reduce(0))
+    while r0 or r1 or r2:
+        r2, r1, r0 = step(r2), step(r1), step(r0)
     wire.drain()
 
-
-def reduce_kernel(g_wide, g_down, final, final_down, wide, down, sems, *rest):
-    nb = len(reduce_shapes())
-    bufs, tbufs, (send, recv) = rest[:nb], rest[nb:-2], rest[-2:]
-    place = Place()
-    greet(place)
-    a = pltpu.make_async_copy(g_wide, wide, sems.at[0])
-    b = pltpu.make_async_copy(g_down, down, sems.at[1])
-    a.start()
-    b.start()
-    a.wait()
-    b.wait()
-    wire = Wire(place, send, recv)
-    tail = make_tail(tbufs, final, final_down)
-    streams = []
-    for g in (2, 1, 0):
-        for p in range(2):
-            k = 9 * (2 * g + p)
-            streams.append(reduce_stream(wire, wide, down, bufs[k : k + 9], tail, g, p))
-    run(*streams)
-    wire.drain()
-
-
-ANY = pl.BlockSpec(memory_space=pl.ANY)
+    dd_ref[...] = final_down[...]
+    for i, ref in enumerate((dq_ref, dk_ref, dv_ref)):
+        ref[...] = final[:12, 768 * i : 768 * i + 768]
+    do_ref[...] = final[:12, O_AT:UP_AT]
+    du_ref[...] = final[:12, UP_AT:]
+    diag = lax.broadcasted_iota(jnp.int32, (16, 128), 0) == lax.broadcasted_iota(jnp.int32, (16, 128), 1)
+    for at, refs in ((N1_AT, (dn1g_ref, dn1b_ref)), (N2_AT, (dn2g_ref, dn2b_ref))):
+        for k, ref in enumerate(refs):
+            col = final[:, at + k : at + k + 1]
+            ref[...] = jnp.sum(jnp.where(diag, col, 0.0), axis=0, keepdims=True)[:, :12]
+
+
 VM = pl.BlockSpec(memory_space=pltpu.VMEM)
 
 
-def gather_call(own, own_down):
-    return pl.pallas_call(
-        gather_kernel,
+def per_device(*args):
+    args = [a.reshape(1, 12) if a.ndim == 1 else a for a in args]
+    like = jax.ShapeDtypeStruct
+    vec, square = like((1, 12), F32), like((12, D), F32)
+    scratch = [pltpu.VMEM(s, t) for s, t in reduce_shapes() + tail_shapes()]
+    wide, down = pltpu.VMEM((4, 4, 48, WIDE), BF), pltpu.VMEM((4, 4, 2, 2, 48, D), BF)
+    scratch += [wide, down, wide, down, pltpu.VMEM((4, 16, WIDE), BF), pltpu.VMEM((16, WIDE), F32), pltpu.VMEM((48, D), F32)]
+    f32s, bfs = pltpu.VMEM((T, D), F32), pltpu.VMEM((T, D), BF)
+    one, turned = pltpu.VMEM((T, 1), F32), pltpu.VMEM((D, T), BF)
+    scratch += [pltpu.VMEM((T, T), F32), f32s, one, f32s, one]
+    scratch += [bfs, turned, bfs, pltpu.VMEM((T, 3 * D), BF), bfs]
+    scratch += [pltpu.VMEM((HEADS, T, T), BF), f32s]
+    scratch += [pltpu.VMEM((T, FF), BF), pltpu.VMEM((T, FF), F32), f32s, f32s]
+    scratch += [pltpu.VMEM((T, 3 * D), BF), pltpu.VMEM((8, D), F32), pltpu.VMEM((8, D), F32)]
+    scratch += [pltpu.SemaphoreType.DMA((N_SEND,)), pltpu.SemaphoreType.DMA((N_RECV,))]
+    outs = pl.pallas_call(
+        layer_kernel,
         out_shape=(
-            jax.ShapeDtypeStruct((4, 4, 48, WIDE), BF),
-            jax.ShapeDtypeStruct((4, 4, 2, 2, 48, 768), BF),
+            like((T, D), BF), like((T, D), F32), vec, vec, square, square, square, square, vec, vec,
+            like((12, FF), F32), like((48, D), F32),
         ),
-        in_specs=[VM, VM],
-        out_specs=(VM, VM),
-        scratch_shapes=[
-            pltpu.VMEM((4, 16, WIDE), BF),
-            pltpu.SemaphoreType.DMA((N_SEND,)),
-            pltpu.SemaphoreType.DMA((N_RECV,)),
-        ],
+        in_specs=[VM] * 13,
+        out_specs=(VM,) * 12,
+        scratch_shapes=scratch,
         compiler_params=pltpu.CompilerParams(
-            collective_id=0, has_side_effects=True, vmem_limit_bytes=56 << 20
+            collective_id=0, has_side_effects=True, vmem_limit_bytes=VMEM_BYTES
         ),
-        name="gather",
-    )(own, own_down)
-
-
-def reduce_call(g_wide, g_down):
-    return pl.pallas_call(
-        reduce_kernel,
-        out_shape=(
-            jax.ShapeDtypeStruct((16, WIDE), F32),
-            jax.ShapeDtypeStruct((48, 768), F32),
-        ),
-        in_specs=[ANY, ANY],
-        out_specs=(VM, VM),
-        scratch_shapes=[
-            pltpu.VMEM((4, 4, 48, WIDE), BF),
-            pltpu.VMEM((4, 4, 2, 2, 48, 768), BF),
-            pltpu.SemaphoreType.DMA((2,)),
-            *[pltpu.VMEM(s, t) for s, t in reduce_shapes()],
-            *[pltpu.VMEM(s, t) for s, t in tail_shapes()],
-            pltpu.SemaphoreType.DMA((N_SEND,)),
-            pltpu.SemaphoreType.DMA((N_RECV,)),
-        ],
-        compiler_params=pltpu.CompilerParams(
-            collective_id=1, has_side_effects=True, vmem_limit_bytes=56 << 20
-        ),
-        name="reduce",
-    )(g_wide, g_down)
-
-
-def pack_own(n1g, n1b, wq, wk, wv, wo, n2g, n2b, wu):
-    def pad(*vs):
-        return jnp.pad(jnp.stack(vs, axis=1), ((0, 0), (0, 128 - len(vs))))
-
-    own = jnp.concatenate([wq, wk, wv, pad(n1g, n1b), pad(n2g, n2b), wo, wu], axis=1)
-    return jnp.pad(own, ((0, 4), (0, 0)))
-
-
-def layer_norm(values, gain, shift):
-    centre = jnp.mean(values, axis=-1, keepdims=True)
-    centred = values - centre
-    spread = jnp.mean(centred * centred, axis=-1, keepdims=True)
-    return centred * lax.rsqrt(spread + 1e-05) * gain + shift
-
-
-def masked_scores(query, key, segment_ids):
-    tokens = query.shape[0]
-    query_heads = query.reshape(tokens, HEADS, HEAD_DIM)
-    key_heads = key.reshape(tokens, HEADS, HEAD_DIM)
-    scaled = jnp.einsum(
-        "qhd,khd->hqk", query_heads, key_heads, preferred_element_type=jnp.float32
-    ) * HEAD_DIM ** (-0.5)
-    segments = segment_ids.reshape(tokens)
-    rows_iota = lax.broadcasted_iota(jnp.int32, (tokens, tokens), 0)
-    cols_iota = lax.broadcasted_iota(jnp.int32, (tokens, tokens), 1)
-    allowed = (rows_iota >= cols_iota) & (segments[:, None] == segments[None, :])
-    return jnp.where(allowed[None], scaled, -1e30)
-
-
-def matmul_back(left, right):
-    return jnp.einsum("te,de->td", left, right, preferred_element_type=jnp.float32)
-
-
-def matmul_outer(left, right):
-    return jnp.einsum("td,te->de", left, right, preferred_element_type=jnp.float32)
-
-
-def per_device(
-    block_input, segment_ids, norm1_gain, norm1_bias, query_weight, key_weight, value_weight, out_weight,
-    norm2_gain, norm2_bias, up_weight, down_weight, out_cotangent,
-):
-    tokens = block_input.shape[0]
-    inputs = block_input.astype(F32)
-    own = pack_own(
-        norm1_gain, norm1_bias, query_weight, key_weight, value_weight, out_weight, norm2_gain, norm2_bias, up_weight
-    )
-    wide, down = gather_call(own, down_weight)
-    wide = wide.reshape(D, WIDE)
-    down = down.reshape(FF, D)
-    wq, wk, wv = wide[:, :768], wide[:, 768:1536], wide[:, 1536:2304]
-    gain1, bias1 = wide[:, 2304].astype(F32), wide[:, 2305].astype(F32)
-    gain2, bias2 = wide[:, 2432].astype(F32), wide[:, 2433].astype(F32)
-    wo, wu = wide[:, 2560:3328], wide[:, 3328:]
-    normed1_f, norm1_pull = jax.vjp(layer_norm, inputs, gain1, bias1)
-    normed1 = normed1_f.astype(jnp.bfloat16)
-    query = jnp.dot(normed1, wq, preferred_element_type=jnp.float32).astype(jnp.bfloat16)
-    key = jnp.dot(normed1, wk, preferred_element_type=jnp.float32).astype(jnp.bfloat16)
-    value = jnp.dot(normed1, wv, preferred_element_type=jnp.float32).astype(jnp.bfloat16)
-    scores = masked_scores(query, key, segment_ids)
-    maximum = jnp.max(scores, axis=-1, keepdims=True)
-    exponent = jnp.exp(scores - maximum)
-    summed = jnp.sum(exponent, axis=-1, keepdims=True)
-    probs = exponent / summed
-    log_total = maximum + jnp.log(summed)
-    value_heads = value.reshape(tokens, HEADS, HEAD_DIM)
-    mixed = jnp.einsum(
-        "hqk,khd->qhd", probs.astype(jnp.bfloat16), value_heads, preferred_element_type=jnp.float32
-    )
-    mixed = mixed.reshape(tokens, HEADS * HEAD_DIM).astype(jnp.bfloat16)
-    hidden_state = inputs + jnp.dot(mixed, wo, preferred_element_type=jnp.float32)
-    normed2_f, norm2_pull = jax.vjp(layer_norm, hidden_state, gain2, bias2)
-    normed2 = normed2_f.astype(jnp.bfloat16)
-    pre_act = jnp.dot(normed2, wu, preferred_element_type=jnp.float32)
-    activated_f, gelu_pull = jax.vjp(jax.nn.gelu, pre_act)
-    activated = activated_f.astype(jnp.bfloat16)
-    output = (
-        hidden_state + jnp.dot(activated, down, preferred_element_type=jnp.float32)
-    ).astype(jnp.bfloat16)
-    down_term = matmul_outer(activated, out_cotangent)
-    act_grad = matmul_back(out_cotangent, down)
-    pre_grad = gelu_pull(act_grad)[0].astype(jnp.bfloat16)
-    up_term = matmul_outer(normed2, pre_grad)
-    normed2_grad = matmul_back(pre_grad, wu)
-    hidden_extra, gain2_term, bias2_term = norm2_pull(normed2_grad)
-    hidden_grad = out_cotangent.astype(jnp.float32) + hidden_extra
-    branch_grad = hidden_grad.astype(jnp.bfloat16)
-    outproj_term = matmul_outer(mixed, branch_grad)
-    mixed_grad = matmul_back(branch_grad, wo).astype(jnp.bfloat16)
-    mixed_heads = mixed_grad.reshape(tokens, HEADS, HEAD_DIM)
-    again_probs = jnp.exp(masked_scores(query, key, segment_ids) - log_total)
-    prob_grad = jnp.einsum(
-        "qhd,khd->hqk", mixed_heads, value_heads, preferred_element_type=jnp.float32
-    )
-    value_act = jnp.einsum(
-        "hqk,qhd->khd",
-        again_probs.astype(jnp.bfloat16),
-        mixed_heads,
-        preferred_element_type=jnp.float32,
-    )
-    value_act = value_act.reshape(tokens, HEADS * HEAD_DIM).astype(jnp.bfloat16)
-    row_dot = jnp.sum(prob_grad * again_probs, axis=-1, keepdims=True)
-    score_grad = (again_probs * (prob_grad - row_dot)).astype(jnp.bfloat16)
-    query_heads = query.reshape(tokens, HEADS, HEAD_DIM)
-    key_heads = key.reshape(tokens, HEADS, HEAD_DIM)
-    query_act = jnp.einsum(
-        "hqk,khd->qhd", score_grad, key_heads, preferred_element_type=jnp.float32
-    ) * HEAD_DIM ** (-0.5)
-    key_act = jnp.einsum(
-        "hqk,qhd->khd", score_grad, query_heads, preferred_element_type=jnp.float32
-    ) * HEAD_DIM ** (-0.5)
-    query_act = query_act.reshape(tokens, HEADS * HEAD_DIM).astype(jnp.bfloat16)
-    key_act = key_act.reshape(tokens, HEADS * HEAD_DIM).astype(jnp.bfloat16)
-    query_term = matmul_outer(normed1, query_act)
-    key_term = matmul_outer(normed1, key_act)
-    value_term = matmul_outer(normed1, value_act)
-    normed1_grad = (
-        matmul_back(query_act, wq)
-        + matmul_back(key_act, wk)
-        + matmul_back(value_act, wv)
-    )
-    input_extra, gain1_term, bias1_term = norm1_pull(normed1_grad)
-    input_grad = hidden_grad + input_extra
-
-    def columns(*vs):
-        return jnp.pad(jnp.stack(vs, axis=1), ((0, 0), (0, 128 - len(vs)))).astype(BF)
-
-    g_wide = jnp.concatenate(
-        [
-            query_term.astype(BF),
-            key_term.astype(BF),
-            value_term.astype(BF),
-            columns(gain1_term, bias1_term),
-            columns(gain2_term, bias2_term),
-            outproj_term.astype(BF),
-            up_term.astype(BF),
-        ],
-        axis=1,
-    ).reshape(4, 4, 48, WIDE)
-    g_down = down_term.astype(BF).reshape(4, 4, 2, 2, 48, 768)
-    total, down_total = reduce_call(g_wide, g_down)
-    total = total[:12]
-    return (
-        output,
-        input_grad,
-        total[:, 2304],
-        total[:, 2305],
-        total[:, :768],
-        total[:, 768:1536],
-        total[:, 1536:2304],
-        total[:, 2560:3328],
-        total[:, 2432],
-        total[:, 2433],
-        total[:, 3328:],
-        down_total,
-    )
+        cost_estimate=pl.CostEstimate(flops=13 * 10**9, bytes_accessed=6 * 10**6, transcendentals=3 * 10**6),
+        name="layer",
+    )(*args)
+    return tuple(o.reshape(12) if o.shape == (1, 12) else o for o in outs)
 
 
 def solution(mesh):

time: 225 us -> 168 us (0.75)
  matrix products: 52.9 us -> 0 us
  Pallas kernels: 134 us -> 157 us
  local copies, waits for them, and re-layouts: 28.4 us -> 9.36 us
  other arithmetic: 7.38 us -> 0 us
    dot_general x24 -> x0, matrix products: 52.9 us -> none  [the longest x6 16.5 us: matmul_outer(): jnp.einsum('td,te->de', left, right, preferred_element_type=jnp.float32)]
    pallas_call x2 -> x1, Pallas kernels: 134 us -> 157 us  [per_device(): pl.pallas_call(layer_kernel, out_shape=(like((T, D), BF), like((T, D), F3...]
    convert_element_type x8 -> x0, local copies, waits for them, and re-layouts: 6.27 us -> none  [the longest x1 1.79 us: per_device(): query_term.astype(BF)]
    slice x4 -> x0, local copies, waits for them, and re-layouts: 6.1 us -> none  [the longest x1 1.62 us: per_device(): total[:, 3328:]]
    unnamed x95 -> x34, local copies, waits for them, and re-layouts: 13.9 us -> 9.36 us
    reduce_sum x6 -> x0, other arithmetic: 2.47 us -> none  [the longest x1 1.06 us: per_device(): summed = jnp.sum(exponent, axis=-1, keepdims=True)]
where the time goes in v2:
time: 168 us; the launch traced here: 167 us
  Pallas kernels  157 us (93%)
  local copies, waits for them, and re-layouts  9.36 us (6%)
    pallas_call x1, Pallas kernels, per_device(): pl.pallas_call(layer_kernel, out_shape=(like((T, D), BF), like((T, D), F3...  157 us
    unnamed x34, local copies, waits for them, and re-layouts  9.36 us

profile of v2, /device:TPU:1, one launch (start us, length us, event | category | flops | bytes accessed | tf_op | source)
XLA Modules:
  0.0 167.5 jit_solution(16820250782773197134)
XLA Ops:
  0.6 157.4 %layer.1 = (bf16[256,768]{1,0:T(8,128)(2,1)}, f32[256,768]{1,0:T(8,128)}, f32[1,12]{1,0:T(1,128)}, f32[1,12]{1,0:T(1,128)}, f32[12,768]{1,0:T(8,128)}, /*index=5...) custom-call(bf16[256,768]{1,0:T(8,128)(2,1)} %x_ref.1, ...), custom_call_target="tpu_custom_call" | custom-call | flops 12999999488 | bytes 6000000 | tf_op jit(solution)/shard_map/layer/pallas_call | solution.py:776
  158.1 0.0 copy-start
  158.1 1.8 %copy.37 = bf16[256,768]{1,0:T(8,128)(2,1)} copy(bf16[256,768]{1,0:T(8,128)(2,1)} %get-tuple-element.48) | data formatting | bytes 786432
  159.9 0.0 copy-done
  159.9 0.0 copy-start.10
  159.9 0.0 copy-start.6
  159.9 0.0 copy-start.5
  159.9 0.0 copy-start.4
  160.0 0.9 copy.38
  160.8 0.0 copy-done.10
  160.8 0.0 copy-start.9
  160.8 0.5 copy.39
  161.4 0.1 copy-done.9
  161.4 0.5 copy.40
  162.0 0.0 copy-done.6
  162.0 0.0 copy-start.1
  162.0 0.6 copy.41
  162.6 0.0 copy-done.5
  162.6 0.6 copy.42
  163.2 0.0 copy-done.4
  163.2 0.0 copy-start.3
  163.2 0.6 copy.43
  163.8 0.2 copy-done.3
  164.0 0.0 copy-start.8
  164.0 0.6 copy.44
  164.6 0.0 copy-done.8
  164.7 0.0 copy-start.7
  164.7 0.5 copy.45
  165.2 0.1 copy-done.7
  165.3 0.5 copy.46
  165.8 0.0 copy-done.1
  165.8 0.0 copy-start.2
  165.8 0.7 copy.47
  166.5 0.3 copy-done.2
  166.8 0.7 copy.48
Async XLA Ops:
  158.1 1.9 %copy-start = (f32[256,768]{1,0:T(8,128)S(1)}, f32[256,768]{1,0:T(8,128)}, u32[]{:S(2)}) copy-start(f32[256,768]{1,0:T(8,128)} %get-tuple-element.49) | copy-start | bytes 2359300
  159.9 0.9 copy-start.10
  159.9 2.0 %copy-start.6 = (f32[12,768]{1,0:T(8,128)S(1)}, f32[12,768]{1,0:T(8,128)}, u32[]{:S(2)}) copy-start(f32[12,768]{1,0:T(8,128)} %get-tuple-element.52) | copy-start | bytes 110596
  159.9 2.6 %copy-start.5 = (f32[12,768]{1,0:T(8,128)S(1)}, f32[12,768]{1,0:T(8,128)}, u32[]{:S(2)}) copy-start(f32[12,768]{1,0:T(8,128)} %get-tuple-element.53) | copy-start | bytes 110596
  159.9 3.3 %copy-start.4 = (f32[12,768]{1,0:T(8,128)S(1)}, f32[12,768]{1,0:T(8,128)}, u32[]{:S(2)}) copy-start(f32[12,768]{1,0:T(8,128)} %get-tuple-element.54) | copy-start | bytes 110596
  160.8 0.6 copy-start.9
  162.0 3.9 %copy-start.1 = (f32[12,3072]{1,0:T(8,128)S(1)}, f32[12,3072]{1,0:T(8,128)}, u32[]{:S(2)}) copy-start(f32[12,3072]{1,0:T(8,128)} %get-tuple-element.58) | copy-start | bytes 442372
  163.2 0.8 copy-start.3
  164.0 0.7 copy-start.8
  164.7 0.6 copy-start.7
  165.8 1.0 copy-start.2

commit v3 on v2

v3 whole, which is shorter than its diff:
```python
import functools

import jax
import jax.numpy as jnp
from jax import lax
from jax.experimental import pallas as pl
from jax.experimental.pallas import tpu as pltpu
from jax.sharding import PartitionSpec as P

HEADS = 24
HEAD_DIM = 32
D = 768
FF = 3072
BF = jnp.bfloat16
F32 = jnp.float32
MESH = pl.DeviceIdType.MESH

WIDE = 6400
DOWN = 2
START = (0, 2560, 0, 0, 1536)
HALF = (1280, 1920, 0, 768, 512)
SIZE = ((512, 384), (896, 512), (384, 384), (384, 384), (256, 256))
LOW = ((256, 128), (384, 256), (128, 256), (128, 256), (128, 128))
ZED = (True, True, False, False, False)
P_, QM, QO = 0, 1, 2
N_RECV = 305
N_SEND = 40
VMEM_BYTES = 66700000


class Place:
    def __init__(self):
        f = lax.axis_index("fsdp")
        r = lax.axis_index("rep")
        c = lax.rem(f, 2)
        zl = lax.rem(lax.div(f, 2), 2)
        y = lax.rem(lax.div(f, 4), 4)
        x = lax.div(f, 16)
        self.r, self.c, self.zl, self.y, self.x = r, c, zl, y, x
        self.xs = {d: lax.rem(x + (d + 4), 4) if d else x for d in (-1, 0, 1, 2)}
        self.ys = {d: lax.rem(y + (d + 4), 4) if d else y for d in (-1, 0, 1, 2)}
        low = zl * 2 + c
        self.dx = {d: {"fsdp": self.xs[d] * 16 + y * 4 + low, "rep": r} for d in (-1, 1)}
        self.dy = {d: {"fsdp": x * 16 + self.ys[d] * 4 + low, "rep": r} for d in (-1, 1)}
        turned = f + 2 - 4 * zl
        self.sibling = {"fsdp": f + 1 - 2 * c, "rep": r}
        self.other = {"fsdp": f, "rep": 1 - r}
        self.above = {"fsdp": turned, "rep": lax.rem(r + zl, 2)}
        self.below = {"fsdp": turned, "rep": lax.rem(r + 1 - zl, 2)}
        self.share_to = {"fsdp": turned, "rep": lax.rem(r + zl * (1 - c) + (1 - zl) * c, 2)}
        self.peers = [self.sibling, self.above, self.below, self.other, *self.dx.values(), *self.dy.values()]
        self.starts = {}
        for g in range(len(START)):
            for core, cc in ((0, c), (1, 1 - c)):
                base = START[g] + cc * HALF[g]
                q = base + SIZE[g][0]
                self.starts[g, P_, core] = base
                self.starts[g, QM, core] = q + zl * SIZE[g][1] if ZED[g] else q
                self.starts[g, QO, core] = q + (1 - zl) * SIZE[g][1]


class Wire:
    def __init__(self, place, send, recv):
        self.place, self.send_sem, self.recv_sem = place, send, recv
        self.n = self.m = 0
        self.open = {}

    def slot(self):
        k = self.m % N_SEND
        self.m += 1
        if k in self.open:
            self.open.pop(k).wait_send()
        return k

    def put(self, src, dst, to):
        k = self.slot()
        assert self.n < N_RECV
        copy = pltpu.make_async_remote_copy(
            src_ref=src,
            dst_ref=dst,
            send_sem=self.send_sem.at[k],
            recv_sem=self.recv_sem.at[self.n],
            device_id=to,
            device_id_type=MESH,
        )
        copy.start()
        self.open[k] = copy
        self.n += 1
        return copy

    def drain(self):
        for copy in self.open.values():
            copy.wait_send()
        self.open = {}


def greet(place):
    barrier = pltpu.get_barrier_semaphore()
    for peer in place.peers:
        pl.semaphore_signal(barrier, inc=1, device_id=peer, device_id_type=MESH)
    pl.semaphore_wait(barrier, len(place.peers))


def kind(k):
    return 0 if k == P_ else 1


def halves(g, k):
    n, low = SIZE[g][kind(k)], LOW[g][kind(k)]
    return pl.ds(0, low), pl.ds(low, n - low)


def columns_of(g, k, me, h=None, core=0):
    n, low = SIZE[g][kind(k)], LOW[g][kind(k)]
    off, width = (0, n) if h is None else ((0, low) if h == 0 else (low, n - low))
    base = me.starts[g, k, core]
    return pl.ds(pl.multiple_of(base + off if off else base, 128), width)


class Piece:
    def __init__(self, me, wide, down, g, k):
        self.me, self.wide, self.down, self.g, self.k = me, wide, down, g, k
        self.us, self.ws = (me.xs, me.ys) if k == P_ else (me.ys, me.xs)
        self.first, self.second = (me.dx, me.dy) if k == P_ else (me.dy, me.dx)

    def ref(self, bu, bw, h=None, core=0):
        bx, by = (bu, bw) if self.k == P_ else (bw, bu)
        at = columns_of(self.g, self.k, self.me, h, core)
        if self.g != DOWN:
            return self.wide.at[bx, by, :, at]
        return self.down.at[bx, by, :, 1 - self.me.c if core else self.me.c, :, at]

    def at(self, du, dw, h=None):
        return self.ref(self.us[du], self.ws[dw], h)

    def across(self, dw, h=None):
        return self.ref(slice(None), self.ws[dw], h)

    def along(self, du, h=None):
        return self.ref(self.us[du], slice(None), h)

    def of_sibling(self):
        return self.ref(slice(None), slice(None), core=1)


def wait(*copies):
    yield copies
    for copy in copies:
        copy.wait_recv()


def gather_plane(wire, wide, down, g, k, sib, zs):
    me = wire.place
    s = Piece(me, wide, down, g, k)

    def go(ref, to):
        return wire.put(ref, ref, to)

    def share(name, *where):
        if k == QM and ZED[g]:
            out = [getattr(s, name)(*where, h) for h in range(2)]
            zs.append(((go(out[0], me.above), go(out[1], me.below)), name, where))
        sib.append(go(getattr(s, name)(*where), me.sibling))

    up, dn = {}, {}

    def spread(du):
        up[du] = go(s.at(du, 0), s.second[1])
        dn[du] = go(s.at(du, 0), s.second[-1])

    a, b = go(s.at(0, 0), s.first[1]), go(s.at(0, 0), s.first[-1])
    spread(0)
    yield from wait(a)
    a = go(s.at(-1, 0, 0), s.first[1])
    spread(-1)
    share("at", -1, 0)
    yield from wait(b)
    b = go(s.at(1, 0, 1), s.first[-1])
    spread(1)
    share("at", 1, 0)
    yield from wait(a, b)
    spread(2)
    share("at", 2, 0)
    yield from wait(*[up[du] for du in (0, -1, 1, 2)])
    a = go(s.across(-1, 0), s.second[1])
    share("across", -1)
    yield from wait(*[dn[du] for du in (0, -1, 1, 2)])
    b = go(s.across(1, 1), s.second[-1])
    share("across", 1)
    yield from wait(a, b)
    share("across", 2)


def gather_cross(wire, wide, down, g, sib, zs):
    me = wire.place
    theirs = Piece(me, wide, down, g, QO)
    for n in range(6):
        yield lambda: zs[n][0] if len(zs) > n else None
        copies, name, where = zs[n]
        for copy in copies:
            copy.wait_recv()
        ref = getattr(theirs, name)(*where)
        sib.append(wire.put(ref, ref, me.sibling))


def gather_end(g, sib):
    n = 18 if ZED[g] else 12
    for i in range(n):
        yield lambda: (sib[i],) if len(sib) > i else None
        sib[i].wait_recv()


def gather_streams(wire, wide, down, g):
    sib, zs = [], []
    streams = [gather_plane(wire, wide, down, g, k, sib, zs) for k in (P_, QM)]
    if ZED[g]:
        streams.append(gather_cross(wire, wide, down, g, sib, zs))
    return streams + [gather_end(g, sib)]


def join(stage, wide, me, g):
    step = 640

    def body(i, carry):
        at = pl.ds(pl.multiple_of(START[g] + i * step, 128), step)
        rows = [stage[o, :, at].astype(F32)[:12] for o in range(4)]
        wide[me.x, me.y, :, at] = jnp.concatenate(rows, axis=0).astype(BF)
        return carry

    lax.fori_loop(0, 2 * HALF[g] // step, body, 0)


def gather_front(wire, own_down, stage, wide, down, g):
    me = wire.place
    mine = 2 * me.zl + me.c
    if g != DOWN:
        at = pl.ds(START[g], 2 * HALF[g])
        src = dst = stage.at[mine, :, at]
        hers = stage.at[2 * (1 - me.zl) + me.c, :, at]
    else:
        src, dst = own_down, down.at[me.x, me.y, me.zl, me.c]
        hers = down.at[me.x, me.y, 1 - me.zl, me.c]
        down[me.x, me.y, me.zl, me.c] = own_down[...]
    a = wire.put(src, dst, me.share_to)
    b = wire.put(src, dst, me.sibling)
    yield from wait(a)
    c = wire.put(hers, hers, me.sibling)
    yield from wait(b, c)
    if g != DOWN:
        join(stage, wide, me, g)


def rows_of(g):
    return (2, 48) if g == DOWN else (48,)


REDUCED = (1, 2, 3, 4)


def reduce_shapes(g):
    rows, shapes = rows_of(g), []
    for k in (P_, QM):
        n, low = SIZE[g][kind(k)], LOW[g][kind(k)]
        high = n - low
        own = (48,) if g == DOWN else (2, 16)
        shapes += [(4, 4, *rows, n), (4, *rows, low), (4, *rows, high), (4, *rows, n), (4, *rows, n)]
        shapes += [(*rows, low), (*rows, high), (*rows, n), (*rows, n), (2, *own, n), (*own, n), (*own, n), (*own, n)]
    if ZED[g]:
        shapes += [(4, 4, *rows, SIZE[g][1])] * 2
    shapes = [(s, BF) for s in shapes]
    return shapes if g == DOWN else shapes + [((16, HALF[g]), F32)]


def add_blocks(dst, src):
    def body(i, carry):
        ref = dst(i)
        ref[...] = ref[...] + src(i)[...]
        return carry

    lax.fori_loop(0, 4, body, 0)


def add_one(ref, a):
    ref[...] = ref[...] + a[...]


def add_two(ref, a, b):
    ref[...] = (ref[...].astype(F32) + a[...].astype(F32) + b[...].astype(F32)).astype(BF)


def owners_rows(st, ref, a, b, g):
    total = ref[...].astype(F32) + a[...].astype(F32) + b[...].astype(F32)
    if g != DOWN:
        zero = jnp.zeros((4, total.shape[1]), F32)
        for o in range(4):
            st[o // 2, o % 2] = jnp.concatenate([total[12 * o : 12 * o + 12], zero], axis=0).astype(BF)
    else:
        st[...] = total.astype(BF)


def add_planes(me, g, k, st, rzp, rzm, rr, final, final_down, so):
    def total_of(core):
        def pick(ref):
            return (ref[...] if g == DOWN else ref[core]).astype(F32)

        first = pick(st.at[me.zl]) + pick(rr)
        second = pick(rzp) + pick(rzm)
        if k == QM and ZED[g]:
            return (QM, first), (QO, second)
        return ((k, first + second),)

    out = final_down if g == DOWN else final
    for kk, v in total_of(me.c):
        out[:, columns_of(g, kk, me)] = v
    if g != DOWN:
        for kk, v in total_of(1 - me.c):
            base = me.starts[g, kk, 0] - me.starts[g, P_, 0]
            so[:, pl.ds(pl.multiple_of(base, 128), v.shape[1])] = v


def reduce_plane(wire, wide, down, bufs, got, z_in, done, finals, g, k):
    me = wire.place
    s = Piece(me, wide, down, g, k)
    sb, b1p, b1m, b2p, b2m, c1p, c1m, c2p, c2m, st, rzp, rzm, rr = bufs[13 * k : 13 * k + 13]
    lo, hi = halves(g, k)
    any_lo, any_hi = (..., lo), (..., hi)
    crosses = k == QM and ZED[g]

    def add_along(du, buf):
        bu = s.us[du]
        add_blocks(lambda i: s.ref(bu, i), lambda i: buf.at[bu, i] if k == P_ else buf.at[i, bu])

    def add_half(du, h, buf):
        bu = s.us[du]
        add_blocks(lambda i: s.ref(bu, i, h), lambda i: buf.at[i])

    def ready(du):
        if crosses:
            yield lambda: z_in.get(du)
            for copy in z_in[du]:
                copy.wait_recv()
            add_along(du, bufs[27])
        else:
            add_along(du, sb)

    yield from wait(got)
    if crosses:
        for du in (2, 1, -1, 0):
            add_along(du, sb)
    yield from ready(2)
    r1p = wire.put(s.along(2, 0), b1p, s.first[1])
    r1m = wire.put(s.along(2, 1), b1m, s.first[-1])
    yield from ready(1)
    r2p_hi = wire.put(s.along(1, 1), b2p.at[any_hi], s.first[1])
    yield from ready(-1)
    r2m_lo = wire.put(s.along(-1, 0), b2m.at[any_lo], s.first[-1])
    yield from ready(0)
    yield from wait(r1p)
    add_half(1, 0, b1p)
    r2p_lo = wire.put(s.along(1, 0), b2p.at[any_lo], s.first[1])
    yield from wait(r1m)
    add_half(-1, 1, b1m)
    r2m_hi = wire.put(s.along(-1, 1), b2m.at[any_hi], s.first[-1])
    yield from wait(r2p_hi, r2m_lo, r2p_lo, r2m_hi)

    def close(dw):
        add_two(s.at(0, dw), b2p.at[s.ws[dw]], b2m.at[s.ws[dw]])

    close(2)
    r1p = wire.put(s.at(0, 2, 0), c1p, s.second[1])
    r1m = wire.put(s.at(0, 2, 1), c1m, s.second[-1])
    close(1)
    r2p_hi = wire.put(s.at(0, 1, 1), c2p.at[any_hi], s.second[1])
    close(-1)
    r2m_lo = wire.put(s.at(0, -1, 0), c2m.at[any_lo], s.second[-1])
    close(0)
    yield from wait(r1p)
    add_one(s.at(0, 1, 0), c1p)
    r2p_lo = wire.put(s.at(0, 1, 0), c2p.at[any_lo], s.second[1])
    yield from wait(r1m)
    add_one(s.at(0, -1, 1), c1m)
    r2m_hi = wire.put(s.at(0, -1, 1), c2m.at[any_hi], s.second[-1])
    yield from wait(r2p_hi, r2m_lo, r2p_lo, r2m_hi)
    owners_rows(st, s.at(0, 0), c2p, c2m, g)
    a = wire.put(st.at[1 - me.zl], rzp, me.above)
    b = wire.put(st.at[1 - me.zl], rzm, me.below)
    c = wire.put(st.at[me.zl], rr, me.other)
    yield from wait(a, b, c)
    add_planes(me, g, k, st, rzp, rzm, rr, *finals, None if g == DOWN else bufs[-1])
    done.append(k)
    if g != DOWN and len(done) == 2:
        at = pl.ds(pl.multiple_of(me.starts[g, P_, 0], 128), HALF[g])
        yield from wait(wire.put(bufs[-1], finals[0].at[:, at], me.sibling))


def reduce_cross(wire, wide, down, bufs, got, z_in, g):
    me = wire.place
    theirs = Piece(me, wide, down, g, QO)
    lo, hi = halves(g, QO)
    yield from wait(got)
    for du in (2, 1, -1, 0):
        bu = theirs.us[du]
        add_blocks(lambda i: theirs.ref(bu, i), lambda i: bufs[26].at[i, bu])
        a = wire.put(theirs.along(du, 0), bufs[27].at[:, bu, ..., lo], me.below)
        b = wire.put(theirs.along(du, 1), bufs[27].at[:, bu, ..., hi], me.above)
        z_in[du] = a, b
        if du:
            yield None


def reduce_streams(wire, wide, down, bufs, finals, g):
    me = wire.place
    pieces = {k: Piece(me, wide, down, g, k) for k in (P_, QM, QO)}
    z_in, done, streams = {}, [], []
    if ZED[g]:
        got = wire.put(pieces[QO].of_sibling(), bufs[26], me.sibling)
        streams.append(reduce_cross(wire, wide, down, bufs, got, z_in, g))
    for k in (P_, QM):
        got = wire.put(pieces[k].of_sibling(), bufs[13 * k], me.sibling)
        streams.append(reduce_plane(wire, wide, down, bufs, got, z_in, done, finals, g, k))
    return streams


class Conductor:
    def __init__(self, openers):
        self.openers = openers
        self.streams = {}
        self.place = 0

    def serve(self):
        for key, i in SCHEDULE[self.place]:
            if i < 0:
                self.streams.update({(key, k): s for k, s in enumerate(self.openers[key]())})
                for k in self.streams:
                    if k[0] == key:
                        next(self.streams[k])
            else:
                next(self.streams[key, i], None)
        self.place += 1


SCHEDULE = (
    ((5, -1),),
    (),
    ((6, -1), (7, -1),),
    ((5, 0), (5, 0), (0, -1), (6, 0), (7, 0), (6, 0), (0, 0), (0, 0), (7, 0), (0, 1), (0, 1), (0, 3), (0, 3), (0, 3),
     (0, 0), (0, 3), (0, 2), (0, 2), (0, 3), (0, 3), (0, 3), (0, 1), (1, -1), (0, 0), (0, 0), (0, 3), (0, 2), (0, 1),
     (0, 1), (0, 3), (0, 3), (0, 3), (0, 3), (0, 3), (1, 0), (1, 0), (1, 1), (1, 1), (1, 3), (0, 2), (1, 3), (1, 3),
     (1, 3), (0, 0), (0, 3), (0, 1), (0, 2), (1, 2), (0, 3), (1, 0), (1, 2), (0, 3), (0, 3), (1, 3), (1, 3), (1, 3),
     (0, 2), (1, 1), (0, 3), (2, -1), (1, 3),),
    ((1, 0), (1, 0), (1, 1), (1, 1), (1, 2), (2, 0), (2, 0),),
    ((1, 3), (1, 3), (1, 3), (2, 1), (2, 1), (1, 3), (1, 3),),
    ((1, 1), (1, 0), (1, 2), (1, 2), (2, 0), (2, 2), (2, 2), (2, 2), (2, 2),),
    ((1, 3), (1, 3), (1, 3),),
    ((1, 2), (1, 3), (2, 1), (2, 2), (2, 0), (2, 0), (1, 3),),
    ((2, 1), (2, 1), (2, 2), (2, 2), (2, 2),),
    ((2, 2), (2, 2),),
    ((2, 0),),
    ((2, 1), (2, 2),),
    ((2, 2),),
    ((12, -1),),
    (),
    ((12, 0), (12, 1),),
    ((12, 0),),
    ((12, 0), (12, 1), (12, 1),),
    ((11, -1),),
    (),
    ((11, 0), (11, 0), (11, 0), (11, 0), (12, 0), (11, 1), (12, 0), (12, 1), (11, 2), (11, 2), (12, 0),),
    ((11, 1), (11, 1), (11, 2), (11, 2),),
    ((11, 2), (11, 2), (11, 2), (12, 0), (12, 1), (12, 1),),
    ((13, -1),),
    ((11, 2), (12, 0), (13, 0), (11, 1), (13, 1), (11, 2), (11, 2), (12, 1), (13, 0), (11, 1), (11, 1),),
    ((14, -1), (13, 0), (11, 2), (13, 1), (13, 1), (12, 1), (14, 0), (14, 1), (13, 0), (11, 1), (14, 0), (14, 0),
     (11, 2), (13, 1), (14, 1), (14, 0), (14, 1), (13, 1), (13, 1), (13, 0), (13, 0), (11, 1), (13, 1), (14, 1),
     (14, 0), (14, 0), (11, 1), (13, 0), (14, 1), (14, 1), (14, 0), (13, 1), (14, 1), (13, 0), (14, 0), (13, 0),
     (14, 1), (14, 1),),
)


def dot(a, b):
    return lax.dot_general(a, b, (((1,), (0,)), ((), ())), preferred_element_type=F32)


def dot_nt(a, b):
    return lax.dot_general(a, b, (((1,), (1,)), ((), ())), preferred_element_type=F32)


def loop(n, body):
    def step(i, carry):
        body(i)
        return carry

    lax.fori_loop(0, n, step, 0)


def ds(i, n):
    return pl.ds(pl.multiple_of(i * n, n), n)


T = 256
SCALE = HEAD_DIM ** (-0.5)
O_AT, UP_AT, N1_AT, N2_AT = 2560, 3328, 2304, 2432
ROW = 64


def standardise(v):
    centre = jnp.mean(v, axis=-1, keepdims=True)
    centred = v - centre
    spread = jnp.mean(centred * centred, axis=-1, keepdims=True)
    rstd = lax.rsqrt(spread + 1e-05)
    return centred * rstd, rstd


def weight(wide, at, width):
    return wide[:, :, :, pl.ds(at, width)].reshape(D, width)


def layer_kernel(
    x_ref, seg_ref, n1g_ref, n1b_ref, wq_ref, wk_ref, wv_ref, wo_ref, n2g_ref, n2b_ref, wu_ref, wd_ref, cot_ref,
    out_ref, ig_ref, dn1g_ref, dn1b_ref, dq_ref, dk_ref, dv_ref, do_ref, dn2g_ref, dn2b_ref, du_ref, dd_ref,
    *scratch,
):
    bufs = {}
    for g in REDUCED:
        n = len(reduce_shapes(g))
        bufs[g], scratch = scratch[:n], scratch[n:]
    (
        wide, down, gwide, gdown, stage, final, final_down,
        mask, xhat, rstd1, xhat2, rstd2, n1, n1t, n2, qkv, mixed, probs, hidden,
        act, slope, acc_out, acc_in, dqkv, rows1, rows2, send, recv,
    ) = scratch
    place = me = Place()
    greet(place)
    wire = Wire(place, send, recv)
    openers = {g: lambda g=g: gather_streams(wire, wide, down, g) for g in range(3)}
    openers.update({5 + g: lambda g=g: [gather_front(wire, wd_ref, stage, wide, down, g)] for g in range(3)})
    finals = final, final_down
    openers.update({10 + g: lambda g=g: reduce_streams(wire, gwide, gdown, bufs[g], finals, g) for g in REDUCED})
    conductor = Conductor(openers)
    serve = conductor.serve
    mine = 2 * me.zl + me.c

    zero4 = lambda n: jnp.zeros((4, n), F32)

    def put_own(ref, at):
        n = ref.shape[1]
        rows = jnp.concatenate([ref[...].astype(F32), zero4(n)], axis=0)
        stage[mine, :, pl.ds(at, n)] = rows.astype(BF)

    def put_norm(gain, shift, at):
        eye = lax.broadcasted_iota(jnp.int32, (16, 12), 0) == lax.broadcasted_iota(jnp.int32, (16, 12), 1)
        lane = lax.broadcasted_iota(jnp.int32, (16, 128), 1)
        a = jnp.sum(jnp.where(eye, gain[...].astype(F32), 0.0), axis=1, keepdims=True)
        b = jnp.sum(jnp.where(eye, shift[...].astype(F32), 0.0), axis=1, keepdims=True)
        both = jnp.where(lane == 0, a, jnp.where(lane == 1, b, 0.0))
        stage[mine, :, pl.ds(at, 128)] = both.astype(BF)

    for i, ref in enumerate((wq_ref, wk_ref, wv_ref)):
        put_own(ref, 768 * i)
    put_norm(n1g_ref, n1b_ref, N1_AT)
    put_norm(n2g_ref, n2b_ref, N2_AT)
    serve()
    put_own(wo_ref, O_AT)
    put_own(wu_ref, UP_AT)
    serve()

    segs = jnp.broadcast_to(seg_ref[...], (T, T))
    rows_iota = lax.broadcasted_iota(jnp.int32, (T, T), 0)
    cols_iota = lax.broadcasted_iota(jnp.int32, (T, T), 1)
    allowed = (rows_iota >= cols_iota) & (segs.astype(F32).T == segs.astype(F32))
    mask[...] = jnp.where(allowed, 0.0, -1e30)

    serve()

    def norm1_rows(i):
        at = ds(i, ROW)
        hat, rstd = standardise(x_ref[at, :].astype(F32))
        xhat[at, :] = hat
        rstd1[at, :] = rstd

    loop(T // ROW, norm1_rows)
    serve()

    eye = (
        lax.broadcasted_iota(jnp.int32, (128, 128), 0) == lax.broadcasted_iota(jnp.int32, (128, 128), 1)
    ).astype(BF)
    rows1[...] = dot_nt(eye, weight(wide, N1_AT, 128))[:8]
    rows2[...] = dot_nt(eye, weight(wide, N2_AT, 128))[:8]

    def norm1_apply(i):
        at = ds(i, ROW)
        n1[at, :] = (xhat[at, :] * rows1[0:1, :] + rows1[1:2, :]).astype(BF)

    loop(T // ROW, norm1_apply)

    def project(i):
        at = ds(i, 256)
        w = wide[:, :, :, at].reshape(D, 256)
        qkv[:, at] = dot(n1[...], w).astype(BF)

    loop(9, project)
    serve()
    lane = lax.broadcasted_iota(jnp.int32, (1, 128), 1)
    heads = [((lane >= 32 * h) & (lane < 32 * h + 32)).astype(F32).astype(BF) for h in range(4)]

    def group(ref, which, t):
        return ref[:, pl.ds(pl.multiple_of(768 * which + 128 * t, 128), 128)]

    def attend(t):
        q4, k4, v4 = [group(qkv, i, t) for i in range(3)]
        vh = [v4 * heads[h] for h in range(4)]
        for rb in range(2):
            rows, nk = slice(128 * rb, 128 * rb + 128), 128 * rb + 128
            total = jnp.zeros((128, 128), F32)
            for h in range(4):
                s = dot_nt(q4[rows] * heads[h], k4[:nk]) * SCALE + mask[rows, :nk]
                e = jnp.exp(s - jnp.max(s, axis=1, keepdims=True))
                p = (e * (1.0 / jnp.sum(e, axis=1, keepdims=True))).astype(BF)
                probs[4 * t + h, rows, :nk] = p
                total = total + dot(p, vh[h][:nk])
            mixed[rows, pl.ds(pl.multiple_of(128 * t, 128), 128)] = total.astype(BF)

    for part in range(3):
        loop(2, lambda i: attend(2 * part + i))
        serve()

    n2t, mixt = [gwide.at[:, :, :, pl.ds(256 * k, 256)] for k in range(2)]

    def transpose(src, dst):
        def body(i):
            dst[ds(i, 2)] = src[:, ds(i, 384)].T.reshape(2, 4, 48, T)

        loop(2, body)

    def turn_n1(i):
        n1t[ds(i, 384), :] = n1[:, ds(i, 384)].T

    transpose(mixed, mixt)
    loop(2, turn_n1)
    serve()

    def out_project(i):
        at = ds(i, 256)
        w = wide[:, :, :, pl.ds(pl.multiple_of(O_AT + 256 * i, 128), 256)].reshape(D, 256)
        hidden[:, at] = x_ref[:, at].astype(F32) + dot(mixed[...], w)

    loop(3, out_project)

    def norm2_rows(i):
        at = ds(i, ROW)
        hat, rstd = standardise(hidden[at, :])
        xhat2[at, :] = hat
        rstd2[at, :] = rstd
        n2[at, :] = (hat * rows2[0:1, :] + rows2[1:2, :]).astype(BF)

    loop(T // ROW, norm2_rows)
    transpose(n2, n2t)
    serve()

    c0 = (2.0 / 3.141592653589793) ** 0.5

    def feed(i):
        def part(j):
            at = pl.ds(pl.multiple_of(UP_AT + 768 * i + 256 * j, 128), 256)
            v = dot(n2[...], wide[:, :, :, at].reshape(D, 256))
            sq = v * v
            th = jnp.tanh(c0 * v * (1.0 + 0.044715 * sq))
            half = 0.5 + 0.5 * th
            a = (v * half).astype(BF)
            keep = pl.ds(pl.multiple_of(768 * i + 256 * j, 128), 256)
            act[:, keep] = a
            slope[:, keep] = half + 0.5 * v * (1.0 - th * th) * (c0 * (1.0 + 0.134145 * sq))

        loop(3, part)
        a = act[:, ds(i, 768)].T

        def grad(j):
            at = ds(j, 256)
            gdown[i, :, :, :, :, at] = dot(a, cot_ref[:, at]).astype(BF).reshape(4, 2, 2, 48, 256)

        loop(3, grad)

    for i in range(4):
        feed(i)
        serve()
    serve()

    acc_out[...] = hidden[...]
    acc_in[...] = jnp.zeros((T, D), F32)

    def feed_back(i):
        at = ds(i, 768)
        wd = down[i].reshape(768, 768)
        acc_out[...] += dot(act[:, at], wd)
        pg = (dot_nt(cot_ref[...], wd) * slope[:, at]).astype(BF)
        act[:, at] = pg
        up_at = pl.ds(pl.multiple_of(UP_AT + 768 * i, 128), 768)
        acc_in[...] += dot_nt(pg, wide[:, :, :, up_at].reshape(D, 768))

        def grad(j):
            cols_j = pl.ds(pl.multiple_of(UP_AT + 768 * i + 256 * j, 128), 256)
            pg_j = act[:, pl.ds(pl.multiple_of(768 * i + 256 * j, 128), 256)]
            gwide[:, :, :, cols_j] = dot(n2t[...].reshape(D, T), pg_j).astype(BF).reshape(4, 4, 48, 256)

        loop(3, grad)

    for i in range(4):
        feed_back(i)
        serve()
    out_ref[...] = acc_out[...].astype(BF)

    def norm_back(grad, hat, rstd, gain, at):
        gn = gain * grad
        m1 = jnp.mean(gn, axis=-1, keepdims=True)
        m2 = jnp.mean(gn * hat, axis=-1, keepdims=True)
        return (gn - m1 - hat * m2) * rstd

    def norm2_back(i, sums):
        at = ds(i, ROW)
        grad, hat = acc_in[at, :], xhat2[at, :]
        extra = norm_back(grad, hat, rstd2[at, :], rows2[0:1, :], at)
        hidden[at, :] = cot_ref[at, :].astype(F32) + extra
        a, b = sums
        return a + jnp.sum(grad * hat, axis=0, keepdims=True), b + jnp.sum(grad, axis=0, keepdims=True)

    def as_columns(sums, at):
        rows = jnp.concatenate([*sums, jnp.zeros((126, D), F32)], axis=0)
        gwide[:, :, :, pl.ds(at, 128)] = rows.T.astype(BF).reshape(4, 4, 48, 128)

    nothing = jnp.zeros((1, D), F32)
    as_columns(lax.fori_loop(0, T // ROW, norm2_back, (nothing, nothing)), N2_AT)
    n2[...] = hidden[...].astype(BF)

    def o_back(i):
        at = ds(i, 256)
        b = n2[:, at]
        gwide[:, :, :, pl.ds(pl.multiple_of(O_AT + 256 * i, 128), 256)] = (
            dot(mixt[...].reshape(D, T), b).astype(BF).reshape(4, 4, 48, 256)
        )

    loop(3, o_back)
    serve()
    mgrad = n1
    mgrad[...] = dot_nt(n2[...], weight(wide, O_AT, D)).astype(BF)
    serve()

    def attend_back(t):
        q4, k4, v4 = [group(qkv, i, t) for i in range(3)]
        do4, o4 = group(mgrad, 0, t), group(mixed, 0, t)
        q4t, do4t = q4.T, do4.T
        kh = [k4 * heads[h] for h in range(4)]
        dk, dv = [], []
        total = [jnp.zeros((128, 128), F32)] * 2
        for h in range(4):
            hrows = slice(32 * h, 32 * h + 32)
            dkh, dvh = [], []
            for rb in range(2):
                rows, nk = slice(128 * rb, 128 * rb + 128), 128 * rb + 128
                dob = do4[rows] * heads[h]
                dot_row = jnp.sum(dob.astype(F32) * o4[rows].astype(F32), axis=1, keepdims=True)
                p = probs[4 * t + h, rows, :nk]
                sg = (p.astype(F32) * (dot_nt(dob, v4[:nk]) - dot_row)).astype(BF)
                total[rb] = total[rb] + dot(sg, kh[h][:nk])
                dkh.append(dot(q4t[hrows, rows], sg))
                dvh.append(dot(do4t[hrows, rows], p))
            for both, parts in ((dk, dkh), (dv, dvh)):
                both.append(jnp.concatenate([parts[1][:, :128] + parts[0], parts[1][:, 128:]], axis=1))
        at = pl.multiple_of(128 * t, 128)
        for rb in range(2):
            dqkv[pl.ds(128 * rb, 128), pl.ds(at, 128)] = (total[rb] * SCALE).astype(BF)
        dqkv[:, pl.ds(at + 768, 128)] = (jnp.concatenate(dk, axis=0).T * SCALE).astype(BF)
        dqkv[:, pl.ds(at + 1536, 128)] = jnp.concatenate(dv, axis=0).T.astype(BF)

    for part in range(3):
        loop(2, lambda i: attend_back(2 * part + i))
        serve()

    def qkv_grad(i):
        at = ds(i, 256)
        gwide[:, :, :, at] = dot(n1t[...], dqkv[:, at]).astype(BF).reshape(4, 4, 48, 256)

    loop(6, qkv_grad)
    serve()
    acc_in[...] = dot_nt(dqkv[:, :768], weight(wide, 0, D))
    acc_in[...] += dot_nt(dqkv[:, 768:1536], weight(wide, 768, D))
    acc_in[...] += dot_nt(dqkv[:, 1536:], weight(wide, 1536, D))
    serve()

    def norm1_back(i, sums):
        at = ds(i, ROW)
        grad, hat = acc_in[at, :], xhat[at, :]
        extra = norm_back(grad, hat, rstd1[at, :], rows1[0:1, :], at)
        ig_ref[at, :] = hidden[at, :] + extra
        a, b = sums
        return a + jnp.sum(grad * hat, axis=0, keepdims=True), b + jnp.sum(grad, axis=0, keepdims=True)

    as_columns(lax.fori_loop(0, T // ROW, norm1_back, (nothing, nothing)), N1_AT)
    loop(3, lambda i: qkv_grad(6 + i))
    serve()

    wire.drain()

    dd_ref[...] = final_down[...]
    for i, ref in enumerate((dq_ref, dk_ref, dv_ref)):
        ref[...] = final[:12, 768 * i : 768 * i + 768]
    do_ref[...] = final[:12, O_AT:UP_AT]
    du_ref[...] = final[:12, UP_AT:]
    diag = lax.broadcasted_iota(jnp.int32, (16, 128), 0) == lax.broadcasted_iota(jnp.int32, (16, 128), 1)
    for at, refs in ((N1_AT, (dn1g_ref, dn1b_ref)), (N2_AT, (dn2g_ref, dn2b_ref))):
        for k, ref in enumerate(refs):
            col = final[:, at + k : at + k + 1]
            ref[...] = jnp.sum(jnp.where(diag, col, 0.0), axis=0, keepdims=True)[:, :12]


def publish_kernel(*refs):
    n = len(refs) // 2
    for i in range(n):
        refs[n + i][...] = refs[i][...]


VM = pl.BlockSpec(memory_space=pltpu.VMEM)


def per_device(*args):
    args = [a.reshape(1, 12) if a.ndim == 1 else a for a in args]
    like = jax.ShapeDtypeStruct
    vec, square = like((1, 12), F32), like((12, D), F32)
    scratch = [pltpu.VMEM(s, t) for g in REDUCED for s, t in reduce_shapes(g)]
    wide, down = pltpu.VMEM((4, 4, 48, WIDE), BF), pltpu.VMEM((4, 4, 2, 2, 48, D), BF)
    scratch += [wide, down, wide, down, pltpu.VMEM((4, 16, WIDE), BF), pltpu.VMEM((16, WIDE), F32), pltpu.VMEM((48, D), F32)]
    f32s, bfs = pltpu.VMEM((T, D), F32), pltpu.VMEM((T, D), BF)
    one, turned = pltpu.VMEM((T, 1), F32), pltpu.VMEM((D, T), BF)
    scratch += [pltpu.VMEM((T, T), F32), f32s, one, f32s, one]
    scratch += [bfs, turned, bfs, pltpu.VMEM((T, 3 * D), BF), bfs]
    scratch += [pltpu.VMEM((HEADS, T, T), BF), f32s]
    scratch += [pltpu.VMEM((T, FF), BF), pltpu.VMEM((T, FF), F32), f32s, f32s]
    scratch += [pltpu.VMEM((T, 3 * D), BF), pltpu.VMEM((8, D), F32), pltpu.VMEM((8, D), F32)]
    scratch += [pltpu.SemaphoreType.DMA((N_SEND,)), pltpu.SemaphoreType.DMA((N_RECV,))]
    outs = pl.pallas_call(
        layer_kernel,
        out_shape=(
            like((T, D), BF), like((T, D), F32), vec, vec, square, square, square, square, vec, vec,
            like((12, FF), F32), like((48, D), F32),
        ),
        in_specs=[VM] * 13,
        out_specs=(VM,) * 12,
        scratch_shapes=scratch,
        compiler_params=pltpu.CompilerParams(
            collective_id=0, has_side_effects=True, vmem_limit_bytes=VMEM_BYTES
        ),
        cost_estimate=pl.CostEstimate(flops=13 * 10**9, bytes_accessed=6 * 10**6, transcendentals=3 * 10**6),
        name="layer",
    )(*args)
    outs = pl.pallas_call(
        publish_kernel,
        out_shape=tuple(like(o.shape, o.dtype) for o in outs),
        in_specs=[VM] * 12,
        out_specs=(VM,) * 12,
        name="publish",
    )(*outs)
    return tuple(o.reshape(12) if o.shape == (1, 12) else o for o in outs)


def solution(mesh):
    placed = (
        P(("fsdp", "rep"), None),
        P(("fsdp", "rep"), None),
        P("fsdp"),
        P("fsdp"),
        P("fsdp", None),
        P("fsdp", None),
        P("fsdp", None),
        P("fsdp", None),
        P("fsdp"),
        P("fsdp"),
        P("fsdp", None),
        P("fsdp", None),
        P(("fsdp", "rep"), None),
    )
    return jax.shard_map(
        per_device,
        mesh=mesh,
        in_specs=placed,
        out_specs=(
            P(("fsdp", "rep"), None),
            P(("fsdp", "rep"), None),
            P("fsdp"),
            P("fsdp"),
            P("fsdp", None),
            P("fsdp", None),
            P("fsdp", None),
            P("fsdp", None),
            P("fsdp"),
            P("fsdp"),
            P("fsdp", None),
            P("fsdp", None),
        ),
        check_vma=False,
    )
```

time: 168 us -> 134 us (0.80)
  Pallas kernels: 157 us -> 133 us
  local copies, waits for them, and re-layouts: 9.36 us -> 0 us
    pallas_call x1, Pallas kernels: 157 us -> 130 us  [per_device(): pl.pallas_call(layer_kernel, out_shape=(like((T, D), BF), like((T, D), F3...]
    unnamed x34 -> x0, local copies, waits for them, and re-layouts: 9.36 us -> none
    pallas_call x0 -> x1, Pallas kernels: none -> 2.67 us  [per_device(): pl.pallas_call(publish_kernel, out_shape=tuple((like(o.shape, o.dtype) fo...]
where the time goes in v3:
time: 134 us; the launch traced here: 133 us
  Pallas kernels  133 us (99%)
    pallas_call x1, Pallas kernels, per_device(): pl.pallas_call(layer_kernel, out_shape=(like((T, D), BF), like((T, D), F3...  130 us

profile of v3, /device:TPU:1, one launch (start us, length us, event | category | flops | bytes accessed | tf_op | source)
XLA Modules:
  0.0 133.4 jit_solution(1218007095750985197)
XLA Ops:
  0.6 130.0 %layer.1 = (bf16[256,768]{1,0:T(8,128)(2,1)}, f32[256,768]{1,0:T(8,128)}, f32[1,12]{1,0:T(1,128)}, f32[1,12]{1,0:T(1,128)}, f32[12,768]{1,0:T(8,128)}, /*index=5...) custom-call(bf16[256,768]{1,0:T(8,128)(2,1)} %x_ref.1, ...), custom_call_target="tpu_custom_call" | custom-call | flops 12999999488 | bytes 6000000 | tf_op jit(solution)/shard_map/layer/pallas_call | solution.py:839
  130.6 2.7 %publish.1 = (bf16[256,768]{1,0:T(8,128)(2,1)}, f32[256,768]{1,0:T(8,128)}, f32[1,12]{1,0:T(1,128)}, f32[1,12]{1,0:T(1,128)}, f32[12,768]{1,0:T(8,128)}, /*index...) custom-call(bf16[256,768]{1,0:T(8,128)(2,1)} %get-tuple-element.36.r, ...), custom_call_target="tpu_custom_call" | custom-call | tf_op jit(solution)/shard_map/publish/pallas_call | solution.py:854

commit v4 on v3

--- a/solution.py
+++ b/solution.py
@@ -17,13 +17,18 @@
 
 WIDE = 6400
 DOWN = 2
-START = (0, 2560, 0, 0, 1536)
-HALF = (1280, 1920, 0, 768, 512)
-SIZE = ((512, 384), (896, 512), (384, 384), (384, 384), (256, 256))
-LOW = ((256, 128), (384, 256), (128, 256), (128, 256), (128, 128))
-ZED = (True, True, False, False, False)
+START = (0, 2560, 0, 0, 384, 768, 2560, 4096)
+HALF = (1280, 1920, 0, 1280, 1280, 1280, 768, 1152)
+WIDTH = (1280, 1920, 768, 384, 384, 512, 768, 1152)
+P_AT = (768, 0, 0, 0, 0, 0, 0, 0)
+Q_AT = (0, 384, 384, 256, 128, 256, 256, 384)
+SIZE = ((512, 384), (384, 768), (384, 384), (256, 128), (128, 256), (256, 256), (256, 256), (384, 384))
+LOW = ((256, 256), (128, 384), (128, 256), (128, 128), (128, 128), (128, 128), (128, 128), (128, 256))
+ZED = (True, True, False, False, False, False, True, True)
+STRAIGHT = (False, False, False)
+DIRECT = (False, False, False, True, True, True, False, True)
 P_, QM, QO = 0, 1, 2
-N_RECV = 305
+N_RECV = 332
 N_SEND = 40
 VMEM_BYTES = 66700000
 
@@ -40,8 +45,8 @@
         self.xs = {d: lax.rem(x + (d + 4), 4) if d else x for d in (-1, 0, 1, 2)}
         self.ys = {d: lax.rem(y + (d + 4), 4) if d else y for d in (-1, 0, 1, 2)}
         low = zl * 2 + c
-        self.dx = {d: {"fsdp": self.xs[d] * 16 + y * 4 + low, "rep": r} for d in (-1, 1)}
-        self.dy = {d: {"fsdp": x * 16 + self.ys[d] * 4 + low, "rep": r} for d in (-1, 1)}
+        self.dx = {d: {"fsdp": self.xs[d] * 16 + y * 4 + low, "rep": r} for d in (-1, 1, 2)}
+        self.dy = {d: {"fsdp": x * 16 + self.ys[d] * 4 + low, "rep": r} for d in (-1, 1, 2)}
         turned = f + 2 - 4 * zl
         self.sibling = {"fsdp": f + 1 - 2 * c, "rep": r}
         self.other = {"fsdp": f, "rep": 1 - r}
@@ -53,8 +58,9 @@
         for g in range(len(START)):
             for core, cc in ((0, c), (1, 1 - c)):
                 base = START[g] + cc * HALF[g]
-                q = base + SIZE[g][0]
-                self.starts[g, P_, core] = base
+                self.starts[g, None, core] = base
+                q = base + Q_AT[g]
+                self.starts[g, P_, core] = base + P_AT[g]
                 self.starts[g, QM, core] = q + zl * SIZE[g][1] if ZED[g] else q
                 self.starts[g, QO, core] = q + (1 - zl) * SIZE[g][1]
 
@@ -158,37 +164,52 @@
 
     def share(name, *where):
         if k == QM and ZED[g]:
-            out = [getattr(s, name)(*where, h) for h in range(2)]
-            zs.append(((go(out[0], me.above), go(out[1], me.below)), name, where))
+            lo, hi = [getattr(s, name)(*where, h) for h in range(2)]
+            zs.append(((go(lo, me.above), go(hi, me.below)), name, where))
         sib.append(go(getattr(s, name)(*where), me.sibling))
 
-    up, dn = {}, {}
+    out = {}
 
     def spread(du):
-        up[du] = go(s.at(du, 0), s.second[1])
-        dn[du] = go(s.at(du, 0), s.second[-1])
-
-    a, b = go(s.at(0, 0), s.first[1]), go(s.at(0, 0), s.first[-1])
+        for d in reach:
+            out[d, du] = go(s.at(du, 0), s.second[d])
+
+    if not STRAIGHT[g]:
+        reach = (1, -1)
+        a, b = go(s.at(0, 0), s.first[1]), go(s.at(0, 0), s.first[-1])
+        spread(0)
+        yield from wait(a)
+        a = go(s.at(-1, 0, 0), s.first[1])
+        spread(-1)
+        share("at", -1, 0)
+        yield from wait(b)
+        b = go(s.at(1, 0, 1), s.first[-1])
+        spread(1)
+        share("at", 1, 0)
+        yield from wait(a, b)
+        spread(2)
+        share("at", 2, 0)
+        yield from wait(*[out[1, du] for du in (0, -1, 1, 2)])
+        a = go(s.across(-1, 0), s.second[1])
+        share("across", -1)
+        yield from wait(*[out[-1, du] for du in (0, -1, 1, 2)])
+        b = go(s.across(1, 1), s.second[-1])
+        share("across", 1)
+        yield from wait(a, b)
+        share("across", 2)
+        return
+    reach = (1, -1, 2)
+    near = {d: go(s.at(0, 0), s.first[d]) for d in reach}
     spread(0)
-    yield from wait(a)
-    a = go(s.at(-1, 0, 0), s.first[1])
-    spread(-1)
-    share("at", -1, 0)
-    yield from wait(b)
-    b = go(s.at(1, 0, 1), s.first[-1])
-    spread(1)
-    share("at", 1, 0)
-    yield from wait(a, b)
-    spread(2)
-    share("at", 2, 0)
-    yield from wait(*[up[du] for du in (0, -1, 1, 2)])
-    a = go(s.across(-1, 0), s.second[1])
-    share("across", -1)
-    yield from wait(*[dn[du] for du in (0, -1, 1, 2)])
-    b = go(s.across(1, 1), s.second[-1])
-    share("across", 1)
-    yield from wait(a, b)
-    share("across", 2)
+    for d in (1, -1, 2):
+        du = -d if d < 2 else 2
+        yield from wait(near[d])
+        spread(du)
+        share("at", du, 0)
+    for d in (1, -1, 2):
+        dw = -d if d < 2 else 2
+        yield from wait(*[out[d, du] for du in (0, -1, 1, 2)])
+        share("across", dw)
 
 
 def gather_cross(wire, wide, down, g, sib, zs):
@@ -203,19 +224,19 @@
         sib.append(wire.put(ref, ref, me.sibling))
 
 
-def gather_end(g, sib):
-    n = 18 if ZED[g] else 12
+def gather_end(n, sib):
     for i in range(n):
         yield lambda: (sib[i],) if len(sib) > i else None
         sib[i].wait_recv()
 
 
 def gather_streams(wire, wide, down, g):
-    sib, zs = [], []
-    streams = [gather_plane(wire, wide, down, g, k, sib, zs) for k in (P_, QM)]
+    sib, zs = {P_: [], QM: [], QO: []}, []
+    streams = [gather_plane(wire, wide, down, g, k, sib[k], zs) for k in (P_, QM)]
+    streams += [gather_end(6, sib[k]) for k in (P_, QM)]
     if ZED[g]:
-        streams.append(gather_cross(wire, wide, down, g, sib, zs))
-    return streams + [gather_end(g, sib)]
+        streams += [gather_cross(wire, wide, down, g, sib[QO], zs), gather_end(6, sib[QO])]
+    return streams
 
 
 def join(stage, wide, me, g):
@@ -254,7 +275,7 @@
     return (2, 48) if g == DOWN else (48,)
 
 
-REDUCED = (1, 2, 3, 4)
+REDUCED = (2, 3, 4, 5, 6, 7)
 
 
 def reduce_shapes(g):
@@ -262,13 +283,15 @@
     for k in (P_, QM):
         n, low = SIZE[g][kind(k)], LOW[g][kind(k)]
         high = n - low
+        if DIRECT[g]:
+            low, high = n, 128
         own = (48,) if g == DOWN else (2, 16)
         shapes += [(4, 4, *rows, n), (4, *rows, low), (4, *rows, high), (4, *rows, n), (4, *rows, n)]
         shapes += [(*rows, low), (*rows, high), (*rows, n), (*rows, n), (2, *own, n), (*own, n), (*own, n), (*own, n)]
     if ZED[g]:
         shapes += [(4, 4, *rows, SIZE[g][1])] * 2
     shapes = [(s, BF) for s in shapes]
-    return shapes if g == DOWN else shapes + [((16, HALF[g]), F32)]
+    return shapes if g == DOWN else shapes + [((16, WIDTH[g]), F32)]
 
 
 def add_blocks(dst, src):
@@ -288,8 +311,15 @@
     ref[...] = (ref[...].astype(F32) + a[...].astype(F32) + b[...].astype(F32)).astype(BF)
 
 
-def owners_rows(st, ref, a, b, g):
-    total = ref[...].astype(F32) + a[...].astype(F32) + b[...].astype(F32)
+def add_three(ref, a, b, c):
+    total = ref[...].astype(F32) + a[...].astype(F32) + (b[...].astype(F32) + c[...].astype(F32))
+    ref[...] = total.astype(BF)
+
+
+def owners_rows(st, ref, others, g):
+    total = ref[...].astype(F32)
+    for other in others:
+        total = total + other[...].astype(F32)
     if g != DOWN:
         zero = jnp.zeros((4, total.shape[1]), F32)
         for o in range(4):
@@ -314,7 +344,7 @@
         out[:, columns_of(g, kk, me)] = v
     if g != DOWN:
         for kk, v in total_of(1 - me.c):
-            base = me.starts[g, kk, 0] - me.starts[g, P_, 0]
+            base = me.starts[g, kk, 0] - me.starts[g, None, 0]
             so[:, pl.ds(pl.multiple_of(base, 128), v.shape[1])] = v
 
 
@@ -347,6 +377,23 @@
     if crosses:
         for du in (2, 1, -1, 0):
             add_along(du, sb)
+    if DIRECT[g]:
+        got = []
+        for du, buf in ((2, b1p), (1, b2p), (-1, b2m)):
+            yield from ready(du)
+            got.append(wire.put(s.along(du), buf, s.first[du]))
+        yield from ready(0)
+        yield from wait(*got)
+        got = []
+        for dw, buf in ((2, c1p), (1, c2p), (-1, c2m), (0, None)):
+            bw = s.ws[dw]
+            add_three(s.at(0, dw), b1p.at[bw], b2p.at[bw], b2m.at[bw])
+            if dw:
+                got.append(wire.put(s.at(0, dw), buf, s.second[dw]))
+        yield from wait(*got)
+        owners_rows(st, s.at(0, 0), (c1p, c2p, c2m), g)
+        yield from over_planes(wire, me, g, k, bufs, st, rzp, rzm, rr, finals, done)
+        return
     yield from ready(2)
     r1p = wire.put(s.along(2, 0), b1p, s.first[1])
     r1m = wire.put(s.along(2, 1), b1m, s.first[-1])
@@ -381,7 +428,11 @@
     add_one(s.at(0, -1, 1), c1m)
     r2m_hi = wire.put(s.at(0, -1, 1), c2m.at[any_hi], s.second[-1])
     yield from wait(r2p_hi, r2m_lo, r2p_lo, r2m_hi)
-    owners_rows(st, s.at(0, 0), c2p, c2m, g)
+    owners_rows(st, s.at(0, 0), (c2p, c2m), g)
+    yield from over_planes(wire, me, g, k, bufs, st, rzp, rzm, rr, finals, done)
+
+
+def over_planes(wire, me, g, k, bufs, st, rzp, rzm, rr, finals, done):
     a = wire.put(st.at[1 - me.zl], rzp, me.above)
     b = wire.put(st.at[1 - me.zl], rzm, me.below)
     c = wire.put(st.at[me.zl], rr, me.other)
@@ -389,7 +440,7 @@
     add_planes(me, g, k, st, rzp, rzm, rr, *finals, None if g == DOWN else bufs[-1])
     done.append(k)
     if g != DOWN and len(done) == 2:
-        at = pl.ds(pl.multiple_of(me.starts[g, P_, 0], 128), HALF[g])
+        at = pl.ds(pl.multiple_of(me.starts[g, None, 0], 128), WIDTH[g])
         yield from wait(wire.put(bufs[-1], finals[0].at[:, at], me.sibling))
 
 
@@ -443,37 +494,63 @@
     ((5, -1),),
     (),
     ((6, -1), (7, -1),),
-    ((5, 0), (5, 0), (0, -1), (6, 0), (7, 0), (6, 0), (0, 0), (0, 0), (7, 0), (0, 1), (0, 1), (0, 3), (0, 3), (0, 3),
-     (0, 0), (0, 3), (0, 2), (0, 2), (0, 3), (0, 3), (0, 3), (0, 1), (1, -1), (0, 0), (0, 0), (0, 3), (0, 2), (0, 1),
-     (0, 1), (0, 3), (0, 3), (0, 3), (0, 3), (0, 3), (1, 0), (1, 0), (1, 1), (1, 1), (1, 3), (0, 2), (1, 3), (1, 3),
-     (1, 3), (0, 0), (0, 3), (0, 1), (0, 2), (1, 2), (0, 3), (1, 0), (1, 2), (0, 3), (0, 3), (1, 3), (1, 3), (1, 3),
-     (0, 2), (1, 1), (0, 3), (2, -1), (1, 3),),
-    ((1, 0), (1, 0), (1, 1), (1, 1), (1, 2), (2, 0), (2, 0),),
-    ((1, 3), (1, 3), (1, 3), (2, 1), (2, 1), (1, 3), (1, 3),),
-    ((1, 1), (1, 0), (1, 2), (1, 2), (2, 0), (2, 2), (2, 2), (2, 2), (2, 2),),
-    ((1, 3), (1, 3), (1, 3),),
-    ((1, 2), (1, 3), (2, 1), (2, 2), (2, 0), (2, 0), (1, 3),),
-    ((2, 1), (2, 1), (2, 2), (2, 2), (2, 2),),
-    ((2, 2), (2, 2),),
-    ((2, 0),),
-    ((2, 1), (2, 2),),
+    ((5, 0), (6, 0), (5, 0), (0, -1), (7, 0), (6, 0), (7, 0), (0, 0), (0, 0), (0, 1), (0, 1), (0, 2), (0, 2), (0, 0),
+     (1, -1), (0, 3), (0, 3), (0, 4), (0, 4), (0, 2), (0, 1), (1, 0), (0, 5), (1, 0), (0, 0), (0, 0), (0, 5), (0, 3),
+     (0, 4), (1, 2), (1, 2), (0, 1), (0, 1), (0, 2), (1, 1), (1, 1), (1, 0), (0, 2), (0, 5), (0, 3), (0, 3), (1, 3),
+     (1, 3), (1, 2), (0, 1), (0, 4), (0, 0), (1, 1), (1, 0), (1, 0), (0, 4), (0, 3), (0, 5), (0, 2), (2, -1), (1, 4),),
+    ((1, 2), (1, 2), (1, 3), (1, 4),),
+    ((0, 5), (1, 1), (1, 1), (1, 5),),
+    ((0, 4), (1, 0),),
+    (),
+    ((1, 4), (1, 5), (2, 0), (2, 0),),
+    ((1, 3),),
+    ((1, 3), (2, 1), (0, 5),),
+    (),
+    ((1, 2), (1, 5), (2, 1), (2, 2), (2, 2),),
+    ((1, 4),),
+    ((2, 3),),
+    ((1, 1), (2, 0), (2, 3), (1, 5), (2, 1), (1, 4), (1, 3), (2, 2), (2, 3), (2, 0), (2, 0), (1, 5), (2, 1), (2, 1),
+     (1, 4), (2, 2), (2, 2), (2, 3), (2, 3), (1, 5),),
+    ((2, 0), (2, 1),),
+    (),
+    (),
+    (),
+    (),
+    (),
+    (),
+    (),
     ((2, 2),),
-    ((12, -1),),
-    (),
-    ((12, 0), (12, 1),),
+    ((12, -1), (2, 3),),
+    (),
+    (),
+    (),
+    (),
+    (),
+    ((16, -1), (12, 0),),
+    (),
+    ((12, 1), (16, 0), (16, 0), (16, 0), (16, 0),),
+    ((16, 1), (12, 0), (16, 2),),
+    ((16, 2),),
     ((12, 0),),
-    ((12, 0), (12, 1), (12, 1),),
-    ((11, -1),),
-    (),
-    ((11, 0), (11, 0), (11, 0), (11, 0), (12, 0), (11, 1), (12, 0), (12, 1), (11, 2), (11, 2), (12, 0),),
-    ((11, 1), (11, 1), (11, 2), (11, 2),),
-    ((11, 2), (11, 2), (11, 2), (12, 0), (12, 1), (12, 1),),
-    ((13, -1),),
-    ((11, 2), (12, 0), (13, 0), (11, 1), (13, 1), (11, 2), (11, 2), (12, 1), (13, 0), (11, 1), (11, 1),),
-    ((14, -1), (13, 0), (11, 2), (13, 1), (13, 1), (12, 1), (14, 0), (14, 1), (13, 0), (11, 1), (14, 0), (14, 0),
-     (11, 2), (13, 1), (14, 1), (14, 0), (14, 1), (13, 1), (13, 1), (13, 0), (13, 0), (11, 1), (13, 1), (14, 1),
-     (14, 0), (14, 0), (11, 1), (13, 0), (14, 1), (14, 1), (14, 0), (13, 1), (14, 1), (13, 0), (14, 0), (13, 0),
-     (14, 1), (14, 1),),
+    ((16, 2),),
+    ((16, 2),),
+    ((17, -1), (12, 1), (12, 1),),
+    ((16, 2), (16, 1), (16, 1),),
+    (),
+    ((17, 0), (17, 0), (17, 0), (17, 0), (17, 1), (16, 2), (16, 2),),
+    ((13, -1), (17, 2),),
+    ((12, 0),),
+    ((13, 0), (13, 1), (17, 2), (12, 1), (16, 1), (17, 2), (12, 0), (12, 0), (16, 2),),
+    ((17, 2),),
+    ((14, -1),),
+    ((13, 1), (17, 1),),
+    ((14, 0), (17, 2), (14, 1),),
+    ((13, 0), (12, 1), (12, 1), (16, 1), (16, 1),),
+    (),
+    ((15, -1), (16, 2), (16, 2), (12, 0), (13, 1), (17, 2), (17, 1), (15, 0), (14, 0), (15, 1), (12, 1), (16, 2),
+     (12, 0), (17, 2), (13, 1), (17, 1), (14, 1), (13, 0), (16, 1), (12, 1), (14, 0), (16, 2), (15, 0), (17, 2),
+     (14, 1), (13, 0), (16, 1), (17, 2), (14, 0), (15, 1), (13, 0), (14, 1), (15, 0), (16, 1), (15, 1), (14, 1),
+     (15, 0), (15, 1), (15, 1),),
 )
 
 
@@ -486,6 +563,11 @@
 
 
 def loop(n, body):
+    if n <= UNROLLED:
+        for i in range(n):
+            body(i)
+        return
+
     def step(i, carry):
         body(i)
         return carry
@@ -493,13 +575,28 @@
     lax.fori_loop(0, n, step, 0)
 
 
+def mult(v, n):
+    return v if isinstance(v, int) else pl.multiple_of(v, n)
+
+
 def ds(i, n):
-    return pl.ds(pl.multiple_of(i * n, n), n)
-
-
+    return pl.ds(mult(i * n, n), n)
+
+
+UNROLLED = 3
 T = 256
 SCALE = HEAD_DIM ** (-0.5)
-O_AT, UP_AT, N1_AT, N2_AT = 2560, 3328, 2304, 2432
+O_AT, N1_AT, N2_AT = 4096, 1152, 2432
+
+
+def set_at(half, s):
+    return 1280 * half + 384 * s
+
+
+def up_at(i):
+    return 2560 + 768 * i + (768 if i > 1 else 0)
+
+
 ROW = 64
 
 
@@ -525,16 +622,18 @@
         n = len(reduce_shapes(g))
         bufs[g], scratch = scratch[:n], scratch[n:]
     (
-        wide, down, gwide, gdown, stage, final, final_down,
+        wide, down, gwide, gdown, final,
         mask, xhat, rstd1, xhat2, rstd2, n1, n1t, n2, qkv, mixed, probs, hidden,
-        act, slope, acc_out, acc_in, dqkv, rows1, rows2, send, recv,
+        act, slope, acc_in, dqkv, rows1, rows2, send, recv,
     ) = scratch
+    stage = gwide.at[0, :, pl.ds(0, 16)]
+    acc_out = ig_ref
     place = me = Place()
     greet(place)
     wire = Wire(place, send, recv)
     openers = {g: lambda g=g: gather_streams(wire, wide, down, g) for g in range(3)}
     openers.update({5 + g: lambda g=g: [gather_front(wire, wd_ref, stage, wide, down, g)] for g in range(3)})
-    finals = final, final_down
+    finals = final, dd_ref
     openers.update({10 + g: lambda g=g: reduce_streams(wire, gwide, gdown, bufs[g], finals, g) for g in REDUCED})
     conductor = Conductor(openers)
     serve = conductor.serve
@@ -542,10 +641,10 @@
 
     zero4 = lambda n: jnp.zeros((4, n), F32)
 
-    def put_own(ref, at):
-        n = ref.shape[1]
-        rows = jnp.concatenate([ref[...].astype(F32), zero4(n)], axis=0)
-        stage[mine, :, pl.ds(at, n)] = rows.astype(BF)
+    def put_own(ref, width, place_of):
+        for i in range(ref.shape[1] // width):
+            rows = jnp.concatenate([ref[:, pl.ds(width * i, width)].astype(F32), zero4(width)], axis=0)
+            stage[mine, :, pl.ds(place_of(i), width)] = rows.astype(BF)
 
     def put_norm(gain, shift, at):
         eye = lax.broadcasted_iota(jnp.int32, (16, 12), 0) == lax.broadcasted_iota(jnp.int32, (16, 12), 1)
@@ -555,13 +654,13 @@
         both = jnp.where(lane == 0, a, jnp.where(lane == 1, b, 0.0))
         stage[mine, :, pl.ds(at, 128)] = both.astype(BF)
 
-    for i, ref in enumerate((wq_ref, wk_ref, wv_ref)):
-        put_own(ref, 768 * i)
+    for k, ref in enumerate((wq_ref, wk_ref, wv_ref)):
+        put_own(ref, 128, lambda i: set_at(i // 3, i % 3) + 128 * k)
     put_norm(n1g_ref, n1b_ref, N1_AT)
     put_norm(n2g_ref, n2b_ref, N2_AT)
     serve()
-    put_own(wo_ref, O_AT)
-    put_own(wu_ref, UP_AT)
+    put_own(wo_ref, D, lambda i: O_AT)
+    put_own(wu_ref, D, up_at)
     serve()
 
     segs = jnp.broadcast_to(seg_ref[...], (T, T))
@@ -593,18 +692,15 @@
 
     loop(T // ROW, norm1_apply)
 
-    def project(i):
-        at = ds(i, 256)
-        w = wide[:, :, :, at].reshape(D, 256)
-        qkv[:, at] = dot(n1[...], w).astype(BF)
-
-    loop(9, project)
-    serve()
+    def project(half, s):
+        w = wide[:, :, :, pl.ds(mult(set_at(half, s), 128), 384)].reshape(D, 384)
+        qkv[:, pl.ds(mult(384 * (3 * half + s), 128), 384)] = dot(n1[...], w).astype(BF)
+
     lane = lax.broadcasted_iota(jnp.int32, (1, 128), 1)
     heads = [((lane >= 32 * h) & (lane < 32 * h + 32)).astype(F32).astype(BF) for h in range(4)]
 
-    def group(ref, which, t):
-        return ref[:, pl.ds(pl.multiple_of(768 * which + 128 * t, 128), 128)]
+    def group(ref, which, t, width=384):
+        return ref[:, pl.ds(mult(width * t + 128 * which, 128), 128)]
 
     def attend(t):
         q4, k4, v4 = [group(qkv, i, t) for i in range(3)]
@@ -618,11 +714,17 @@
                 p = (e * (1.0 / jnp.sum(e, axis=1, keepdims=True))).astype(BF)
                 probs[4 * t + h, rows, :nk] = p
                 total = total + dot(p, vh[h][:nk])
-            mixed[rows, pl.ds(pl.multiple_of(128 * t, 128), 128)] = total.astype(BF)
-
-    for part in range(3):
-        loop(2, lambda i: attend(2 * part + i))
+            mixed[rows, pl.ds(mult(128 * t, 128), 128)] = total.astype(BF)
+
+    for turn, s in enumerate((2, me.zl, 1 - me.zl)):
+        if turn:
+            serve()
+        for half in range(2):
+            project(half, s)
         serve()
+        for half in range(2):
+            attend(3 * half + s)
+            serve()
 
     n2t, mixt = [gwide.at[:, :, :, pl.ds(256 * k, 256)] for k in range(2)]
 
@@ -641,7 +743,7 @@
 
     def out_project(i):
         at = ds(i, 256)
-        w = wide[:, :, :, pl.ds(pl.multiple_of(O_AT + 256 * i, 128), 256)].reshape(D, 256)
+        w = wide[:, :, :, pl.ds(mult(O_AT + 256 * i, 128), 256)].reshape(D, 256)
         hidden[:, at] = x_ref[:, at].astype(F32) + dot(mixed[...], w)
 
     loop(3, out_project)
@@ -661,17 +763,18 @@
 
     def feed(i):
         def part(j):
-            at = pl.ds(pl.multiple_of(UP_AT + 768 * i + 256 * j, 128), 256)
+            at = pl.ds(up_at(i) + 256 * j, 256)
             v = dot(n2[...], wide[:, :, :, at].reshape(D, 256))
             sq = v * v
             th = jnp.tanh(c0 * v * (1.0 + 0.044715 * sq))
             half = 0.5 + 0.5 * th
             a = (v * half).astype(BF)
-            keep = pl.ds(pl.multiple_of(768 * i + 256 * j, 128), 256)
+            keep = pl.ds(mult(768 * i + 256 * j, 128), 256)
             act[:, keep] = a
             slope[:, keep] = half + 0.5 * v * (1.0 - th * th) * (c0 * (1.0 + 0.134145 * sq))
 
         loop(3, part)
+        serve()
         a = act[:, ds(i, 768)].T
 
         def grad(j):
@@ -694,12 +797,13 @@
         acc_out[...] += dot(act[:, at], wd)
         pg = (dot_nt(cot_ref[...], wd) * slope[:, at]).astype(BF)
         act[:, at] = pg
-        up_at = pl.ds(pl.multiple_of(UP_AT + 768 * i, 128), 768)
-        acc_in[...] += dot_nt(pg, wide[:, :, :, up_at].reshape(D, 768))
+        serve()
+        acc_in[...] += dot_nt(pg, weight(wide, up_at(i), D))
+        serve()
 
         def grad(j):
-            cols_j = pl.ds(pl.multiple_of(UP_AT + 768 * i + 256 * j, 128), 256)
-            pg_j = act[:, pl.ds(pl.multiple_of(768 * i + 256 * j, 128), 256)]
+            cols_j = pl.ds(up_at(i) + 256 * j, 256)
+            pg_j = act[:, pl.ds(mult(768 * i + 256 * j, 128), 256)]
             gwide[:, :, :, cols_j] = dot(n2t[...].reshape(D, T), pg_j).astype(BF).reshape(4, 4, 48, 256)
 
         loop(3, grad)
@@ -731,10 +835,12 @@
     as_columns(lax.fori_loop(0, T // ROW, norm2_back, (nothing, nothing)), N2_AT)
     n2[...] = hidden[...].astype(BF)
 
+    serve()
+
     def o_back(i):
         at = ds(i, 256)
         b = n2[:, at]
-        gwide[:, :, :, pl.ds(pl.multiple_of(O_AT + 256 * i, 128), 256)] = (
+        gwide[:, :, :, pl.ds(mult(O_AT + 256 * i, 128), 256)] = (
             dot(mixt[...].reshape(D, T), b).astype(BF).reshape(4, 4, 48, 256)
         )
 
@@ -746,7 +852,7 @@
 
     def attend_back(t):
         q4, k4, v4 = [group(qkv, i, t) for i in range(3)]
-        do4, o4 = group(mgrad, 0, t), group(mixed, 0, t)
+        do4, o4 = group(mgrad, 0, t, 128), group(mixed, 0, t, 128)
         q4t, do4t = q4.T, do4.T
         kh = [k4 * heads[h] for h in range(4)]
         dk, dv = [], []
@@ -765,26 +871,26 @@
                 dvh.append(dot(do4t[hrows, rows], p))
             for both, parts in ((dk, dkh), (dv, dvh)):
                 both.append(jnp.concatenate([parts[1][:, :128] + parts[0], parts[1][:, 128:]], axis=1))
-        at = pl.multiple_of(128 * t, 128)
+        at = 384 * t
         for rb in range(2):
             dqkv[pl.ds(128 * rb, 128), pl.ds(at, 128)] = (total[rb] * SCALE).astype(BF)
-        dqkv[:, pl.ds(at + 768, 128)] = (jnp.concatenate(dk, axis=0).T * SCALE).astype(BF)
-        dqkv[:, pl.ds(at + 1536, 128)] = jnp.concatenate(dv, axis=0).T.astype(BF)
-
-    for part in range(3):
-        loop(2, lambda i: attend_back(2 * part + i))
+        dqkv[:, pl.ds(at + 128, 128)] = (jnp.concatenate(dk, axis=0).T * SCALE).astype(BF)
+        dqkv[:, pl.ds(at + 256, 128)] = jnp.concatenate(dv, axis=0).T.astype(BF)
+
+    for s in range(3):
+        for half in range(2):
+            attend_back(3 * half + s)
+            serve()
+        for half in range(2):
+            part = dqkv[:, pl.ds(384 * (3 * half + s), 384)]
+            gwide[:, :, :, pl.ds(set_at(half, s), 384)] = dot(n1t[...], part).astype(BF).reshape(4, 4, 48, 384)
         serve()
-
-    def qkv_grad(i):
-        at = ds(i, 256)
-        gwide[:, :, :, at] = dot(n1t[...], dqkv[:, at]).astype(BF).reshape(4, 4, 48, 256)
-
-    loop(6, qkv_grad)
-    serve()
-    acc_in[...] = dot_nt(dqkv[:, :768], weight(wide, 0, D))
-    acc_in[...] += dot_nt(dqkv[:, 768:1536], weight(wide, 768, D))
-    acc_in[...] += dot_nt(dqkv[:, 1536:], weight(wide, 1536, D))
-    serve()
+        for half in range(2):
+            part = dqkv[:, pl.ds(384 * (3 * half + s), 384)]
+            grad = dot_nt(part, weight(wide, set_at(half, s), 384))
+            acc_in[...] = grad if s + half == 0 else acc_in[...] + grad
+        if s < 2:
+            serve()
 
     def norm1_back(i, sums):
         at = ds(i, ROW)
@@ -795,16 +901,17 @@
         return a + jnp.sum(grad * hat, axis=0, keepdims=True), b + jnp.sum(grad, axis=0, keepdims=True)
 
     as_columns(lax.fori_loop(0, T // ROW, norm1_back, (nothing, nothing)), N1_AT)
-    loop(3, lambda i: qkv_grad(6 + i))
     serve()
 
+    assert conductor.place == len(SCHEDULE)
     wire.drain()
 
-    dd_ref[...] = final_down[...]
-    for i, ref in enumerate((dq_ref, dk_ref, dv_ref)):
-        ref[...] = final[:12, 768 * i : 768 * i + 768]
-    do_ref[...] = final[:12, O_AT:UP_AT]
-    du_ref[...] = final[:12, UP_AT:]
+    for k, ref in enumerate((dq_ref, dk_ref, dv_ref)):
+        for i in range(6):
+            ref[:, pl.ds(128 * i, 128)] = final[:12, pl.ds(set_at(i // 3, i % 3) + 128 * k, 128)]
+    do_ref[...] = final[:12, pl.ds(O_AT, D)]
+    for i in range(4):
+        du_ref[:, pl.ds(768 * i, 768)] = final[:12, pl.ds(up_at(i), 768)]
     diag = lax.broadcasted_iota(jnp.int32, (16, 128), 0) == lax.broadcasted_iota(jnp.int32, (16, 128), 1)
     for at, refs in ((N1_AT, (dn1g_ref, dn1b_ref)), (N2_AT, (dn2g_ref, dn2b_ref))):
         for k, ref in enumerate(refs):
@@ -827,13 +934,13 @@
     vec, square = like((1, 12), F32), like((12, D), F32)
     scratch = [pltpu.VMEM(s, t) for g in REDUCED for s, t in reduce_shapes(g)]
     wide, down = pltpu.VMEM((4, 4, 48, WIDE), BF), pltpu.VMEM((4, 4, 2, 2, 48, D), BF)
-    scratch += [wide, down, wide, down, pltpu.VMEM((4, 16, WIDE), BF), pltpu.VMEM((16, WIDE), F32), pltpu.VMEM((48, D), F32)]
+    scratch += [wide, down, wide, down, pltpu.VMEM((16, WIDE), F32)]
     f32s, bfs = pltpu.VMEM((T, D), F32), pltpu.VMEM((T, D), BF)
     one, turned = pltpu.VMEM((T, 1), F32), pltpu.VMEM((D, T), BF)
     scratch += [pltpu.VMEM((T, T), F32), f32s, one, f32s, one]
     scratch += [bfs, turned, bfs, pltpu.VMEM((T, 3 * D), BF), bfs]
     scratch += [pltpu.VMEM((HEADS, T, T), BF), f32s]
-    scratch += [pltpu.VMEM((T, FF), BF), pltpu.VMEM((T, FF), F32), f32s, f32s]
+    scratch += [pltpu.VMEM((T, FF), BF), pltpu.VMEM((T, FF), F32), f32s]
     scratch += [pltpu.VMEM((T, 3 * D), BF), pltpu.VMEM((8, D), F32), pltpu.VMEM((8, D), F32)]
     scratch += [pltpu.SemaphoreType.DMA((N_SEND,)), pltpu.SemaphoreType.DMA((N_RECV,))]
     outs = pl.pallas_call(

time: 134 us -> 120 us (0.90)
  Pallas kernels: 133 us -> 119 us
    pallas_call x1, Pallas kernels: 130 us -> 117 us  [per_device(): pl.pallas_call(layer_kernel, out_shape=(like((T, D), BF), like((T, D), F3...]
where the time goes in v4:
time: 120 us
  Pallas kernels  119 us (99%)
    pallas_call x1, Pallas kernels, per_device(): pl.pallas_call(layer_kernel, out_shape=(like((T, D), BF), like((T, D), F3...  117 us
    pallas_call x1, Pallas kernels, per_device(): pl.pallas_call(publish_kernel, out_shape=tuple((like(o.shape, o.dtype) fo...  2.67 us

profile of v4, /device:TPU:1, one launch (start us, length us, event | category | flops | bytes accessed | tf_op | source)
XLA Modules:
  0.0 120.1 jit_solution(11289042611628716553)
XLA Ops:
  0.6 116.6 %layer.1 = (bf16[256,768]{1,0:T(8,128)(2,1)}, f32[256,768]{1,0:T(8,128)}, f32[1,12]{1,0:T(1,128)}, f32[1,12]{1,0:T(1,128)}, f32[12,768]{1,0:T(8,128)}, /*index=5...) custom-call(bf16[256,768]{1,0:T(8,128)(2,1)} %x_ref.1, ...), custom_call_target="tpu_custom_call" | custom-call | flops 12999999488 | bytes 6000000 | tf_op jit(solution)/shard_map/layer/pallas_call | solution.py:946
  117.3 2.7 %publish.1 = (bf16[256,768]{1,0:T(8,128)(2,1)}, f32[256,768]{1,0:T(8,128)}, f32[1,12]{1,0:T(1,128)}, f32[1,12]{1,0:T(1,128)}, f32[12,768]{1,0:T(8,128)}, /*index...) custom-call(bf16[256,768]{1,0:T(8,128)(2,1)} %get-tuple-element.36.r, ...), custom_call_target="tpu_custom_call" | custom-call | tf_op jit(solution)/shard_map/publish/pallas_call | solution.py:961

commit v5 on v4

--- a/solution.py
+++ b/solution.py
@@ -16,19 +16,21 @@
 MESH = pl.DeviceIdType.MESH
 
 WIDE = 6400
-DOWN = 2
-START = (0, 2560, 0, 0, 384, 768, 2560, 4096)
-HALF = (1280, 1920, 0, 1280, 1280, 1280, 768, 1152)
-WIDTH = (1280, 1920, 768, 384, 384, 512, 768, 1152)
+DOWN = 2, 4
+START = (0, 2560, 0, 0, 0, 768, 2560, 4096)
+HALF = (1280, 1920, 0, 1280, 0, 1280, 768, 1152)
+WIDTH = (1280, 1920, 768, 768, 768, 512, 768, 1152)
 P_AT = (768, 0, 0, 0, 0, 0, 0, 0)
-Q_AT = (0, 384, 384, 256, 128, 256, 256, 384)
-SIZE = ((512, 384), (384, 768), (384, 384), (256, 128), (128, 256), (256, 256), (256, 256), (384, 384))
-LOW = ((256, 256), (128, 384), (128, 256), (128, 128), (128, 128), (128, 128), (128, 128), (128, 256))
-ZED = (True, True, False, False, False, False, True, True)
+Q_AT = (0, 384, 384, 256, 384, 256, 384, 384)
+SIZE = ((512, 384), (384, 768), (384, 384), (256, 256), (384, 384), (256, 256), (384, 384), (384, 384))
+LOW = ((256, 256), (128, 384), (128, 256), (128, 128), (128, 256), (128, 128), (128, 256), (128, 256))
+ZED = (True, True, False, True, False, False, False, True)
 STRAIGHT = (False, False, False)
-DIRECT = (False, False, False, True, True, True, False, True)
+SPLIT = (False, False, False, False, False, False, False, False)
+FINE = (0, 0, 0)
+DIRECT = (False, False, False, False, False, True, False, False)
 P_, QM, QO = 0, 1, 2
-N_RECV = 332
+N_RECV = 335
 N_SEND = 40
 VMEM_BYTES = 66700000
 
@@ -100,11 +102,11 @@
         self.open = {}
 
 
-def greet(place):
+def call_out(place):
     barrier = pltpu.get_barrier_semaphore()
     for peer in place.peers:
         pl.semaphore_signal(barrier, inc=1, device_id=peer, device_id_type=MESH)
-    pl.semaphore_wait(barrier, len(place.peers))
+    return barrier
 
 
 def kind(k):
@@ -132,7 +134,7 @@
     def ref(self, bu, bw, h=None, core=0):
         bx, by = (bu, bw) if self.k == P_ else (bw, bu)
         at = columns_of(self.g, self.k, self.me, h, core)
-        if self.g != DOWN:
+        if self.g not in DOWN:
             return self.wide.at[bx, by, :, at]
         return self.down.at[bx, by, :, 1 - self.me.c if core else self.me.c, :, at]
 
@@ -189,6 +191,20 @@
         yield from wait(a, b)
         spread(2)
         share("at", 2, 0)
+        if FINE[g] == 2 or (FINE[g] == 1 and k == QM):
+            far = []
+            for du in (0, -1, 1, 2):
+                yield from wait(out[1, du])
+                a = go(s.at(du, -1, 0), s.second[1])
+                share("at", du, -1)
+                yield from wait(out[-1, du])
+                b = go(s.at(du, 1, 1), s.second[-1])
+                share("at", du, 1)
+                far.append((a, b))
+            for du, copies in zip((0, -1, 1, 2), far):
+                yield from wait(*copies)
+                share("at", du, 2)
+            return
         yield from wait(*[out[1, du] for du in (0, -1, 1, 2)])
         a = go(s.across(-1, 0), s.second[1])
         share("across", -1)
@@ -215,7 +231,7 @@
 def gather_cross(wire, wide, down, g, sib, zs):
     me = wire.place
     theirs = Piece(me, wide, down, g, QO)
-    for n in range(6):
+    for n in range(15 if FINE[g] else 6):
         yield lambda: zs[n][0] if len(zs) > n else None
         copies, name, where = zs[n]
         for copy in copies:
@@ -233,9 +249,10 @@
 def gather_streams(wire, wide, down, g):
     sib, zs = {P_: [], QM: [], QO: []}, []
     streams = [gather_plane(wire, wide, down, g, k, sib[k], zs) for k in (P_, QM)]
-    streams += [gather_end(6, sib[k]) for k in (P_, QM)]
+    fine = {P_: FINE[g] == 2, QM: FINE[g] > 0}
+    streams += [gather_end(15 if fine[k] else 6, sib[k]) for k in (P_, QM)]
     if ZED[g]:
-        streams += [gather_cross(wire, wide, down, g, sib[QO], zs), gather_end(6, sib[QO])]
+        streams += [gather_cross(wire, wide, down, g, sib[QO], zs), gather_end(15 if FINE[g] else 6, sib[QO])]
     return streams
 
 
@@ -254,7 +271,7 @@
 def gather_front(wire, own_down, stage, wide, down, g):
     me = wire.place
     mine = 2 * me.zl + me.c
-    if g != DOWN:
+    if g not in DOWN:
         at = pl.ds(START[g], 2 * HALF[g])
         src = dst = stage.at[mine, :, at]
         hers = stage.at[2 * (1 - me.zl) + me.c, :, at]
@@ -267,15 +284,15 @@
     yield from wait(a)
     c = wire.put(hers, hers, me.sibling)
     yield from wait(b, c)
-    if g != DOWN:
+    if g not in DOWN:
         join(stage, wide, me, g)
 
 
 def rows_of(g):
-    return (2, 48) if g == DOWN else (48,)
-
-
-REDUCED = (2, 3, 4, 5, 6, 7)
+    return (2, 48) if g in DOWN else (48,)
+
+
+REDUCED = (3, 4, 5, 6, 7)
 
 
 def reduce_shapes(g):
@@ -285,13 +302,13 @@
         high = n - low
         if DIRECT[g]:
             low, high = n, 128
-        own = (48,) if g == DOWN else (2, 16)
+        own = (48,) if g in DOWN else (2, 16)
         shapes += [(4, 4, *rows, n), (4, *rows, low), (4, *rows, high), (4, *rows, n), (4, *rows, n)]
         shapes += [(*rows, low), (*rows, high), (*rows, n), (*rows, n), (2, *own, n), (*own, n), (*own, n), (*own, n)]
     if ZED[g]:
         shapes += [(4, 4, *rows, SIZE[g][1])] * 2
     shapes = [(s, BF) for s in shapes]
-    return shapes if g == DOWN else shapes + [((16, WIDTH[g]), F32)]
+    return shapes if g in DOWN else shapes + [((16, WIDTH[g]), F32)]
 
 
 def add_blocks(dst, src):
@@ -320,7 +337,7 @@
     total = ref[...].astype(F32)
     for other in others:
         total = total + other[...].astype(F32)
-    if g != DOWN:
+    if g not in DOWN:
         zero = jnp.zeros((4, total.shape[1]), F32)
         for o in range(4):
             st[o // 2, o % 2] = jnp.concatenate([total[12 * o : 12 * o + 12], zero], axis=0).astype(BF)
@@ -331,7 +348,7 @@
 def add_planes(me, g, k, st, rzp, rzm, rr, final, final_down, so):
     def total_of(core):
         def pick(ref):
-            return (ref[...] if g == DOWN else ref[core]).astype(F32)
+            return (ref[...] if g in DOWN else ref[core]).astype(F32)
 
         first = pick(st.at[me.zl]) + pick(rr)
         second = pick(rzp) + pick(rzm)
@@ -339,10 +356,10 @@
             return (QM, first), (QO, second)
         return ((k, first + second),)
 
-    out = final_down if g == DOWN else final
+    out = final_down if g in DOWN else final
     for kk, v in total_of(me.c):
         out[:, columns_of(g, kk, me)] = v
-    if g != DOWN:
+    if g not in DOWN:
         for kk, v in total_of(1 - me.c):
             base = me.starts[g, kk, 0] - me.starts[g, None, 0]
             so[:, pl.ds(pl.multiple_of(base, 128), v.shape[1])] = v
@@ -371,26 +388,29 @@
                 copy.wait_recv()
             add_along(du, bufs[27])
         else:
+            if len(got) > 1:
+                yield from wait(got[du])
             add_along(du, sb)
 
-    yield from wait(got)
+    if crosses or len(got) == 1:
+        yield from wait(*got.values())
     if crosses:
         for du in (2, 1, -1, 0):
             add_along(du, sb)
     if DIRECT[g]:
-        got = []
+        near = []
         for du, buf in ((2, b1p), (1, b2p), (-1, b2m)):
             yield from ready(du)
-            got.append(wire.put(s.along(du), buf, s.first[du]))
+            near.append(wire.put(s.along(du), buf, s.first[du]))
         yield from ready(0)
-        yield from wait(*got)
-        got = []
+        yield from wait(*near)
+        near = []
         for dw, buf in ((2, c1p), (1, c2p), (-1, c2m), (0, None)):
             bw = s.ws[dw]
             add_three(s.at(0, dw), b1p.at[bw], b2p.at[bw], b2m.at[bw])
             if dw:
-                got.append(wire.put(s.at(0, dw), buf, s.second[dw]))
-        yield from wait(*got)
+                near.append(wire.put(s.at(0, dw), buf, s.second[dw]))
+        yield from wait(*near)
         owners_rows(st, s.at(0, 0), (c1p, c2p, c2m), g)
         yield from over_planes(wire, me, g, k, bufs, st, rzp, rzm, rr, finals, done)
         return
@@ -437,9 +457,9 @@
     b = wire.put(st.at[1 - me.zl], rzm, me.below)
     c = wire.put(st.at[me.zl], rr, me.other)
     yield from wait(a, b, c)
-    add_planes(me, g, k, st, rzp, rzm, rr, *finals, None if g == DOWN else bufs[-1])
+    add_planes(me, g, k, st, rzp, rzm, rr, *finals, None if g in DOWN else bufs[-1])
     done.append(k)
-    if g != DOWN and len(done) == 2:
+    if g not in DOWN and len(done) == 2:
         at = pl.ds(pl.multiple_of(me.starts[g, None, 0], 128), WIDTH[g])
         yield from wait(wire.put(bufs[-1], finals[0].at[:, at], me.sibling))
 
@@ -467,7 +487,15 @@
         got = wire.put(pieces[QO].of_sibling(), bufs[26], me.sibling)
         streams.append(reduce_cross(wire, wide, down, bufs, got, z_in, g))
     for k in (P_, QM):
-        got = wire.put(pieces[k].of_sibling(), bufs[13 * k], me.sibling)
+        s, sb = pieces[k], bufs[13 * k]
+        if SPLIT[g]:
+            got = {}
+            for du in (2, 1, -1, 0):
+                bu = s.us[du]
+                dst = sb.at[bu] if k == P_ else sb.at[:, bu]
+                got[du] = wire.put(s.ref(s.us[du], slice(None), core=1), dst, me.sibling)
+        else:
+            got = {0: wire.put(s.of_sibling(), sb, me.sibling)}
         streams.append(reduce_plane(wire, wide, down, bufs, got, z_in, done, finals, g, k))
     return streams
 
@@ -520,37 +548,38 @@
     (),
     (),
     ((2, 2),),
-    ((12, -1), (2, 3),),
-    (),
-    (),
-    (),
-    (),
-    (),
-    ((16, -1), (12, 0),),
-    (),
-    ((12, 1), (16, 0), (16, 0), (16, 0), (16, 0),),
-    ((16, 1), (12, 0), (16, 2),),
-    ((16, 2),),
-    ((12, 0),),
-    ((16, 2),),
-    ((16, 2),),
-    ((17, -1), (12, 1), (12, 1),),
-    ((16, 2), (16, 1), (16, 1),),
-    (),
-    ((17, 0), (17, 0), (17, 0), (17, 0), (17, 1), (16, 2), (16, 2),),
-    ((13, -1), (17, 2),),
-    ((12, 0),),
-    ((13, 0), (13, 1), (17, 2), (12, 1), (16, 1), (17, 2), (12, 0), (12, 0), (16, 2),),
+    ((14, -1), (2, 3),),
+    (),
+    (),
+    (),
+    (),
+    (),
+    ((16, -1), (14, 0),),
+    (),
+    ((14, 1),),
+    ((16, 0),),
+    ((14, 0), (16, 1),),
+    (),
+    ((14, 0),),
+    (),
+    ((17, -1),),
+    ((14, 1), (14, 1),),
+    ((16, 0),),
+    ((17, 0), (17, 0), (17, 0), (17, 0), (17, 1), (16, 0), (16, 1), (16, 1),),
     ((17, 2),),
-    ((14, -1),),
-    ((13, 1), (17, 1),),
-    ((14, 0), (17, 2), (14, 1),),
-    ((13, 0), (12, 1), (12, 1), (16, 1), (16, 1),),
-    (),
-    ((15, -1), (16, 2), (16, 2), (12, 0), (13, 1), (17, 2), (17, 1), (15, 0), (14, 0), (15, 1), (12, 1), (16, 2),
-     (12, 0), (17, 2), (13, 1), (17, 1), (14, 1), (13, 0), (16, 1), (12, 1), (14, 0), (16, 2), (15, 0), (17, 2),
-     (14, 1), (13, 0), (16, 1), (17, 2), (14, 0), (15, 1), (13, 0), (14, 1), (15, 0), (16, 1), (15, 1), (14, 1),
-     (15, 0), (15, 1), (15, 1),),
+    (),
+    ((17, 2), (17, 1), (14, 0),),
+    ((17, 1), (17, 2), (14, 1),),
+    ((13, -1),),
+    (),
+    ((17, 2), (16, 0), (14, 1), (13, 0), (13, 0), (13, 0), (13, 0), (17, 2), (17, 2), (17, 2), (13, 1), (14, 0),
+     (14, 0), (16, 1), (13, 2), (17, 1), (14, 1),),
+    ((13, 1), (13, 1), (13, 2), (13, 2), (16, 0), (16, 0),),
+    (),
+    ((15, -1), (13, 2), (13, 2), (17, 2), (17, 1), (17, 1), (14, 0), (14, 1), (13, 1), (16, 1), (16, 1), (13, 2),
+     (13, 2), (15, 0), (17, 2), (17, 2), (15, 1), (16, 0), (13, 1), (17, 1), (13, 1), (16, 1), (14, 0), (13, 2),
+     (14, 1), (16, 0), (15, 0), (17, 1), (17, 2), (13, 2), (13, 2), (16, 1), (15, 1), (13, 1), (15, 0), (13, 2),
+     (16, 1), (17, 2), (15, 1), (13, 1), (15, 0), (17, 2), (13, 2), (15, 1), (13, 2), (15, 1),),
 )
 
 
@@ -613,8 +642,8 @@
 
 
 def layer_kernel(
-    x_ref, seg_ref, n1g_ref, n1b_ref, wq_ref, wk_ref, wv_ref, wo_ref, n2g_ref, n2b_ref, wu_ref, wd_ref, cot_ref,
-    out_ref, ig_ref, dn1g_ref, dn1b_ref, dq_ref, dk_ref, dv_ref, do_ref, dn2g_ref, dn2b_ref, du_ref, dd_ref,
+    x_hbm, seg_ref, n1g_ref, n1b_ref, wq_ref, wk_ref, wv_ref, wo_ref, n2g_ref, n2b_ref, wu_ref, wd_ref, cot_hbm,
+    out_hbm, ig_hbm, dn1g_ref, dn1b_ref, dq_ref, dk_ref, dv_ref, do_ref, dn2g_ref, dn2b_ref, du_ref, dd_ref,
     *scratch,
 ):
     bufs = {}
@@ -624,12 +653,16 @@
     (
         wide, down, gwide, gdown, final,
         mask, xhat, rstd1, xhat2, rstd2, n1, n1t, n2, qkv, mixed, probs, hidden,
-        act, slope, acc_in, dqkv, rows1, rows2, send, recv,
+        act, slope, acc_in, dqkv, rows1, rows2, x_ref, cot_ref, out_ref, ig_ref, io, send, recv,
     ) = scratch
     stage = gwide.at[0, :, pl.ds(0, 16)]
     acc_out = ig_ref
     place = me = Place()
-    greet(place)
+    x_in = pltpu.make_async_copy(x_hbm, x_ref, io.at[0])
+    cot_in = pltpu.make_async_copy(cot_hbm, cot_ref, io.at[1])
+    x_in.start()
+    cot_in.start()
+    barrier = call_out(place)
     wire = Wire(place, send, recv)
     openers = {g: lambda g=g: gather_streams(wire, wide, down, g) for g in range(3)}
     openers.update({5 + g: lambda g=g: [gather_front(wire, wd_ref, stage, wide, down, g)] for g in range(3)})
@@ -658,6 +691,7 @@
         put_own(ref, 128, lambda i: set_at(i // 3, i % 3) + 128 * k)
     put_norm(n1g_ref, n1b_ref, N1_AT)
     put_norm(n2g_ref, n2b_ref, N2_AT)
+    pl.semaphore_wait(barrier, len(place.peers))
     serve()
     put_own(wo_ref, D, lambda i: O_AT)
     put_own(wu_ref, D, up_at)
@@ -677,6 +711,7 @@
         xhat[at, :] = hat
         rstd1[at, :] = rstd
 
+    x_in.wait()
     loop(T // ROW, norm1_rows)
     serve()
 
@@ -759,6 +794,7 @@
     transpose(n2, n2t)
     serve()
 
+    cot_in.wait()
     c0 = (2.0 / 3.141592653589793) ** 0.5
 
     def feed(i):
@@ -812,6 +848,8 @@
         feed_back(i)
         serve()
     out_ref[...] = acc_out[...].astype(BF)
+    out_copy = pltpu.make_async_copy(out_ref, out_hbm, io.at[2])
+    out_copy.start()
 
     def norm_back(grad, hat, rstd, gain, at):
         gn = gain * grad
@@ -901,9 +939,13 @@
         return a + jnp.sum(grad * hat, axis=0, keepdims=True), b + jnp.sum(grad, axis=0, keepdims=True)
 
     as_columns(lax.fori_loop(0, T // ROW, norm1_back, (nothing, nothing)), N1_AT)
+    ig_copy = pltpu.make_async_copy(ig_ref, ig_hbm, io.at[3])
+    ig_copy.start()
     serve()
 
     assert conductor.place == len(SCHEDULE)
+    out_copy.wait()
+    ig_copy.wait()
     wire.drain()
 
     for k, ref in enumerate((dq_ref, dk_ref, dv_ref)):
@@ -926,6 +968,7 @@
 
 
 VM = pl.BlockSpec(memory_space=pltpu.VMEM)
+ANY = pl.BlockSpec(memory_space=pl.ANY)
 
 
 def per_device(*args):
@@ -942,6 +985,7 @@
     scratch += [pltpu.VMEM((HEADS, T, T), BF), f32s]
     scratch += [pltpu.VMEM((T, FF), BF), pltpu.VMEM((T, FF), F32), f32s]
     scratch += [pltpu.VMEM((T, 3 * D), BF), pltpu.VMEM((8, D), F32), pltpu.VMEM((8, D), F32)]
+    scratch += [bfs, bfs, bfs, f32s, pltpu.SemaphoreType.DMA((4,))]
     scratch += [pltpu.SemaphoreType.DMA((N_SEND,)), pltpu.SemaphoreType.DMA((N_RECV,))]
     outs = pl.pallas_call(
         layer_kernel,
@@ -949,8 +993,8 @@
             like((T, D), BF), like((T, D), F32), vec, vec, square, square, square, square, vec, vec,
             like((12, FF), F32), like((48, D), F32),
         ),
-        in_specs=[VM] * 13,
-        out_specs=(VM,) * 12,
+        in_specs=[ANY] + [VM] * 11 + [ANY],
+        out_specs=(ANY, ANY) + (VM,) * 10,
         scratch_shapes=scratch,
         compiler_params=pltpu.CompilerParams(
             collective_id=0, has_side_effects=True, vmem_limit_bytes=VMEM_BYTES

time: 120 us -> 119 us (level)
    pallas_call x1, Pallas kernels: 117 us -> 115 us  [per_device(): pl.pallas_call(layer_kernel, out_shape=(like((T, D), BF), like((T, D), F3...]
where the time goes in v5:
time: 119 us
  Pallas kernels  118 us (99%)
    pallas_call x1, Pallas kernels, per_device(): pl.pallas_call(layer_kernel, out_shape=(like((T, D), BF), like((T, D), F3...  115 us
    pallas_call x1, Pallas kernels, per_device(): pl.pallas_call(publish_kernel, out_shape=tuple((like(o.shape, o.dtype) fo...  2.67 us

profile of v5, /device:TPU:1, one launch (start us, length us, event | category | flops | bytes accessed | tf_op | source)
XLA Modules:
  0.0 118.5 jit_solution(12943217137040327424)
XLA Ops:
  0.6 115.1 %layer.1 = (bf16[256,768]{1,0:T(8,128)(2,1)}, f32[256,768]{1,0:T(8,128)}, f32[1,12]{1,0:T(1,128)}, f32[1,12]{1,0:T(1,128)}, f32[12,768]{1,0:T(8,128)}, /*index=5...) custom-call(bf16[256,768]{1,0:T(8,128)(2,1)} %x_hbm.1, ...), custom_call_target="tpu_custom_call" | custom-call | flops 12999999488 | bytes 6000000 | tf_op jit(solution)/shard_map/layer/pallas_call | solution.py:990
  115.7 2.7 %publish.1 = (bf16[256,768]{1,0:T(8,128)(2,1)}, f32[256,768]{1,0:T(8,128)}, f32[1,12]{1,0:T(1,128)}, f32[1,12]{1,0:T(1,128)}, f32[12,768]{1,0:T(8,128)}, /*index...) custom-call(bf16[256,768]{1,0:T(8,128)(2,1)} %get-tuple-element.36.r, ...), custom_call_target="tpu_custom_call" | custom-call | tf_op jit(solution)/shard_map/publish/pallas_call | solution.py:1005

commit v6 on v5

--- a/solution.py
+++ b/solution.py
@@ -21,16 +21,16 @@
 HALF = (1280, 1920, 0, 1280, 0, 1280, 768, 1152)
 WIDTH = (1280, 1920, 768, 768, 768, 512, 768, 1152)
 P_AT = (768, 0, 0, 0, 0, 0, 0, 0)
-Q_AT = (0, 384, 384, 256, 384, 256, 384, 384)
-SIZE = ((512, 384), (384, 768), (384, 384), (256, 256), (384, 384), (256, 256), (384, 384), (384, 384))
-LOW = ((256, 256), (128, 384), (128, 256), (128, 128), (128, 256), (128, 128), (128, 256), (128, 256))
-ZED = (True, True, False, True, False, False, False, True)
+Q_AT = (0, 384, 384, 256, 256, 256, 384, 640)
+SIZE = ((512, 384), (384, 768), (384, 384), (256, 256), (256, 256), (256, 256), (384, 384), (640, 512))
+LOW = ((256, 256), (128, 384), (128, 256), (128, 128), (128, 128), (128, 128), (128, 256), (256, 256))
+ZED = (True, True, False, True, True, False, False, False)
 STRAIGHT = (False, False, False)
 SPLIT = (False, False, False, False, False, False, False, False)
 FINE = (0, 0, 0)
-DIRECT = (False, False, False, False, False, True, False, False)
+DIRECT = (False, False, False, False, False, True, True, False)
 P_, QM, QO = 0, 1, 2
-N_RECV = 335
+N_RECV = 323
 N_SEND = 40
 VMEM_BYTES = 66700000
 
@@ -552,34 +552,34 @@
     (),
     (),
     (),
-    (),
-    (),
-    ((16, -1), (14, 0),),
+    ((14, 0), (14, 0), (14, 0), (14, 0),),
+    (),
+    ((16, -1), (14, 1),),
+    ((14, 2),),
+    ((14, 2),),
+    ((16, 0),),
+    ((16, 1), (14, 1), (14, 1), (14, 2),),
+    (),
+    ((14, 2),),
+    (),
+    ((17, -1),),
+    (),
+    ((14, 2), (14, 2), (14, 2),),
+    (),
+    ((17, 0), (16, 0), (16, 1), (17, 1),),
     (),
     ((14, 1),),
-    ((16, 0),),
-    ((14, 0), (16, 1),),
-    (),
-    ((14, 0),),
-    (),
-    ((17, -1),),
-    ((14, 1), (14, 1),),
-    ((16, 0),),
-    ((17, 0), (17, 0), (17, 0), (17, 0), (17, 1), (16, 0), (16, 1), (16, 1),),
-    ((17, 2),),
-    (),
-    ((17, 2), (17, 1), (14, 0),),
-    ((17, 1), (17, 2), (14, 1),),
-    ((13, -1),),
-    (),
-    ((17, 2), (16, 0), (14, 1), (13, 0), (13, 0), (13, 0), (13, 0), (17, 2), (17, 2), (17, 2), (13, 1), (14, 0),
-     (14, 0), (16, 1), (13, 2), (17, 1), (14, 1),),
-    ((13, 1), (13, 1), (13, 2), (13, 2), (16, 0), (16, 0),),
-    (),
-    ((15, -1), (13, 2), (13, 2), (17, 2), (17, 1), (17, 1), (14, 0), (14, 1), (13, 1), (16, 1), (16, 1), (13, 2),
-     (13, 2), (15, 0), (17, 2), (17, 2), (15, 1), (16, 0), (13, 1), (17, 1), (13, 1), (16, 1), (14, 0), (13, 2),
-     (14, 1), (16, 0), (15, 0), (17, 1), (17, 2), (13, 2), (13, 2), (16, 1), (15, 1), (13, 1), (15, 0), (13, 2),
-     (16, 1), (17, 2), (15, 1), (13, 1), (15, 0), (17, 2), (13, 2), (15, 1), (13, 2), (15, 1),),
+    ((17, 0), (17, 0), (14, 2),),
+    ((13, -1), (16, 0),),
+    (),
+    ((17, 1), (17, 1),),
+    ((13, 0), (13, 0), (13, 0), (13, 0), (13, 1), (13, 2), (16, 0), (16, 1), (17, 0), (14, 1), (14, 1), (14, 2),
+     (14, 2),),
+    ((13, 2),),
+    ((15, -1), (13, 1), (13, 1), (13, 2), (17, 0), (17, 0), (17, 1), (13, 2), (14, 2), (14, 1), (13, 2), (13, 2),
+     (13, 2), (15, 0), (13, 1), (15, 1), (17, 1), (17, 1), (16, 1), (17, 0), (14, 2), (13, 2), (13, 1), (13, 1),
+     (14, 1), (16, 1), (17, 0), (15, 0), (17, 1), (13, 2), (13, 2), (15, 1), (13, 1), (13, 2), (15, 0), (15, 1),
+     (17, 1), (13, 1), (13, 2), (17, 1), (15, 0), (15, 1), (13, 2), (15, 1),),
 )
 
 
@@ -962,9 +962,17 @@
 
 
 def publish_kernel(*refs):
-    n = len(refs) // 2
-    for i in range(n):
-        refs[n + i][...] = refs[i][...]
+    n = len(refs) // 3
+    sems = refs[-1]
+    ins = [pltpu.make_async_copy(refs[i], refs[2 * n + i], sems.at[i]) for i in range(n)]
+    outs = [pltpu.make_async_copy(refs[2 * n + i], refs[n + i], sems.at[n + i]) for i in range(n)]
+    for copy in ins:
+        copy.start()
+    for come, go in zip(ins, outs):
+        come.wait()
+        go.start()
+    for copy in outs:
+        copy.wait()
 
 
 VM = pl.BlockSpec(memory_space=pltpu.VMEM)
@@ -1005,8 +1013,9 @@
     outs = pl.pallas_call(
         publish_kernel,
         out_shape=tuple(like(o.shape, o.dtype) for o in outs),
-        in_specs=[VM] * 12,
-        out_specs=(VM,) * 12,
+        in_specs=[ANY] * 12,
+        out_specs=(ANY,) * 12,
+        scratch_shapes=[*[pltpu.VMEM(o.shape, o.dtype) for o in outs], pltpu.SemaphoreType.DMA((24,))],
         name="publish",
     )(*outs)
     return tuple(o.reshape(12) if o.shape == (1, 12) else o for o in outs)

time: 119 us -> 118 us (level)
  no operation moved by 1% of the time
where the time goes in v6:
time: 118 us
  Pallas kernels  117 us (99%)
    pallas_call x1, Pallas kernels, per_device(): pl.pallas_call(layer_kernel, out_shape=(like((T, D), BF), like((T, D), F3...  114 us
    pallas_call x1, Pallas kernels, per_device(): pl.pallas_call(publish_kernel, out_shape=tuple((like(o.shape, o.dtype) fo...  2.54 us

profile of v6, /device:TPU:1, one launch (start us, length us, event | category | flops | bytes accessed | tf_op | source)
XLA Modules:
  0.0 117.6 jit_solution(1822871187926215670)
XLA Ops:
  0.6 114.2 %layer.1 = (bf16[256,768]{1,0:T(8,128)(2,1)}, f32[256,768]{1,0:T(8,128)}, f32[1,12]{1,0:T(1,128)}, f32[1,12]{1,0:T(1,128)}, f32[12,768]{1,0:T(8,128)}, /*index=5...) custom-call(bf16[256,768]{1,0:T(8,128)(2,1)} %x_hbm.1, ...), custom_call_target="tpu_custom_call" | custom-call | flops 12999999488 | bytes 6000000 | tf_op jit(solution)/shard_map/layer/pallas_call | solution.py:998
  114.8 2.5 %publish.1 = (bf16[256,768]{1,0:T(8,128)(2,1)}, f32[256,768]{1,0:T(8,128)}, f32[1,12]{1,0:T(1,128)}, f32[1,12]{1,0:T(1,128)}, f32[12,768]{1,0:T(8,128)}, /*index...) custom-call(bf16[256,768]{1,0:T(8,128)(2,1)} %get-tuple-element.36.r, ...), custom_call_target="tpu_custom_call" | custom-call | tf_op jit(solution)/shard_map/publish/pallas_call | solution.py:1013

commit v7 on v6

--- a/solution.py
+++ b/solution.py
@@ -30,7 +30,7 @@
 FINE = (0, 0, 0)
 DIRECT = (False, False, False, False, False, True, True, False)
 P_, QM, QO = 0, 1, 2
-N_RECV = 323
+N_RECV = 256
 N_SEND = 40
 VMEM_BYTES = 66700000
 
@@ -72,6 +72,7 @@
         self.place, self.send_sem, self.recv_sem = place, send, recv
         self.n = self.m = 0
         self.open = {}
+        self.key, self.spare = None, []
 
     def slot(self):
         k = self.m % N_SEND
@@ -82,18 +83,24 @@
 
     def put(self, src, dst, to):
         k = self.slot()
-        assert self.n < N_RECV
+        if self.key in (13, 15, 17) and self.spare:
+            at = self.spare.pop(0)
+        else:
+            at = self.n
+            self.n += 1
+            if self.key in (0, 5, 6, 7):
+                self.spare.append(at)
+        assert at < N_RECV
         copy = pltpu.make_async_remote_copy(
             src_ref=src,
             dst_ref=dst,
             send_sem=self.send_sem.at[k],
-            recv_sem=self.recv_sem.at[self.n],
+            recv_sem=self.recv_sem.at[at],
             device_id=to,
             device_id_type=MESH,
         )
         copy.start()
         self.open[k] = copy
-        self.n += 1
         return copy
 
     def drain(self):
@@ -501,13 +508,14 @@
 
 
 class Conductor:
-    def __init__(self, openers):
-        self.openers = openers
+    def __init__(self, wire, openers):
+        self.wire, self.openers = wire, openers
         self.streams = {}
         self.place = 0
 
     def serve(self):
         for key, i in SCHEDULE[self.place]:
+            self.wire.key = key
             if i < 0:
                 self.streams.update({(key, k): s for k, s in enumerate(self.openers[key]())})
                 for k in self.streams:
@@ -668,7 +676,7 @@
     openers.update({5 + g: lambda g=g: [gather_front(wire, wd_ref, stage, wide, down, g)] for g in range(3)})
     finals = final, dd_ref
     openers.update({10 + g: lambda g=g: reduce_streams(wire, gwide, gdown, bufs[g], finals, g) for g in REDUCED})
-    conductor = Conductor(openers)
+    conductor = Conductor(wire, openers)
     serve = conductor.serve
     mine = 2 * me.zl + me.c
 

time: 118 us -> 117 us (level)
  no operation moved by 1% of the time
where the time goes in v7:
time: 117 us
  Pallas kernels  116 us (99%)
    pallas_call x1, Pallas kernels, per_device(): pl.pallas_call(layer_kernel, out_shape=(like((T, D), BF), like((T, D), F3...  114 us
    pallas_call x1, Pallas kernels, per_device(): pl.pallas_call(publish_kernel, out_shape=tuple((like(o.shape, o.dtype) fo...  2.54 us

profile of v7, /device:TPU:1, one launch (start us, length us, event | category | flops | bytes accessed | tf_op | source)
XLA Modules:
  0.0 117.0 jit_solution(12870834050578670772)
XLA Ops:
  0.6 113.6 %layer.1 = (bf16[256,768]{1,0:T(8,128)(2,1)}, f32[256,768]{1,0:T(8,128)}, f32[1,12]{1,0:T(1,128)}, f32[1,12]{1,0:T(1,128)}, f32[12,768]{1,0:T(8,128)}, /*index=5...) custom-call(bf16[256,768]{1,0:T(8,128)(2,1)} %x_hbm.1, ...), custom_call_target="tpu_custom_call" | custom-call | flops 12999999488 | bytes 6000000 | tf_op jit(solution)/shard_map/layer/pallas_call | solution.py:1006
  114.2 2.5 %publish.1 = (bf16[256,768]{1,0:T(8,128)(2,1)}, f32[256,768]{1,0:T(8,128)}, f32[1,12]{1,0:T(1,128)}, f32[1,12]{1,0:T(1,128)}, f32[12,768]{1,0:T(8,128)}, /*index...) custom-call(bf16[256,768]{1,0:T(8,128)(2,1)} %get-tuple-element.36.r, ...), custom_call_target="tpu_custom_call" | custom-call | tf_op jit(solution)/shard_map/publish/pallas_call | solution.py:1021
